TPU v7x, 32 devices: a whole 2x2x4 slice. The times are simulated.
32 devices in a mesh: dp: 8 (over z, x), ctx: 4 (over y, core).
Axes of the slice: x: 2, y: 2, z: 4, core: 2. Of those that a mesh axis runs over, the one named last changes fastest.
Arguments:
- prefix_tokens: bfloat16 [8, 624, 2048], P('dp', 'ctx'), may hold values from -6 to 6
- actions: bfloat16 [8, 4, 50, 32], P('dp', 'ctx'), may hold values from -6 to 6
- robot_state: bfloat16 [8, 32], P('dp'), may hold values from -6 to 6
- text_len: int32 [8], P('dp'), may hold values from 5 to 48, as said below
- flow_index: int32 [8, 4], P('dp', 'ctx'), may hold values from 0 to 999
- query_pre: bfloat16 [2048, 2048], P(('dp', 'ctx')), may hold values from -0.125 to 0.125
- key_pre: bfloat16 [2048, 256], P(('dp', 'ctx')), may hold values from -0.125 to 0.125
- value_pre: bfloat16 [2048, 256], P(('dp', 'ctx')), may hold values from -0.125 to 0.125
- out_pre: bfloat16 [2048, 2048], P(('dp', 'ctx')), may hold values from -1.5 to 1.5
- gain_attn_pre: bfloat16 [2048], P(('dp', 'ctx')), may hold values from 0.5 to 1.5
- gain_ffn_pre: bfloat16 [2048], P(('dp', 'ctx')), may hold values from 0.5 to 1.5
- query_act: bfloat16 [1024, 2048], P(('dp', 'ctx')), may hold values from -0.1875 to 0.1875
- key_act: bfloat16 [1024, 256], P(('dp', 'ctx')), may hold values from -0.1875 to 0.1875
- value_act: bfloat16 [1024, 256], P(('dp', 'ctx')), may hold values from -0.1875 to 0.1875
- out_act: bfloat16 [2048, 1024], P(('dp', 'ctx')), may hold values from -1.5 to 1.5
- gain_attn_act: bfloat16 [1024], P(('dp', 'ctx')), may hold values from 0.5 to 1.5
- gain_ffn_act: bfloat16 [1024], P(('dp', 'ctx')), may hold values from 0.5 to 1.5
- action_in: bfloat16 [1024, 32], P(('dp', 'ctx')), may hold values from -1 to 1
- mix_first: bfloat16 [2048, 1024], P(('dp', 'ctx')), may hold values from -0.125 to 0.125
- mix_second: bfloat16 [1024, 1024], P(('dp', 'ctx')), may hold values from -0.1875 to 0.1875
- state_in: bfloat16 [1024, 32], P(('dp', 'ctx')), may hold values from -1 to 1
- gate_pre: bfloat16 [2048, 16384], P('dp', 'ctx'), may hold values from -0.125 to 0.125
- up_pre: bfloat16 [2048, 16384], P('dp', 'ctx'), may hold values from -0.125 to 0.125
- down_pre: bfloat16 [16384, 2048], P('ctx', 'dp'), may hold values from -0.046875 to 0.046875
- gate_act: bfloat16 [1024, 4096], P('dp', 'ctx'), may hold values from -0.1875 to 0.1875
- up_act: bfloat16 [1024, 4096], P('dp', 'ctx'), may hold values from -0.1875 to 0.1875
- down_act: bfloat16 [4096, 1024], P('ctx', 'dp'), may hold values from -0.09375 to 0.09375
- grad_pre: bfloat16 [8, 624, 2048], P('dp', 'ctx'), may hold values from -6 to 6
- grad_act: bfloat16 [8, 4, 51, 1024], P('dp', 'ctx'), may hold values from -6 to 6
Outputs:
- out_prefix: float32 [8, 624, 2048], P('dp', 'ctx')
- out_actions: float32 [8, 4, 51, 1024], P('dp', 'ctx')
- grad_prefix: float32 [8, 624, 2048], P('dp', 'ctx')
- grad_actions: float32 [8, 4, 50, 32], P('dp', 'ctx')
- grad_query_pre: float32 [2048, 2048], P(('dp', 'ctx'))
- grad_key_pre: float32 [2048, 256], P(('dp', 'ctx'))
- grad_value_pre: float32 [2048, 256], P(('dp', 'ctx'))
- grad_out_pre: float32 [2048, 2048], P(('dp', 'ctx'))
- grad_gain_attn_pre: float32 [2048], P(('dp', 'ctx'))
- grad_gain_ffn_pre: float32 [2048], P(('dp', 'ctx'))
- grad_query_act: float32 [1024, 2048], P(('dp', 'ctx'))
- grad_key_act: float32 [1024, 256], P(('dp', 'ctx'))
- grad_value_act: float32 [1024, 256], P(('dp', 'ctx'))
- grad_out_act: float32 [2048, 1024], P(('dp', 'ctx'))
- grad_gain_attn_act: float32 [1024], P(('dp', 'ctx'))
- grad_gain_ffn_act: float32 [1024], P(('dp', 'ctx'))
- grad_action_in: float32 [1024, 32], P(('dp', 'ctx'))
- grad_mix_first: float32 [2048, 1024], P(('dp', 'ctx'))
- grad_mix_second: float32 [1024, 1024], P(('dp', 'ctx'))
- grad_state_in: float32 [1024, 32], P(('dp', 'ctx'))
- grad_gate_pre: float32 [2048, 16384], P('dp', 'ctx')
- grad_up_pre: float32 [2048, 16384], P('dp', 'ctx')
- grad_down_pre: float32 [16384, 2048], P('ctx', 'dp')
- grad_gate_act: float32 [1024, 4096], P('dp', 'ctx')
- grad_up_act: float32 [1024, 4096], P('dp', 'ctx')
- grad_down_act: float32 [4096, 1024], P('ctx', 'dp')
Inputs may be any that keep to these rules, and one draw needn't show every extreme that they name: `text_len`: the rest of the 48 text slots are padding; some item has exactly 48 given tokens and another exactly 5.
All inputs are finite; a program needn't handle non-finite values.
Results may differ from a plain program's by a relative error of at most 0.024.
Values may be sent and summed in bfloat16 or wider, within the bound.
No kernel may reach another device: no remote copies, remote signals or barrier semaphores. Data moves between devices by JAX's collectives and lax.ppermute only.
A program may use at most 384 MiB of HBM per device.

v0:
```python
import math

import jax
import jax.numpy as jnp
from jax import lax
from jax.sharding import PartitionSpec as P

DS = 1024
HEADS = 8
HD = 256
CAMS = 3
PATCH = 192
NTIME = 1000


masked_score = -1e30


def rms_norm(values, norm_gain):
    return values * lax.rsqrt(jnp.mean(values * values, axis=-1, keepdims=True) + 1e-06) * norm_gain


def norm_back(values, norm_gain, cotangent):
    _, pullback = jax.vjp(rms_norm, values, norm_gain)
    return pullback(cotangent)


def time_embed(sample_index):
    flow_time = (sample_index.astype(jnp.float32) + 0.5) / NTIME
    halves = DS // 2
    fraction = jnp.arange(halves, dtype=jnp.float32) / (halves - 1)
    period = 0.004 * jnp.power(1000.0, fraction)
    angles = 2.0 * math.pi * flow_time[..., None] / period
    return jnp.concatenate([jnp.sin(angles), jnp.cos(angles)], axis=-1)


def matmul_low(left, right):
    return jnp.dot(left, right, preferred_element_type=jnp.float32)


def matmul_tr(left, right):
    return lax.dot_general(
        left, right, (((left.ndim - 1,), (1,)), ((), ())), preferred_element_type=jnp.float32
    )


def outer_sum(left, right):
    flat_left = left.reshape(-1, left.shape[-1])
    flat_right = right.reshape(-1, right.shape[-1])
    return lax.dot_general(
        flat_left, flat_right, (((0,), (0,)), ((), ())), preferred_element_type=jnp.float32
    )


def soft_rows(scores):
    highest = jnp.max(scores, axis=-1, keepdims=True)
    totals = jnp.sum(jnp.exp(scores - highest), axis=-1, keepdims=True)
    log_total = highest + jnp.log(totals)
    return (jnp.exp(scores - log_total), log_total)


def prefix_scores(queries, combined_keys, key_valid):
    query_head_rows = queries.reshape(queries.shape[0], queries.shape[1], HEADS, HD)
    scores = jnp.einsum(
        "yisf,yof->ysio", query_head_rows, combined_keys, preferred_element_type=jnp.float32
    ) * HD ** (-0.5)
    return (jnp.where(key_valid[:, None, None, :], scores, masked_score), query_head_rows)


def side_scores(queries, combined_keys, keys_act, key_valid):
    query_head_rows = queries.reshape(queries.shape[:3] + (HEADS, HD))
    far_part = jnp.einsum(
        "ycsgz,yrz->ycgsr", query_head_rows, combined_keys, preferred_element_type=jnp.float32
    ) * HD ** (-0.5)
    far_part = jnp.where(key_valid[:, None, None, None, :], far_part, masked_score)
    near_part = jnp.einsum(
        "bfqhd,bfkd->bfhqk", query_head_rows, keys_act, preferred_element_type=jnp.float32
    ) * HD ** (-0.5)
    groups = jnp.arange(keys_act.shape[2]) > 0
    own_block = groups[None, :] <= groups[:, None]
    near_part = jnp.where(own_block, near_part, masked_score)
    return (jnp.concatenate([far_part, near_part], axis=-1), query_head_rows)


def gated_unit(gate_value, up_value):
    return jax.nn.gelu(gate_value, approximate=True) * up_value


def ffn_forward(token_rows, gate_weight, up_weight, down_weight):
    gate_value = matmul_low(token_rows, gate_weight)
    up_value = matmul_low(token_rows, up_weight)
    hidden = gated_unit(gate_value, up_value).astype(jnp.bfloat16)
    return (matmul_low(hidden, down_weight), gate_value, up_value, hidden)


def ffn_backward(
    token_rows, cot_rows, gate_weight, up_weight, down_weight, gate_value, up_value, hidden
):
    d_hidden = matmul_tr(cot_rows, down_weight)
    grad_down = outer_sum(hidden, cot_rows)
    _, pullback = jax.vjp(gated_unit, gate_value, up_value)
    d_gate, d_up = pullback(d_hidden)
    d_gate = d_gate.astype(jnp.bfloat16)
    d_up = d_up.astype(jnp.bfloat16)
    d_rows = matmul_tr(d_gate, gate_weight) + matmul_tr(d_up, up_weight)
    return (d_rows, outer_sum(token_rows, d_gate), outer_sum(token_rows, d_up), grad_down)


def per_device(
    prefix_tokens,
    actions,
    robot_state,
    text_len,
    flow_index,
    query_pre,
    key_pre,
    value_pre,
    out_pre,
    gain_attn_pre,
    gain_ffn_pre,
    query_act,
    key_act,
    value_act,
    out_act,
    gain_attn_act,
    gain_ffn_act,
    action_in,
    mix_first,
    mix_second,
    state_in,
    gate_pre,
    up_pre,
    down_pre,
    gate_act,
    up_act,
    down_act,
    grad_pre,
    grad_act,
):
    light_weights = (
        lax.all_gather(query_pre, ("dp", "ctx"), axis=0, tiled=True),
        lax.all_gather(key_pre, ("dp", "ctx"), axis=0, tiled=True),
        lax.all_gather(value_pre, ("dp", "ctx"), axis=0, tiled=True),
        lax.all_gather(out_pre, ("dp", "ctx"), axis=0, tiled=True),
        lax.all_gather(gain_attn_pre, ("dp", "ctx"), axis=0, tiled=True),
        lax.all_gather(gain_ffn_pre, ("dp", "ctx"), axis=0, tiled=True),
        lax.all_gather(query_act, ("dp", "ctx"), axis=0, tiled=True),
        lax.all_gather(key_act, ("dp", "ctx"), axis=0, tiled=True),
        lax.all_gather(value_act, ("dp", "ctx"), axis=0, tiled=True),
        lax.all_gather(out_act, ("dp", "ctx"), axis=0, tiled=True),
        lax.all_gather(gain_attn_act, ("dp", "ctx"), axis=0, tiled=True),
        lax.all_gather(gain_ffn_act, ("dp", "ctx"), axis=0, tiled=True),
        lax.all_gather(action_in, ("dp", "ctx"), axis=0, tiled=True),
        lax.all_gather(mix_first, ("dp", "ctx"), axis=0, tiled=True),
        lax.all_gather(mix_second, ("dp", "ctx"), axis=0, tiled=True),
        lax.all_gather(state_in, ("dp", "ctx"), axis=0, tiled=True),
    )
    (
        query_full,
        key_full,
        value_full,
        out_full,
        norm_attn,
        norm_ffn,
        query_full_act,
        key_full_act,
        value_full_act,
        out_full_act,
        norm_attn_act,
        norm_ffn_act,
        action_full,
        mixer_first,
        mixer_second,
        state_full,
    ) = light_weights
    norm_attn = norm_attn.astype(jnp.float32)
    norm_ffn = norm_ffn.astype(jnp.float32)
    norm_attn_act = norm_attn_act.astype(jnp.float32)
    norm_ffn_act = norm_ffn_act.astype(jnp.float32)
    gathered = (
        lax.all_gather(gate_pre, "dp", axis=0, tiled=True),
        lax.all_gather(up_pre, "dp", axis=0, tiled=True),
        lax.all_gather(down_pre, "dp", axis=1, tiled=True),
        lax.all_gather(gate_act, "dp", axis=0, tiled=True),
        lax.all_gather(up_act, "dp", axis=0, tiled=True),
        lax.all_gather(down_act, "dp", axis=1, tiled=True),
    )
    time_rows = time_embed(flow_index)
    action_emb = lax.dot_general(
        actions, action_full, (((3,), (1,)), ((), ())), preferred_element_type=jnp.float32
    )
    mix_input = jnp.concatenate(
        [action_emb, jnp.broadcast_to(time_rows[:, :, None, :], action_emb.shape)], axis=-1
    ).astype(jnp.bfloat16)
    pre_mix = matmul_low(mix_input, mixer_first)
    mixed_act = jax.nn.silu(pre_mix).astype(jnp.bfloat16)
    action_rows = matmul_low(mixed_act, mixer_second)
    state_row = lax.dot_general(
        robot_state, state_full, (((1,), (1,)), ((), ())), preferred_element_type=jnp.float32
    )
    state_rows = state_row[:, None, None, :]
    side_input = jnp.concatenate([state_rows, action_rows], axis=2)
    prefix_in = prefix_tokens.astype(jnp.float32)
    normed_pre = rms_norm(prefix_in, norm_attn).astype(jnp.bfloat16)
    normed_act = rms_norm(side_input, norm_attn_act).astype(jnp.bfloat16)
    queries_pre = matmul_low(normed_pre, query_full).astype(jnp.bfloat16)
    keys_pre = matmul_low(normed_pre, key_full).astype(jnp.bfloat16)
    values_pre = matmul_low(normed_pre, value_full).astype(jnp.bfloat16)
    queries_act = matmul_low(normed_act, query_full_act).astype(jnp.bfloat16)
    keys_act = matmul_low(normed_act, key_full_act).astype(jnp.bfloat16)
    values_act = matmul_low(normed_act, value_full_act).astype(jnp.bfloat16)
    combined_keys, combined_values = (
        lax.all_gather(keys_pre, "ctx", axis=1, tiled=True),
        lax.all_gather(values_pre, "ctx", axis=1, tiled=True),
    )
    key_count = combined_keys.shape[1]
    positions = jnp.arange(key_count)
    camera_rows = CAMS * PATCH
    key_valid = (positions[None, :] < camera_rows) | (
        positions[None, :] - camera_rows < text_len[:, None]
    )
    scores_pre, prefix_head_outputs = prefix_scores(queries_pre, combined_keys, key_valid)
    probs_pre, total_pre = soft_rows(scores_pre)
    attn_pre = (
        jnp.einsum(
            "ipno,iou->inpu",
            probs_pre.astype(jnp.bfloat16),
            combined_values,
            preferred_element_type=jnp.float32,
        )
        .reshape(queries_pre.shape)
        .astype(jnp.bfloat16)
    )
    scores_act, action_head_outputs = side_scores(queries_act, combined_keys, keys_act, key_valid)
    probs_act, total_act = soft_rows(scores_act)
    probs_act_low = probs_act.astype(jnp.bfloat16)
    attn_act = jnp.einsum(
        "scgaw,swn->scagn",
        probs_act_low[..., :key_count],
        combined_values,
        preferred_element_type=jnp.float32,
    ) + jnp.einsum(
        "bfhqk,bfkd->bfqhd",
        probs_act_low[..., key_count:],
        values_act,
        preferred_element_type=jnp.float32,
    )
    attn_act = attn_act.reshape(queries_act.shape).astype(jnp.bfloat16)
    mid_pre = prefix_in + matmul_low(attn_pre, out_full)
    mid_act = side_input + matmul_low(attn_act, out_full_act)
    normed_two_pre = rms_norm(mid_pre, norm_ffn).astype(jnp.bfloat16)
    normed_two_act = rms_norm(mid_act, norm_ffn_act).astype(jnp.bfloat16)
    rows_pre, rows_act = (
        lax.all_gather(normed_two_pre, "ctx", axis=1, tiled=True),
        lax.all_gather(normed_two_act, "ctx", axis=1, tiled=True),
    )
    partial_pre, gate_value_pre, up_value_pre, hidden_pre = ffn_forward(
        rows_pre, gathered[0], gathered[1], gathered[2]
    )
    partial_act, gate_value_act, up_value_act, hidden_act = ffn_forward(
        rows_act, gathered[3], gathered[4], gathered[5]
    )
    branch_pre, branch_act = (
        lax.psum_scatter(
            partial_pre.astype(jnp.bfloat16), "ctx", scatter_dimension=1, tiled=True
        ).astype(jnp.float32),
        lax.psum_scatter(
            partial_act.astype(jnp.bfloat16), "ctx", scatter_dimension=1, tiled=True
        ).astype(jnp.float32),
    )
    out_prefix = mid_pre + branch_pre
    out_actions = mid_act + branch_act
    cot_rows_pre, cot_rows_act = (
        lax.all_gather(grad_pre, "ctx", axis=1, tiled=True),
        lax.all_gather(grad_act, "ctx", axis=1, tiled=True),
    )
    ffn_again = (
        lax.all_gather(gate_pre, "dp", axis=0, tiled=True),
        lax.all_gather(up_pre, "dp", axis=0, tiled=True),
        lax.all_gather(down_pre, "dp", axis=1, tiled=True),
        lax.all_gather(gate_act, "dp", axis=0, tiled=True),
        lax.all_gather(up_act, "dp", axis=0, tiled=True),
        lax.all_gather(down_act, "dp", axis=1, tiled=True),
    )
    d_rows_pre, grad_gate_pre, grad_up_pre, grad_down_pre = ffn_backward(
        rows_pre,
        cot_rows_pre,
        ffn_again[0],
        ffn_again[1],
        ffn_again[2],
        gate_value_pre,
        up_value_pre,
        hidden_pre,
    )
    d_rows_act, grad_gate_act, grad_up_act, grad_down_act = ffn_backward(
        rows_act,
        cot_rows_act,
        ffn_again[3],
        ffn_again[4],
        ffn_again[5],
        gate_value_act,
        up_value_act,
        hidden_act,
    )
    ffn_grads = tuple(
        (
            lax.psum_scatter(
                grad_gate_pre.astype(jnp.bfloat16), "dp", scatter_dimension=0, tiled=True
            ).astype(jnp.float32),
            lax.psum_scatter(
                grad_up_pre.astype(jnp.bfloat16), "dp", scatter_dimension=0, tiled=True
            ).astype(jnp.float32),
            lax.psum_scatter(
                grad_down_pre.astype(jnp.bfloat16), "dp", scatter_dimension=1, tiled=True
            ).astype(jnp.float32),
            lax.psum_scatter(
                grad_gate_act.astype(jnp.bfloat16), "dp", scatter_dimension=0, tiled=True
            ).astype(jnp.float32),
            lax.psum_scatter(
                grad_up_act.astype(jnp.bfloat16), "dp", scatter_dimension=0, tiled=True
            ).astype(jnp.float32),
            lax.psum_scatter(
                grad_down_act.astype(jnp.bfloat16), "dp", scatter_dimension=1, tiled=True
            ).astype(jnp.float32),
        )
    )
    d_normed_two_pre, d_normed_two_act = (
        lax.psum_scatter(
            d_rows_pre.astype(jnp.bfloat16), "ctx", scatter_dimension=1, tiled=True
        ).astype(jnp.float32),
        lax.psum_scatter(
            d_rows_act.astype(jnp.bfloat16), "ctx", scatter_dimension=1, tiled=True
        ).astype(jnp.float32),
    )
    d_mid_pre, grad_norm_ffn = norm_back(mid_pre, norm_ffn, d_normed_two_pre)
    d_mid_pre = d_mid_pre + grad_pre.astype(jnp.float32)
    d_mid_act, grad_norm_ffn_act = norm_back(mid_act, norm_ffn_act, d_normed_two_act)
    d_mid_act = d_mid_act + grad_act.astype(jnp.float32)
    d_branch_pre = d_mid_pre.astype(jnp.bfloat16)
    d_branch_act = d_mid_act.astype(jnp.bfloat16)
    grad_out_pre = outer_sum(attn_pre, d_branch_pre)
    grad_out_act = outer_sum(attn_act, d_branch_act)
    d_attn_pre = matmul_tr(d_branch_pre, out_full).astype(jnp.bfloat16)
    d_attn_act = matmul_tr(d_branch_act, out_full_act).astype(jnp.bfloat16)
    score_scale = HD ** (-0.5)
    scores_pre, prefix_head_outputs = prefix_scores(queries_pre, combined_keys, key_valid)
    probs_pre = jnp.exp(scores_pre - total_pre)
    prefix_heads_gradient = d_attn_pre.reshape(prefix_head_outputs.shape)
    d_probs_pre = jnp.einsum(
        "yisf,yof->ysio", prefix_heads_gradient, combined_values, preferred_element_type=jnp.float32
    )
    prefix_scores_gradient = (
        probs_pre * (d_probs_pre - jnp.sum(probs_pre * d_probs_pre, axis=-1, keepdims=True))
    ).astype(jnp.bfloat16)
    d_query_pre = (
        (
            jnp.einsum(
                "ipno,iou->inpu",
                prefix_scores_gradient,
                combined_keys,
                preferred_element_type=jnp.float32,
            )
            * score_scale
        )
        .reshape(queries_pre.shape)
        .astype(jnp.bfloat16)
    )
    key_terms = (
        jnp.einsum(
            "jztl,jtza->jla",
            prefix_scores_gradient,
            prefix_head_outputs,
            preferred_element_type=jnp.float32,
        )
        * score_scale
    )
    value_terms = jnp.einsum(
        "jztl,jtza->jla",
        probs_pre.astype(jnp.bfloat16),
        prefix_heads_gradient,
        preferred_element_type=jnp.float32,
    )
    scores_act, action_head_outputs = side_scores(queries_act, combined_keys, keys_act, key_valid)
    probs_act = jnp.exp(scores_act - total_act)
    probs_act_low = probs_act.astype(jnp.bfloat16)
    action_heads_gradient = d_attn_act.reshape(action_head_outputs.shape)
    d_probs_act = jnp.concatenate(
        [
            jnp.einsum(
                "ycsgz,yrz->ycgsr",
                action_heads_gradient,
                combined_values,
                preferred_element_type=jnp.float32,
            ),
            jnp.einsum(
                "bfqhd,bfkd->bfhqk",
                action_heads_gradient,
                values_act,
                preferred_element_type=jnp.float32,
            ),
        ],
        axis=-1,
    )
    d_scores_act = (
        probs_act * (d_probs_act - jnp.sum(probs_act * d_probs_act, axis=-1, keepdims=True))
    ).astype(jnp.bfloat16)
    distant_scores = d_scores_act[..., :key_count]
    near_scores = d_scores_act[..., key_count:]
    d_query_act = (
        (
            (
                jnp.einsum(
                    "scgaw,swn->scagn",
                    distant_scores,
                    combined_keys,
                    preferred_element_type=jnp.float32,
                )
                + jnp.einsum(
                    "bfhqk,bfkd->bfqhd", near_scores, keys_act, preferred_element_type=jnp.float32
                )
            )
            * score_scale
        )
        .reshape(queries_act.shape)
        .astype(jnp.bfloat16)
    )
    key_terms = (
        key_terms
        + jnp.einsum(
            "zrpiy,zripc->zyc",
            distant_scores,
            action_head_outputs,
            preferred_element_type=jnp.float32,
        )
        * score_scale
    )
    value_terms = value_terms + jnp.einsum(
        "zrpiy,zripc->zyc",
        probs_act_low[..., :key_count],
        action_heads_gradient,
        preferred_element_type=jnp.float32,
    )
    d_keys_act = (
        jnp.einsum(
            "bfhqk,bfqhd->bfkd",
            near_scores,
            action_head_outputs,
            preferred_element_type=jnp.float32,
        )
        * score_scale
    ).astype(jnp.bfloat16)
    d_values_act = jnp.einsum(
        "bfhqk,bfqhd->bfkd",
        probs_act_low[..., key_count:],
        action_heads_gradient,
        preferred_element_type=jnp.float32,
    ).astype(jnp.bfloat16)
    d_keys_sum, d_values_sum = (
        lax.psum_scatter(
            key_terms.astype(jnp.bfloat16), "ctx", scatter_dimension=1, tiled=True
        ).astype(jnp.float32),
        lax.psum_scatter(
            value_terms.astype(jnp.bfloat16), "ctx", scatter_dimension=1, tiled=True
        ).astype(jnp.float32),
    )
    d_keys_pre = d_keys_sum.astype(jnp.bfloat16)
    d_values_pre = d_values_sum.astype(jnp.bfloat16)
    d_normed_pre = (
        matmul_tr(d_query_pre, query_full)
        + matmul_tr(d_keys_pre, key_full)
        + matmul_tr(d_values_pre, value_full)
    )
    grad_query_pre = outer_sum(normed_pre, d_query_pre)
    grad_key_pre = outer_sum(normed_pre, d_keys_pre)
    grad_value_pre = outer_sum(normed_pre, d_values_pre)
    d_normed_act = (
        matmul_tr(d_query_act, query_full_act)
        + matmul_tr(d_keys_act, key_full_act)
        + matmul_tr(d_values_act, value_full_act)
    )
    grad_query_act = outer_sum(normed_act, d_query_act)
    grad_key_act = outer_sum(normed_act, d_keys_act)
    grad_value_act = outer_sum(normed_act, d_values_act)
    grad_prefix, grad_norm_attn = norm_back(prefix_in, norm_attn, d_normed_pre)
    grad_prefix = grad_prefix + d_mid_pre
    d_side, grad_norm_attn_act = norm_back(side_input, norm_attn_act, d_normed_act)
    d_side = d_side + d_mid_act
    d_state_rows = d_side[:, :, 0, :].astype(jnp.bfloat16)
    state_wide = robot_state[:, None, :]
    grad_state_in = outer_sum(d_state_rows, state_wide)
    d_action_rows = d_side[:, :, 1:, :].astype(jnp.bfloat16)
    grad_mix_second = outer_sum(mixed_act, d_action_rows)
    d_mixed = matmul_tr(d_action_rows, mixer_second)
    _, silu_back = jax.vjp(jax.nn.silu, pre_mix)
    d_pre_mix = silu_back(d_mixed)[0].astype(jnp.bfloat16)
    grad_mix_first = outer_sum(mix_input, d_pre_mix)
    d_mix_input = matmul_tr(d_pre_mix, mixer_first)
    d_action_emb = d_mix_input[..., : action_full.shape[0]].astype(jnp.bfloat16)
    grad_action_in = outer_sum(d_action_emb, actions)
    grad_actions = matmul_low(d_action_emb, action_full)
    light_grads = (
        lax.psum_scatter(grad_query_pre, ("dp", "ctx"), scatter_dimension=0, tiled=True),
        lax.psum_scatter(grad_key_pre, ("dp", "ctx"), scatter_dimension=0, tiled=True),
        lax.psum_scatter(grad_value_pre, ("dp", "ctx"), scatter_dimension=0, tiled=True),
        lax.psum_scatter(grad_out_pre, ("dp", "ctx"), scatter_dimension=0, tiled=True),
        lax.psum_scatter(grad_norm_attn, ("dp", "ctx"), scatter_dimension=0, tiled=True),
        lax.psum_scatter(grad_norm_ffn, ("dp", "ctx"), scatter_dimension=0, tiled=True),
        lax.psum_scatter(grad_query_act, ("dp", "ctx"), scatter_dimension=0, tiled=True),
        lax.psum_scatter(grad_key_act, ("dp", "ctx"), scatter_dimension=0, tiled=True),
        lax.psum_scatter(grad_value_act, ("dp", "ctx"), scatter_dimension=0, tiled=True),
        lax.psum_scatter(grad_out_act, ("dp", "ctx"), scatter_dimension=0, tiled=True),
        lax.psum_scatter(grad_norm_attn_act, ("dp", "ctx"), scatter_dimension=0, tiled=True),
        lax.psum_scatter(grad_norm_ffn_act, ("dp", "ctx"), scatter_dimension=0, tiled=True),
        lax.psum_scatter(grad_action_in, ("dp", "ctx"), scatter_dimension=0, tiled=True),
        lax.psum_scatter(grad_mix_first, ("dp", "ctx"), scatter_dimension=0, tiled=True),
        lax.psum_scatter(grad_mix_second, ("dp", "ctx"), scatter_dimension=0, tiled=True),
        lax.psum_scatter(grad_state_in, ("dp", "ctx"), scatter_dimension=0, tiled=True),
    )
    return (
        (out_prefix, out_actions, grad_prefix, grad_actions) + tuple(light_grads) + tuple(ffn_grads)
    )


def solution(mesh):
    return jax.shard_map(
        per_device,
        mesh=mesh,
        in_specs=(
            P("dp", "ctx", None),
            P("dp", "ctx", None, None),
            P("dp", None),
            P("dp"),
            P("dp", "ctx"),
            P(("dp", "ctx"), None),
            P(("dp", "ctx"), None),
            P(("dp", "ctx"), None),
            P(("dp", "ctx"), None),
            P(("dp", "ctx")),
            P(("dp", "ctx")),
            P(("dp", "ctx"), None),
            P(("dp", "ctx"), None),
            P(("dp", "ctx"), None),
            P(("dp", "ctx"), None),
            P(("dp", "ctx")),
            P(("dp", "ctx")),
            P(("dp", "ctx"), None),
            P(("dp", "ctx"), None),
            P(("dp", "ctx"), None),
            P(("dp", "ctx"), None),
            P("dp", "ctx"),
            P("dp", "ctx"),
            P("ctx", "dp"),
            P("dp", "ctx"),
            P("dp", "ctx"),
            P("ctx", "dp"),
            P("dp", "ctx", None),
            P("dp", "ctx", None, None),
        ),
        out_specs=(
            P("dp", "ctx", None),
            P("dp", "ctx", None, None),
            P("dp", "ctx", None),
            P("dp", "ctx", None, None),
            P(("dp", "ctx"), None),
            P(("dp", "ctx"), None),
            P(("dp", "ctx"), None),
            P(("dp", "ctx"), None),
            P(("dp", "ctx")),
            P(("dp", "ctx")),
            P(("dp", "ctx"), None),
            P(("dp", "ctx"), None),
            P(("dp", "ctx"), None),
            P(("dp", "ctx"), None),
            P(("dp", "ctx")),
            P(("dp", "ctx")),
            P(("dp", "ctx"), None),
            P(("dp", "ctx"), None),
            P(("dp", "ctx"), None),
            P(("dp", "ctx"), None),
            P("dp", "ctx"),
            P("dp", "ctx"),
            P("ctx", "dp"),
            P("dp", "ctx"),
            P("dp", "ctx"),
            P("ctx", "dp"),
        ),
        check_vma=False,
    )
```

profile of v0, /device:TPU:0, one launch (start us, length us, event | category | flops | bytes accessed | tf_op | source)
XLA Modules:
  0.0 4334.4 jit_solution(5646902186879428110)
XLA Ops:
  18.2 42.2 all-reduce.17
  75.6 47.9 %all-gather.25.cloned.1.call-done = bf16[2048,256]{1,0:T(8,128)(2,1)} async-done(((bf16[64,256]{1,0:T(8,128)(2,1)}), bf16[2048,256]{1,0:T(8,128)(2,1)}) %all-gather.25.cloned.1.call-update) | async-done | bytes 1048592 | tf_op jit(solution)/shard_map/all_gather | solution.py:142
  131.3 71.5 %all-gather.27.cloned.1.call-done = bf16[2048,2048]{1,0:T(8,128)(2,1)} async-done(((bf16[64,2048]{1,0:T(8,128)(2,1)}), bf16[2048,2048]{1,0:T(8,128)(2,1)}) %all-gather.27.cloned.1.call-update) | async-done | bytes 8388624 | tf_op jit(solution)/shard_map/all_gather | solution.py:141
  212.2 69.5 %all-gather.29.cloned.1.call-done = bf16[2048,2048]{1,0:T(8,128)(2,1)} async-done(((bf16[64,2048]{1,0:T(8,128)(2,1)}), bf16[2048,2048]{1,0:T(8,128)(2,1)}) %all-gather.29.cloned.1.call-update) | async-done | bytes 8388624 | tf_op jit(solution)/shard_map/all_gather | solution.py:144
  295.2 40.8 all_gather.103
  336.0 37.5 all_gather.102
  381.3 40.3 all_gather.109
  421.6 38.5 all_gather.108
  469.2 51.8 %all-gather.43.cloned.1.call-done = bf16[1024,2048]{1,0:T(8,128)(2,1)} async-done(((bf16[32,2048]{1,0:T(8,128)(2,1)}), bf16[1024,2048]{1,0:T(8,128)(2,1)}) %all-gather.43.cloned.1.call-update) | async-done | bytes 4194320 | tf_op jit(solution)/shard_map/all_gather | solution.py:147
  527.8 56.7 %all-gather.45.cloned.1.call-done = bf16[2048,1024]{1,0:T(8,128)(2,1)} async-done(((bf16[64,1024]{1,0:T(8,128)(2,1)}), bf16[2048,1024]{1,0:T(8,128)(2,1)}) %all-gather.45.cloned.1.call-update) | async-done | bytes 4194320 | tf_op jit(solution)/shard_map/all_gather | solution.py:150
  595.3 39.0 all-gather.47.cloned.1.call-done
  636.6 47.7 %all-gather.49.cloned.1.call-done = bf16[1024,1024]{1,0:T(8,128)(2,1)} async-done(((bf16[128,1024]{1,0:T(8,128)(2,1)}), bf16[1024,1024]{1,0:T(8,128)(2,1)}) %all-gather.49.cloned.1.call-update) | async-done | bytes 2097168 | tf_op jit(solution)/shard_map/all_gather | solution.py:185
  728.5 225.7 %all-gather.33.cloned.1.call-done = bf16[2048,4096]{1,0:T(8,128)(2,1)} async-done(((bf16[256,4096]{1,0:T(8,128)(2,1)}), bf16[2048,4096]{1,0:T(8,128)(2,1)}) %all-gather.33.cloned.1.call-update) | async-done | bytes 16777232 | tf_op jit(solution)/shard_map/all_gather | solution.py:181
  970.9 211.1 %all-gather.35.cloned.1.call-done = bf16[2048,4096]{1,0:T(8,128)(2,1)} async-done(((bf16[256,4096]{1,0:T(8,128)(2,1)}), bf16[2048,4096]{1,0:T(8,128)(2,1)}) %all-gather.35.cloned.1.call-update) | async-done | bytes 16777232 | tf_op jit(solution)/shard_map/all_gather | solution.py:182
  1221.9 229.7 %all-gather.37.cloned.1.call-done = bf16[4096,2048]{1,0:T(8,128)(2,1)} async-done(((bf16[4096,256]{1,0:T(8,128)(2,1)}), bf16[4096,2048]{1,0:T(8,128)(2,1)}) %all-gather.37.cloned.1.call-update) | async-done | bytes 16777232 | tf_op jit(solution)/shard_map/all_gather | solution.py:183
  1680.3 33.1 fusion.193
  1773.6 42.6 all-reduce.16
  1821.7 175.4 %reduce-scatter.63.cloned.1.call-done = bf16[256,4096]{1,0:T(8,128)(2,1)} async-done(((bf16[2048,4096]{1,0:T(8,128)(2,1)}), bf16[256,4096]{1,0:T(8,128)(2,1)}) %reduce-scatter.63.cloned.1.call-update) | async-done | bytes 2097168 | tf_op jit(solution)/shard_map/reduce_scatter | solution.py:307
  2001.2 281.9 %reduce-scatter.65.cloned.1.call-done = bf16[256,4096]{1,0:T(8,128)(2,1)} async-done(((bf16[2048,4096]{1,0:T(8,128)(2,1)}), bf16[256,4096]{1,0:T(8,128)(2,1)}) %reduce-scatter.65.cloned.1.call-update) | async-done | bytes 2097168 | tf_op jit(solution)/shard_map/reduce_scatter | solution.py:310
  2287.2 281.2 %reduce-scatter.67.cloned.1.call-done = bf16[4096,256]{1,0:T(8,128)(2,1)} async-done(((bf16[4096,2048]{1,0:T(8,128)(2,1)}), bf16[4096,256]{1,0:T(8,128)(2,1)}) %reduce-scatter.67.cloned.1.call-update) | async-done | bytes 2097168 | tf_op jit(solution)/shard_map/reduce_scatter | solution.py:313
  2572.4 132.2 %reduce-scatter.55.cloned.1.call-done = f32[32,32]{1,0:T(8,128)} async-done(((f32[1024,32]{1,0:T(8,128)}), f32[32,32]{1,0:T(8,128)}) %reduce-scatter.55.cloned.1.call-update) | async-done | bytes 4112 | tf_op jit(solution)/shard_map/reduce_scatter | solution.py:514
  2704.5 132.3 %reduce-scatter.61.cloned.1.call-done = f32[32,32]{1,0:T(8,128)} async-done(((f32[1024,32]{1,0:T(8,128)}), f32[32,32]{1,0:T(8,128)}) %reduce-scatter.61.cloned.1.call-update) | async-done | bytes 4112 | tf_op jit(solution)/shard_map/reduce_scatter | solution.py:517
  2836.8 133.5 %reduce-scatter.49.cloned.1.call-done = f32[32,256]{1,0:T(8,128)} async-done(((f32[1024,256]{1,0:T(8,128)}), f32[32,256]{1,0:T(8,128)}) %reduce-scatter.49.cloned.1.call-update) | async-done | bytes 32784 | tf_op jit(solution)/shard_map/reduce_scatter | solution.py:509
  2970.3 133.5 %reduce-scatter.51.cloned.1.call-done = f32[32,256]{1,0:T(8,128)} async-done(((f32[1024,256]{1,0:T(8,128)}), f32[32,256]{1,0:T(8,128)}) %reduce-scatter.51.cloned.1.call-update) | async-done | bytes 32784 | tf_op jit(solution)/shard_map/reduce_scatter | solution.py:510
  3103.8 140.0 %reduce-scatter.59.cloned.1.call-done = f32[32,1024]{1,0:T(8,128)} async-done(((f32[1024,1024]{1,0:T(8,128)}), f32[32,1024]{1,0:T(8,128)}) %reduce-scatter.59.cloned.1.call-update) | async-done | bytes 131088 | tf_op jit(solution)/shard_map/reduce_scatter | solution.py:516
  3243.8 147.7 %reduce-scatter.47.cloned.1.call-done = f32[32,2048]{1,0:T(8,128)} async-done(((f32[1024,2048]{1,0:T(8,128)}), f32[32,2048]{1,0:T(8,128)}) %reduce-scatter.47.cloned.1.call-update) | async-done | bytes 262160 | tf_op jit(solution)/shard_map/reduce_scatter | solution.py:508
  3391.5 147.7 %reduce-scatter.53.cloned.1.call-done = f32[64,1024]{1,0:T(8,128)} async-done(((f32[2048,1024]{1,0:T(8,128)}), f32[64,1024]{1,0:T(8,128)}) %reduce-scatter.53.cloned.1.call-update) | async-done | bytes 262160 | tf_op jit(solution)/shard_map/reduce_scatter | solution.py:511
  3539.2 147.7 %reduce-scatter.57.cloned.1.call-done = f32[64,1024]{1,0:T(8,128)} async-done(((f32[2048,1024]{1,0:T(8,128)}), f32[64,1024]{1,0:T(8,128)}) %reduce-scatter.57.cloned.1.call-update) | async-done | bytes 262160 | tf_op jit(solution)/shard_map/reduce_scatter | solution.py:515
  3686.9 135.6 %reduce-scatter.41.cloned.1.call-done = f32[64,256]{1,0:T(8,128)} async-done(((f32[2048,256]{1,0:T(8,128)}), f32[64,256]{1,0:T(8,128)}) %reduce-scatter.41.cloned.1.call-update) | async-done | bytes 65552 | tf_op jit(solution)/shard_map/reduce_scatter | solution.py:503
  3822.5 135.6 %reduce-scatter.43.cloned.1.call-done = f32[64,256]{1,0:T(8,128)} async-done(((f32[2048,256]{1,0:T(8,128)}), f32[64,256]{1,0:T(8,128)}) %reduce-scatter.43.cloned.1.call-update) | async-done | bytes 65552 | tf_op jit(solution)/shard_map/reduce_scatter | solution.py:504
  3958.1 181.9 %reduce-scatter.39.cloned.1.call-done = f32[64,2048]{1,0:T(8,128)} async-done(((f32[2048,2048]{1,0:T(8,128)}), f32[64,2048]{1,0:T(8,128)}) %reduce-scatter.39.cloned.1.call-update) | async-done | bytes 524304 | tf_op jit(solution)/shard_map/reduce_scatter | solution.py:502
  4140.0 187.4 %reduce-scatter.45.cloned.1.call-done = f32[64,2048]{1,0:T(8,128)} async-done(((f32[2048,2048]{1,0:T(8,128)}), f32[64,2048]{1,0:T(8,128)}) %reduce-scatter.45.cloned.1.call-update) | async-done | bytes 524304 | tf_op jit(solution)/shard_map/reduce_scatter | solution.py:505
  (503 shorter events, 496.6 us)
Async XLA Ops:
  10.0 450.1 %all-gather.51.cloned.1.call-start = ((), (), s32[]{:S(2)}) async-start(), calls=%async_computation.34 | async-start | bytes 2359296 | tf_op jit(solution)/shard_map/all_gather | solution.py:186
  10.6 453.1 %all-gather.39.cloned.1.call-start = ((), (), s32[]{:S(2)}) async-start(), calls=%async_computation.28 | async-start | bytes 4325376 | tf_op jit(solution)/shard_map/all_gather | solution.py:154
  11.2 455.6 %all-gather.41.cloned.1.call-start = ((), (), s32[]{:S(2)}) async-start(), calls=%async_computation.29 | async-start | bytes 2162688 | tf_op jit(solution)/shard_map/all_gather | solution.py:155
  11.9 509.1 %all-gather.43.cloned.1.call-start = ((), (), s32[]{:S(2)}) async-start(), calls=%async_computation.30 | async-start | bytes 4325376 | tf_op jit(solution)/shard_map/all_gather | solution.py:147
  12.7 571.8 %all-gather.45.cloned.1.call-start = ((), (), s32[]{:S(2)}) async-start(), calls=%async_computation.31 | async-start | bytes 4325376 | tf_op jit(solution)/shard_map/all_gather | solution.py:150
  13.4 620.9 %all-gather.47.cloned.1.call-start = ((), (), s32[]{:S(2)}) async-start(), calls=%async_computation.32 | async-start | bytes 2359296 | tf_op jit(solution)/shard_map/all_gather | solution.py:184
  14.0 670.3 %all-gather.49.cloned.1.call-start = ((), (), s32[]{:S(2)}) async-start(), calls=%async_computation.33 | async-start | bytes 2359296 | tf_op jit(solution)/shard_map/all_gather | solution.py:185
  14.7 709.7 %all-gather.31.cloned.1.call-start = ((), (), s32[]{:S(2)}) async-start(), calls=%async_computation.24 | async-start | bytes 6389760 | tf_op jit(solution)/shard_map/all_gather | solution.py:254
  290.1 664.1 %all-gather.33.cloned.1.call-start = ((), (), s32[]{:S(2)}) async-start(), calls=%async_computation.25 | async-start | bytes 18874368 | tf_op jit(solution)/shard_map/all_gather | solution.py:181
  290.9 891.2 %all-gather.35.cloned.1.call-start = ((), (), s32[]{:S(2)}) async-start(), calls=%async_computation.26 | async-start | bytes 18874368 | tf_op jit(solution)/shard_map/all_gather | solution.py:182
  291.5 930.5 %all-gather.53.cloned.1.call-start = ((), (), s32[]{:S(2)}) async-start(), calls=%async_computation.36 | async-start | bytes 6389760 | tf_op jit(solution)/shard_map/all_gather | solution.py:274
  293.8 1157.9 %all-gather.37.cloned.1.call-start = ((), (), s32[]{:S(2)}) async-start(), calls=%async_computation.27 | async-start | bytes 18874368 | tf_op jit(solution)/shard_map/all_gather | solution.py:183
  294.3 1245.4 %reduce-scatter.37.cloned.1.call-start = ((), (), s32[]{:S(2)}) async-start(), calls=%async_computation.37 | async-start | bytes 573440 | tf_op jit(solution)/shard_map/reduce_scatter | solution.py:331
  691.6 848.1 %reduce-scatter.35.cloned.1.call-start = ((), (), s32[]{:S(2)}) async-start(), calls=%async_computation.35 | async-start | bytes 573440 | tf_op jit(solution)/shard_map/reduce_scatter | solution.py:267
  694.4 1056.8 %reduce-scatter.73.cloned.1.call-start = ((), (), s32[]{:S(2)}) async-start(), calls=%async_computation.55 | async-start | bytes 2359296
  699.0 1054.2 %reduce-scatter.69.cloned.1.call-start = ((), (), s32[]{:S(2)}) async-start(), calls=%async_computation.53 | async-start | bytes 2359296 | tf_op jit(solution)/shard_map/reduce_scatter | solution.py:316
  701.1 1053.9 %reduce-scatter.71.cloned.1.call-start = ((), (), s32[]{:S(2)}) async-start(), calls=%async_computation.54 | async-start | bytes 2359296 | tf_op jit(solution)/shard_map/reduce_scatter | solution.py:319
  703.3 1293.8 %reduce-scatter.63.cloned.1.call-start = ((), (), s32[]{:S(2)}) async-start(), calls=%async_computation.50 | async-start | bytes 18874368 | tf_op jit(solution)/shard_map/reduce_scatter | solution.py:307
  1499.9 783.1 %reduce-scatter.65.cloned.1.call-start = ((), (), s32[]{:S(2)}) async-start(), calls=%async_computation.51 | async-start | bytes 18874368 | tf_op jit(solution)/shard_map/reduce_scatter | solution.py:310
  1518.6 1049.9 %reduce-scatter.67.cloned.1.call-start = ((), (), s32[]{:S(2)}) async-start(), calls=%async_computation.52 | async-start | bytes 18874368 | tf_op jit(solution)/shard_map/reduce_scatter | solution.py:313
  1539.1 1165.4 %reduce-scatter.55.cloned.1.call-start = ((), (), s32[]{:S(2)}) async-start(), calls=%async_computation.46 | async-start | bytes 540672 | tf_op jit(solution)/shard_map/reduce_scatter | solution.py:514
  1559.8 1277.0 %reduce-scatter.61.cloned.1.call-start = ((), (), s32[]{:S(2)}) async-start(), calls=%async_computation.49 | async-start | bytes 540672 | tf_op jit(solution)/shard_map/reduce_scatter | solution.py:517
  1560.9 1409.4 %reduce-scatter.49.cloned.1.call-start = ((), (), s32[]{:S(2)}) async-start(), calls=%async_computation.43 | async-start | bytes 1081344 | tf_op jit(solution)/shard_map/reduce_scatter | solution.py:509
  1562.4 1541.5 %reduce-scatter.51.cloned.1.call-start = ((), (), s32[]{:S(2)}) async-start(), calls=%async_computation.44 | async-start | bytes 1081344 | tf_op jit(solution)/shard_map/reduce_scatter | solution.py:510
  1563.7 1680.1 %reduce-scatter.59.cloned.1.call-start = ((), (), s32[]{:S(2)}) async-start(), calls=%async_computation.48 | async-start | bytes 4325376 | tf_op jit(solution)/shard_map/reduce_scatter | solution.py:516
  1566.6 1824.9 %reduce-scatter.47.cloned.1.call-start = ((), (), s32[]{:S(2)}) async-start(), calls=%async_computation.42 | async-start | bytes 8650752 | tf_op jit(solution)/shard_map/reduce_scatter | solution.py:508
  1571.3 1967.9 %reduce-scatter.53.cloned.1.call-start = ((), (), s32[]{:S(2)}) async-start(), calls=%async_computation.45 | async-start | bytes 8650752 | tf_op jit(solution)/shard_map/reduce_scatter | solution.py:511
  1576.8 2110.1 %reduce-scatter.57.cloned.1.call-start = ((), (), s32[]{:S(2)}) async-start(), calls=%async_computation.47 | async-start | bytes 8650752 | tf_op jit(solution)/shard_map/reduce_scatter | solution.py:515
  1583.3 2239.2 %reduce-scatter.41.cloned.1.call-start = ((), (), s32[]{:S(2)}) async-start(), calls=%async_computation.39 | async-start | bytes 2162688 | tf_op jit(solution)/shard_map/reduce_scatter | solution.py:503
  1717.9 2240.2 %reduce-scatter.43.cloned.1.call-start = ((), (), s32[]{:S(2)}) async-start(), calls=%async_computation.40 | async-start | bytes 2162688 | tf_op jit(solution)/shard_map/reduce_scatter | solution.py:504
  1726.2 2413.8 %reduce-scatter.39.cloned.1.call-start = ((), (), s32[]{:S(2)}) async-start(), calls=%async_computation.38 | async-start | bytes 17301504 | tf_op jit(solution)/shard_map/reduce_scatter | solution.py:502
  1738.2 2589.2 %reduce-scatter.45.cloned.1.call-start = ((), (), s32[]{:S(2)}) async-start(), calls=%async_computation.41 | async-start | bytes 17301504 | tf_op jit(solution)/shard_map/reduce_scatter | solution.py:505
  (127 other events, 7559.1 us)
Sparse Core Ops, SparseCore 0:
  10.9 56.5 all-gather.22
  70.4 52.9 all-gather.24
  126.3 76.4 all-gather.26
  205.5 76.1 all-gather.28
  283.6 51.0 all-gather.50
  337.4 60.7 all-gather.38
  401.1 55.6 all-gather.40
  459.7 61.2 all-gather.42
  523.9 60.5 all-gather.44
  586.5 47.8 all-gather.46
  636.5 47.7 all-gather.48
  726.6 227.5 all-gather.32
  956.2 225.7 all-gather.34
  1223.8 227.7 all-gather.36
  1501.7 67.8 reduce-scatter.72
  1573.6 66.7 reduce-scatter.68
  1643.9 66.6 reduce-scatter.70
  1714.4 282.6 reduce-scatter.62
  2001.4 281.6 reduce-scatter.64
  2286.7 281.6 reduce-scatter.66
  2571.3 133.1 reduce-scatter.54
  2707.2 129.5 reduce-scatter.60
  2839.6 130.6 reduce-scatter.48
  2973.1 130.6 reduce-scatter.50
  3106.8 136.9 reduce-scatter.58
  3246.6 144.8 reduce-scatter.46
  3394.4 144.6 reduce-scatter.52
  3542.2 144.6 reduce-scatter.56
  3689.7 132.7 reduce-scatter.40
  3825.3 132.7 reduce-scatter.42
  3961.1 178.8 reduce-scatter.38
  4142.8 184.5 reduce-scatter.44
  (4 shorter events, 116.4 us)
where the time goes:
time: 4350 us; the launch traced here: 4330 us
  waiting for transfers between devices  3600 us (83%)
  blocking collectives  329 us (8%)
  matrix products  296 us (7%)
    reduce_scatter x1, waiting for transfers between devices, per_device(): lax.psum_scatter(grad_up_pre.astype(jnp.bfloat16), 'dp', scatter_dimensio...  282 us
    reduce_scatter x1, waiting for transfers between devices, per_device(): lax.psum_scatter(grad_down_pre.astype(jnp.bfloat16), 'dp', scatter_dimens...  281 us
    all_gather x1, waiting for transfers between devices, per_device(): lax.all_gather(down_pre, 'dp', axis=1, tiled=True)  230 us
    all_gather x1, waiting for transfers between devices, per_device(): lax.all_gather(gate_pre, 'dp', axis=0, tiled=True)  226 us
    all_gather x1, waiting for transfers between devices, per_device(): lax.all_gather(up_pre, 'dp', axis=0, tiled=True)  211 us
    reduce_scatter x1, waiting for transfers between devices, per_device(): lax.psum_scatter(grad_out_pre, ('dp', 'ctx'), scatter_dimension=0, tiled=...  187 us
    reduce_scatter x1, waiting for transfers between devices, per_device(): lax.psum_scatter(grad_query_pre, ('dp', 'ctx'), scatter_dimension=0, tile...  182 us
    reduce_scatter x1, waiting for transfers between devices, per_device(): lax.psum_scatter(grad_gate_pre.astype(jnp.bfloat16), 'dp', scatter_dimens...  175 us
  transfers between devices with their start and end apart: 40, of which 30 were waited for; matrix products, arithmetic and copies ran while one was open for 10% of the time, Pallas kernels for 0%

commit v1 on v0

v1 whole, which is shorter than its diff:
```python
import math

import jax
import jax.numpy as jnp
from jax import lax
from jax.sharding import PartitionSpec as P

DS = 1024
HEADS = 8
HD = 256
CAMS = 3
PATCH = 192
NTIME = 1000
AXES = ("dp", "ctx")

masked_score = -1e30
F32 = jnp.float32
BF16 = jnp.bfloat16


def rms_norm(values, norm_gain):
    return values * lax.rsqrt(jnp.mean(values * values, axis=-1, keepdims=True) + 1e-06) * norm_gain


def norm_back(values, norm_gain, cotangent):
    _, pullback = jax.vjp(rms_norm, values, norm_gain)
    return pullback(cotangent)


def time_embed(sample_index):
    flow_time = (sample_index.astype(F32) + 0.5) / NTIME
    halves = DS // 2
    fraction = jnp.arange(halves, dtype=F32) / (halves - 1)
    period = 0.004 * jnp.power(1000.0, fraction)
    angles = 2.0 * math.pi * flow_time[..., None] / period
    return jnp.concatenate([jnp.sin(angles), jnp.cos(angles)], axis=-1)


def mm(left, right):
    return jnp.dot(left, right, preferred_element_type=F32)


def mm_tr(left, right):
    return lax.dot_general(left, right, (((1,), (1,)), ((), ())), preferred_element_type=F32)


def outer_sum(left, right):
    return lax.dot_general(left, right, (((0,), (0,)), ((), ())), preferred_element_type=F32)


def ein(spec, left, right):
    return jnp.einsum(spec, left, right, preferred_element_type=F32)


def add_low(left, right):
    return (left.astype(F32) + right.astype(F32)).astype(BF16)


def gate(array, *after):
    return lax.optimization_barrier((array,) + after)[0]


def pad_rows(array, rows):
    return jnp.pad(array, ((0, rows - array.shape[0]), (0, 0)))


def gated_unit(gate_value, up_value):
    return jax.nn.gelu(gate_value, approximate=True) * up_value


def make_body(n, q):
    m = 4 if n >= 8 else n // 2
    high = n // (2 * m)

    def flat(dp, ctx):
        return dp * q + ctx

    def xor_pairs(dp_mask, ctx_mask):
        return [(flat(d, c), flat(d ^ dp_mask, c ^ ctx_mask)) for d in range(n) for c in range(q)]

    swap_c = xor_pairs(0, 1)
    swap_y = xor_pairs(0, 2)
    swap_x = xor_pairs(1, 0)
    swap_high = [xor_pairs(2 * m * 2**i, 0) for i in range(high.bit_length() - 1)]

    def z_step(step, low, end):
        return [
            (flat((h * m + z) * 2 + x, c), flat((h * m + z + step) * 2 + x, c))
            for h in range(high)
            for z in range(low, end)
            for x in range(2)
            for c in range(q)
        ]

    def send(array, pairs):
        return lax.ppermute(array, AXES, pairs)

    def z_xor(array, k):
        return send(array, xor_pairs(2 * k, 0))

    def pick(pieces, index):
        out = pieces[-1]
        for k in range(len(pieces) - 2, -1, -1):
            out = jnp.where(index == k, pieces[k], out)
        return out

    def in_order(bit, mine, other, axis):
        return jnp.where(bit == 0, jnp.stack([mine, other], axis), jnp.stack([other, mine], axis))

    def gather_rows(own, z):
        ups, downs = [], []
        up = down = own
        for s in range(1, m):
            up = send(up, z_step(1, s - 1, m - 1))
            down = send(down, z_step(-1, 1, m - s + 1))
            ups.append(up)
            downs.append(down)
        slots = [own]
        for s in range(1, m):
            slots.append(jnp.where(z + s < m, downs[s - 1], ups[m - s - 1]))
        out = []
        for pair in ((0, 2), (1, 3)):
            near = jnp.concatenate([slots[s] for s in pair])
            near = jnp.concatenate([near, send(near, swap_y)])
            out.append((near, send(near, swap_c)))
        return out

    def scatter_rows(even, odd, rows):
        mine = {}
        for pair, (near, far) in (((1, 3), odd), ((0, 2), even)):
            near = add_low(near, send(far, swap_c))
            near = add_low(near[: 2 * rows], send(near[2 * rows :], swap_y))
            mine[pair[0]], mine[pair[1]] = near[:rows], near[rows:]
        up = down = None
        for s in range(m - 1, 0, -1):
            above = mine[s] if up is None else add_low(mine[s], up)
            up = send(above, z_step(1, 0, m - s))
            below = mine[m - s] if down is None else add_low(mine[m - s], down)
            down = send(below, z_step(-1, s, m))
        return mine[0].astype(F32) + up.astype(F32) + down.astype(F32), up

    def gather_ctx(own):
        pair = jnp.stack([own, send(own, swap_y)])
        return jnp.concatenate([pair, send(pair, swap_c)])

    def scatter_ctx(parts):
        pair = add_low(parts[:2], send(parts[2:], swap_c))
        return pair[0].astype(F32) + send(pair[1], swap_y).astype(F32)

    def gather_light(own, parts, place, after):
        z, x, y, c, highs = place
        pieces = [own] + [z_xor(own, k) for k in range(1, m)]
        lines = jnp.stack([pick(pieces, z ^ t) for t in range(m)])
        for bit, pairs in zip(highs, swap_high, strict=True):
            lines = in_order(bit, lines, send(lines, pairs), 0)
        lines = lines.reshape((high * m,) + own.shape)
        if after:
            lines = gate(lines, *after)
        out, last = [], []
        start = 0
        for at, size in enumerate(parts):
            cut = lines[:, :, start : start + size]
            start += size
            if at % 2 == 0:
                cut = in_order(y, cut, send(cut, swap_y), 1)
                got = send(cut, swap_x)
                cut = in_order(x, cut, got, 1)
            else:
                cut = in_order(x, cut, send(cut, swap_x), 1)
                got = send(cut, swap_y)
                cut = in_order(y, cut, got, 2)
            last.append(got)
            cut = in_order(c, cut, send(cut, swap_c), 3)
            out.append(cut.reshape(n * q * own.shape[0], size))
        return out, pieces[1:], last

    def scatter_light(parts, place):
        z, x, y, c, highs = place

        out = []
        for at, part in enumerate(parts):
            rows = part.shape[0] // (n * q)
            part = fold(part.reshape(high * m, 2, 2, 2, rows, part.shape[1]), c, swap_c, 3)
            if at % 2 == 0:
                part = fold(fold(part, x, swap_x, 1), y, swap_y, 1)
            else:
                part = fold(fold(part, y, swap_y, 2), x, swap_x, 1)
            for bit, pairs in zip(reversed(highs), reversed(swap_high), strict=True):
                part = fold(part.reshape((2, -1) + part.shape[1:]), bit, pairs, 0)
            total = lax.dynamic_index_in_dim(part, z, 0, keepdims=False).astype(F32)
            for k in range(1, m):
                piece = lax.dynamic_index_in_dim(part, z ^ k, 0, keepdims=False)
                total = total + z_xor(piece, k).astype(F32)
            out.append(total)
        return out

    def narrowed(array):
        size = array.shape[-1] // high
        return jnp.concatenate([array[..., i * size : (i + 1) * size] for i in range(high)], axis=-2)

    def widened(array):
        size = array.shape[-2] // high
        return jnp.concatenate([array[..., i * size : (i + 1) * size, :] for i in range(high)], axis=-1)

    def cut(array, index, size, axis):
        return lax.dynamic_slice_in_dim(array, index * size, size, axis)

    def gather_ffn(gate_pre, up_pre, down_pre, gate_act, up_act, down_act, place, after_z, after_x):
        z, x, _, _, highs = place
        w = gate_pre.shape[0]
        cols = gate_pre.shape[1] // m
        w_act = gate_act.shape[0]
        cols_act = gate_act.shape[1] // m
        flat_act = high * w_act

        def exchange(piece_of, after):
            pieces = [piece_of(z)]
            for k in range(1, m):
                pieces.append(z_xor(gate(piece_of(z ^ k), *after), k))
            return pieces

        def down_piece(t):
            last = cut(down_act, t, cols_act, 0)
            return jnp.concatenate(
                [
                    cut(down_pre, t, cols, 0),
                    narrowed(cut(gate_act, t, cols_act, 1)),
                    narrowed(cut(up_act, t, cols_act, 1)),
                    jnp.concatenate([last[: cols_act // 2], last[cols_act // 2 :]], axis=1),
                ],
                axis=0,
            )

        downs = exchange(down_piece, after_z)
        gates = exchange(lambda t: cut(gate_pre, t, cols, 1), downs[1:])
        ups = exchange(lambda t: cut(up_pre, t, cols, 1), gates[1:])

        near = jnp.concatenate([pick(downs, z ^ t) for t in range(m)], axis=1)
        far = send(gate(near, *after_x), swap_x)
        blocks = []
        for t in range(m):
            a, b = near[:, t * w : (t + 1) * w], far[:, t * w : (t + 1) * w]
            blocks += [jnp.where(x == 0, a, b), jnp.where(x == 0, b, a)]
        down_full = jnp.concatenate(blocks, axis=1)
        for bit, pairs in zip(highs, swap_high, strict=True):
            other = send(down_full, pairs)
            down_full = jnp.concatenate(
                [jnp.where(bit == 0, down_full, other), jnp.where(bit == 0, other, down_full)], axis=1
            )

        def rows_of(pieces, after):
            lines = jnp.stack([pick(pieces, z ^ t) for t in range(m)])
            got = send(gate(lines, *after), swap_x)
            full = in_order(x, lines, got, 1).reshape(1, 2 * m * w, cols)
            for bit, pairs in zip(highs, swap_high, strict=True):
                full = in_order(bit, full, send(full, pairs), 0).reshape(1, -1, cols)
            return full.reshape(n * w, cols), got

        gate_full, got = rows_of(gates, (far,))
        up_full, _ = rows_of(ups, (got,))
        narrow = down_full[:cols]

        def rows_act(start):
            part = down_full[start : start + flat_act]
            return jnp.concatenate([widened(part[:, d * w : (d + 1) * w]) for d in range(n)])

        wide_act = (rows_act(cols), rows_act(cols + flat_act))
        last = down_full[cols + 2 * flat_act :]
        narrow_act = jnp.concatenate(
            [
                jnp.concatenate([last[:, d * w : d * w + w_act], last[:, d * w + w_act : (d + 1) * w]])
                for d in range(n)
            ],
            axis=1,
        )
        return (gate_full, up_full), narrow, wide_act, narrow_act, ups[1:]

    def fold(array, bit, pairs, axis):
        theirs = lax.dynamic_index_in_dim(array, 1 - bit, axis, keepdims=False)
        mine = lax.dynamic_index_in_dim(array, bit, axis, keepdims=False)
        return add_low(mine, send(theirs, pairs))

    def scatter_ffn_rows(total, place, after):
        z, x, _, _, highs = place
        part = fold(total.reshape(n // 2, 2, total.shape[0] // n, total.shape[1]), x, swap_x, 1)
        for bit, pairs in zip(reversed(highs), reversed(swap_high), strict=True):
            part = fold(part.reshape((2, -1) + part.shape[1:]), bit, pairs, 0)
        part = gate(part, *after)
        pieces = []
        for k in range(m):
            piece = lax.dynamic_index_in_dim(part, z ^ k, 0, keepdims=False)
            pieces.append(piece if k == 0 else z_xor(piece, k))
        return [pick(pieces, z ^ t) for t in range(m)], pieces[1:]

    def scatter_ffn_columns(total, place, after):
        z, x, _, _, highs = place
        w = total.shape[1] // n
        for bit, pairs in zip(reversed(highs), reversed(swap_high), strict=True):
            half = total.shape[1] // 2
            theirs = jnp.where(bit == 0, total[:, half:], total[:, :half])
            mine = jnp.where(bit == 0, total[:, :half], total[:, half:])
            total = add_low(mine, send(theirs, pairs))
        blocks = [total[:, d * w : (d + 1) * w] for d in range(2 * m)]
        theirs = [jnp.where(x == 0, blocks[2 * t + 1], blocks[2 * t]) for t in range(m)]
        mine = [jnp.where(x == 0, blocks[2 * t], blocks[2 * t + 1]) for t in range(m)]
        got = send(jnp.concatenate(theirs, axis=1), swap_x)
        mine = [add_low(mine[t], got[:, t * w : (t + 1) * w]) for t in range(m)]
        mine[0] = gate(mine[0], *after)
        pieces = []
        for k in range(m):
            piece = pick(mine, z ^ k)
            pieces.append(piece if k == 0 else z_xor(piece, k))
        return [pick(pieces, z ^ t) for t in range(m)], pieces[1:]

    def ffn_unit(rows, wide, narrow):
        gate_value, up_value = mm(rows, wide[0]), mm(rows, wide[1])
        hidden = gated_unit(gate_value, up_value).astype(BF16)
        return gate_value, up_value, hidden, mm(hidden, narrow).astype(BF16)

    def ffn_back(d_hidden, gate_value, up_value, wide):
        _, pullback = jax.vjp(gated_unit, gate_value, up_value)
        d_gate, d_up = pullback(d_hidden)
        d_gate, d_up = d_gate.astype(BF16), d_up.astype(BF16)
        d_rows = (mm_tr(d_gate, wide[0]) + mm_tr(d_up, wide[1])).astype(BF16)
        return d_rows, d_gate, d_up

    def per_device(
        prefix_tokens,
        actions,
        robot_state,
        text_len,
        flow_index,
        query_pre,
        key_pre,
        value_pre,
        out_pre,
        gain_attn_pre,
        gain_ffn_pre,
        query_act,
        key_act,
        value_act,
        out_act,
        gain_attn_act,
        gain_ffn_act,
        action_in,
        mix_first,
        mix_second,
        state_in,
        gate_pre,
        up_pre,
        down_pre,
        gate_act,
        up_act,
        down_act,
        grad_pre,
        grad_act,
    ):
        dp = lax.axis_index("dp")
        ctx = lax.axis_index("ctx")
        z, x = (dp // 2) % m, dp % 2
        y, c = ctx // 2, ctx % 2
        highs = [(dp // (2 * m * 2**i)) % 2 for i in range(len(swap_high))]
        place = (z, x, y, c, highs)
        width = prefix_tokens.shape[2]
        tokens = prefix_tokens.shape[1]
        rows_pre = -(-tokens // 32) * 32
        suffix = grad_act.shape[2]
        rows_act = -(-suffix // 32) * 32
        acts = actions.shape[2]
        devices = n * q
        r64, r32 = query_pre.shape[0], query_act.shape[0]

        pad = jnp.zeros((r64 - r32,), BF16)
        gains = jnp.stack(
            [
                gain_attn_pre,
                gain_ffn_pre,
                jnp.concatenate([gain_attn_act, pad]),
                jnp.concatenate([gain_ffn_act, pad]),
            ],
            axis=1,
        )
        gains = jnp.pad(gains, ((0, 0), (0, 124)))
        first = jnp.concatenate([query_pre, key_pre, value_pre, gains], axis=1)
        small = jnp.pad(jnp.concatenate([action_in, state_in], axis=1), ((0, 0), (0, 64)))
        third = jnp.concatenate(
            [query_act, key_act, value_act, mix_second, mix_first[:r32], mix_first[r32:], small], axis=1
        )
        second = jnp.concatenate([out_pre, out_act], axis=1)
        third = lax.all_gather(third, AXES, axis=0, tiled=True)
        half = width // 2 + HD
        (first_a, first_b), first_z, first_x = gather_light(first, (half, half + 128), place, ())
        (out_a, out_b), out_z, out_x = gather_light(
            gate(second, *first_z), (width, out_act.shape[1]), place, tuple(first_x)
        )
        qkv_w = jnp.concatenate([first_a, first_b[:, :half]], axis=1)
        gain_rows = first_b[:, half:].astype(F32)
        norm_attn, norm_ffn = gain_rows[:, 0], gain_rows[:, 1]
        gain_small = gain_rows[:, 2:4].reshape(devices, r64, 2)[:, :r32].reshape(devices * r32, 2)
        norm_attn_act, norm_ffn_act = gain_small[:, 0], gain_small[:, 1]
        qkv_act_w = third[:, : width + 2 * HD]
        at = width + 2 * HD
        mixer_second = third[:, at : at + DS]
        mixer_first = (
            third[:, at + DS : at + 3 * DS]
            .reshape(devices, r32, 2, DS)
            .transpose(0, 2, 1, 3)
            .reshape(2 * DS, DS)
        )
        action_full = third[:, at + 3 * DS : at + 3 * DS + 32]
        state_full = third[:, at + 3 * DS + 32 : at + 3 * DS + 64]
        out_w, out_act_w = out_a, out_b

        wide, narrow, wide_act, narrow_act, ffn_z = gather_ffn(
            gate_pre, up_pre, down_pre, gate_act, up_act, down_act, place, tuple(out_z), tuple(out_x)
        )
        sharing = [
            [flat((h * m + a) * 2 + b, d) for a in range(m) for d in range(q)]
            for h in range(high)
            for b in range(2)
        ]

        def gather_act(block):
            return lax.all_gather(block, AXES, axis=0, tiled=True, axis_index_groups=sharing)

        def scatter_act(block):
            return lax.psum_scatter(
                block, AXES, scatter_dimension=0, tiled=True, axis_index_groups=sharing
            ).astype(F32)

        (cot_e0, cot_e1), (cot_o0, cot_o1) = gather_rows(
            gate(pad_rows(grad_pre[0], rows_pre), *ffn_z), z
        )
        cot_all_act = gather_act(pad_rows(grad_act[0, 0], rows_act))

        time_rows = time_embed(flow_index[0, 0])
        action_emb = mm_tr(actions[0, 0], action_full)
        mix_input = jnp.concatenate(
            [action_emb, jnp.broadcast_to(time_rows[None, :], action_emb.shape)], axis=-1
        ).astype(BF16)
        pre_mix = mm(mix_input, mixer_first)
        mixed_act = jax.nn.silu(pre_mix).astype(BF16)
        action_rows = mm(mixed_act, mixer_second)
        state_row = mm_tr(robot_state, state_full)
        side_input = pad_rows(jnp.concatenate([state_row, action_rows], axis=0), rows_act)

        prefix_in = pad_rows(prefix_tokens[0], rows_pre).astype(F32)
        normed_pre = rms_norm(prefix_in, norm_attn).astype(BF16)
        normed_act = rms_norm(side_input, norm_attn_act).astype(BF16)
        qkv_pre = mm(normed_pre, qkv_w).astype(BF16)
        qkv_act = mm(normed_act, qkv_act_w).astype(BF16)
        queries_pre = qkv_pre[:, :width].reshape(rows_pre, HEADS, HD)
        queries_act = qkv_act[:, :width].reshape(rows_act, HEADS, HD)
        keys_act = qkv_act[:, width : width + HD]
        values_act = qkv_act[:, width + HD :]
        both_kv = gather_ctx(qkv_pre[:, width:]).reshape(q * rows_pre, 2 * HD)
        keys, values = both_kv[:, :HD], both_kv[:, HD:]
        key_count = q * rows_pre

        order = jnp.array([0, 2, 1, 3])
        spot = jnp.arange(rows_pre)
        positions = (ctx ^ order)[:, None] * tokens + spot[None, :]
        camera_rows = CAMS * PATCH
        key_valid = (positions < camera_rows) | (positions - camera_rows < text_len[0])
        key_valid = (key_valid & (spot < tokens)[None, :]).reshape(-1)
        scale = HD ** (-0.5)

        def prefix_scores():
            scores = ein("qhd,kd->hqk", queries_pre, keys) * scale
            return jnp.where(key_valid[None, None, :], scores, masked_score)

        groups = jnp.arange(rows_act) > 0
        own_block = (groups[None, :] <= groups[:, None]) & (jnp.arange(rows_act) < suffix)[None, :]

        def side_scores():
            far = ein("qhd,kd->hqk", queries_act, keys) * scale
            far = jnp.where(key_valid[None, None, :], far, masked_score)
            near = ein("qhd,kd->hqk", queries_act, keys_act) * scale
            near = jnp.where(own_block[None], near, masked_score)
            return jnp.concatenate([far, near], axis=-1)

        def soft_rows(scores):
            highest = jnp.max(scores, axis=-1, keepdims=True)
            totals = jnp.sum(jnp.exp(scores - highest), axis=-1, keepdims=True)
            log_total = highest + jnp.log(totals)
            return jnp.exp(scores - log_total), log_total

        probs_pre, total_pre = soft_rows(prefix_scores())
        attn_pre = ein("hqk,kd->qhd", probs_pre.astype(BF16), values)
        attn_pre = attn_pre.reshape(rows_pre, width).astype(BF16)
        probs_act, total_act = soft_rows(side_scores())
        probs_act_low = probs_act.astype(BF16)
        attn_act = ein("hqk,kd->qhd", probs_act_low[..., :key_count], values) + ein(
            "hqk,kd->qhd", probs_act_low[..., key_count:], values_act
        )
        attn_act = attn_act.reshape(rows_act, width).astype(BF16)
        mid_pre = prefix_in + mm(attn_pre, out_w)
        mid_act = side_input + mm(attn_act, out_act_w)
        normed_two_pre = rms_norm(mid_pre, norm_ffn).astype(BF16)
        normed_two_act = rms_norm(mid_act, norm_ffn_act).astype(BF16)

        (row_e0, row_e1), (row_o0, row_o1) = gather_rows(normed_two_pre, z)
        rows = (row_o1, row_o0, row_e1, row_e0)
        cots = (cot_o1, cot_o0, cot_e1, cot_e0)
        rows_all_act = gather_act(normed_two_act)
        units = [ffn_unit(r, wide, narrow) for r in rows]
        gate_act_value, up_act_value, hidden_act, part_act = ffn_unit(rows_all_act, wide_act, narrow_act)
        parts = [unit[3] for unit in units]
        branch, branch_last = scatter_rows((parts[3], parts[2]), (parts[1], parts[0]), rows_pre)
        out_prefix = (mid_pre + branch)[:tokens]
        out_actions = (mid_act + scatter_act(part_act))[:suffix]

        backs = [
            ffn_back(mm_tr(cot, narrow), unit[0], unit[1], wide)
            for cot, unit in zip(cots, units, strict=True)
        ]
        d_branch, d_last = scatter_rows((backs[3][0], backs[2][0]), (backs[1][0], backs[0][0]), rows_pre)
        d_rows_act, d_gate_act, d_up_act = ffn_back(
            mm_tr(cot_all_act, narrow_act), gate_act_value, up_act_value, wide_act
        )
        d_branch_act = scatter_act(d_rows_act)

        cols_act = gate_act.shape[1] // m
        w_act = gate_act.shape[0]
        w = gate_pre.shape[0]
        cols = gate_pre.shape[1] // m
        flat_act = high * w_act
        rows_join = jnp.concatenate(rows)
        grad_down_act = outer_sum(hidden_act, cot_all_act).astype(BF16)
        half_act = cols_act // 2

        def blocks_act(total):
            return jnp.concatenate(
                [narrowed(total[d * w_act : (d + 1) * w_act]) for d in range(n)], axis=1
            )

        narrow_parts = jnp.concatenate(
            [
                outer_sum(jnp.concatenate([unit[2] for unit in units]), jnp.concatenate(cots)).astype(BF16),
                blocks_act(outer_sum(rows_all_act, d_gate_act).astype(BF16)),
                blocks_act(outer_sum(rows_all_act, d_up_act).astype(BF16)),
                jnp.concatenate(
                    [
                        grad_down_act[at : at + half_act, d * w_act : (d + 1) * w_act]
                        for d in range(n)
                        for at in (0, half_act)
                    ],
                    axis=1,
                ),
            ],
            axis=0,
        )
        grad_gate = outer_sum(rows_join, jnp.concatenate([back[1] for back in backs])).astype(BF16)
        grad_up = outer_sum(rows_join, jnp.concatenate([back[2] for back in backs])).astype(BF16)
        down_got, down_z = scatter_ffn_columns(narrow_parts, place, (d_last,))
        gate_got, gate_z = scatter_ffn_rows(grad_gate, place, tuple(down_z))
        up_got, _ = scatter_ffn_rows(grad_up, place, tuple(gate_z))

        def beside(pieces):
            return jnp.concatenate(pieces, axis=1).astype(F32)

        grad_gate_pre = beside(gate_got)
        grad_up_pre = beside(up_got)
        grad_down_pre = jnp.concatenate([g[:cols] for g in down_got]).astype(F32)
        grad_gate_act = beside([widened(g[cols : cols + flat_act]) for g in down_got])
        grad_up_act = beside([widened(g[cols + flat_act : cols + 2 * flat_act]) for g in down_got])
        last = [g[cols + 2 * flat_act :] for g in down_got]
        grad_down_act = jnp.concatenate([g[:, at : at + w_act] for g in last for at in (0, w_act)])
        grad_down_act = grad_down_act.astype(F32)

        d_mid_pre, grad_norm_ffn = norm_back(mid_pre, norm_ffn, d_branch)
        d_mid_pre = d_mid_pre + pad_rows(grad_pre[0], rows_pre).astype(F32)
        d_mid_act, grad_norm_ffn_act = norm_back(mid_act, norm_ffn_act, d_branch_act)
        d_mid_act = d_mid_act + pad_rows(grad_act[0, 0], rows_act).astype(F32)
        d_mid_low = d_mid_pre.astype(BF16)
        d_mid_act_low = d_mid_act.astype(BF16)
        grad_out_pre = outer_sum(attn_pre, d_mid_low).astype(BF16)
        grad_out_act = outer_sum(attn_act, d_mid_act_low).astype(BF16)
        got_second = lax.psum_scatter(
            jnp.concatenate([grad_out_pre, grad_out_act], axis=1), AXES, scatter_dimension=0, tiled=True
        ).astype(F32)

        d_attn_pre = mm_tr(d_mid_low, out_w).astype(BF16).reshape(rows_pre, HEADS, HD)
        d_attn_act = mm_tr(d_mid_act_low, out_act_w).astype(BF16).reshape(rows_act, HEADS, HD)
        probs_pre = jnp.exp(prefix_scores() - total_pre)
        d_probs = ein("qhd,kd->hqk", d_attn_pre, values)
        d_scores = probs_pre * (d_probs - jnp.sum(probs_pre * d_probs, axis=-1, keepdims=True))
        d_scores = d_scores.astype(BF16)
        d_query_pre = (ein("hqk,kd->qhd", d_scores, keys) * scale).reshape(rows_pre, width).astype(BF16)
        key_terms = ein("hqk,qhd->kd", d_scores, queries_pre)
        value_terms = ein("hqk,qhd->kd", probs_pre.astype(BF16), d_attn_pre)

        probs_act = jnp.exp(side_scores() - total_act)
        probs_act_low = probs_act.astype(BF16)
        d_probs_act = jnp.concatenate(
            [ein("qhd,kd->hqk", d_attn_act, values), ein("qhd,kd->hqk", d_attn_act, values_act)], axis=-1
        )
        d_scores_act = probs_act * (
            d_probs_act - jnp.sum(probs_act * d_probs_act, axis=-1, keepdims=True)
        )
        d_scores_act = d_scores_act.astype(BF16)
        far, near = d_scores_act[..., :key_count], d_scores_act[..., key_count:]
        d_query_act = ein("hqk,kd->qhd", far, keys) + ein("hqk,kd->qhd", near, keys_act)
        d_query_act = (d_query_act * scale).reshape(rows_act, width).astype(BF16)
        key_terms = (key_terms + ein("hqk,qhd->kd", far, queries_act)) * scale
        value_terms = value_terms + ein("hqk,qhd->kd", probs_act_low[..., :key_count], d_attn_act)
        d_keys_act = (ein("hqk,qhd->kd", near, queries_act) * scale).astype(BF16)
        d_values_act = ein("hqk,qhd->kd", probs_act_low[..., key_count:], d_attn_act).astype(BF16)
        kv_terms = jnp.concatenate([key_terms, value_terms], axis=1).astype(BF16)
        d_kv = scatter_ctx(kv_terms.reshape(q, rows_pre, 2 * HD)).astype(BF16)

        d_qkv_pre = jnp.concatenate([d_query_pre, d_kv], axis=1)
        d_qkv_act = jnp.concatenate([d_query_act, d_keys_act, d_values_act], axis=1)
        d_normed_pre = mm_tr(d_qkv_pre, qkv_w)
        d_normed_act = mm_tr(d_qkv_act, qkv_act_w)
        grad_qkv_pre = outer_sum(normed_pre, d_qkv_pre).astype(BF16)
        grad_qkv_act = outer_sum(normed_act, d_qkv_act).astype(BF16)
        grad_prefix, grad_norm_attn = norm_back(prefix_in, norm_attn, d_normed_pre)
        grad_prefix = (grad_prefix + d_mid_pre)[:tokens]
        d_side, grad_norm_attn_act = norm_back(side_input, norm_attn_act, d_normed_act)
        d_side = d_side + d_mid_act
        grad_state_in = outer_sum(d_side[:1].astype(BF16), robot_state)
        d_action_rows = d_side[1 : 1 + acts].astype(BF16)
        grad_mix_second = outer_sum(mixed_act, d_action_rows).astype(BF16)
        d_mixed = mm_tr(d_action_rows, mixer_second)
        _, silu_back = jax.vjp(jax.nn.silu, pre_mix)
        d_pre_mix = silu_back(d_mixed)[0].astype(BF16)
        grad_mix_first = outer_sum(mix_input, d_pre_mix).astype(BF16)
        d_action_emb = mm_tr(d_pre_mix, mixer_first[:DS]).astype(BF16)
        grad_action_in = outer_sum(d_action_emb, actions[0, 0])
        grad_actions = mm(d_action_emb, action_full)

        act_gains = jnp.stack([grad_norm_attn_act, grad_norm_ffn_act], axis=1).reshape(devices, r32, 2)
        act_gains = jnp.pad(act_gains, ((0, 0), (0, r64 - r32), (0, 0))).reshape(devices * r64, 2)
        gain_grads = jnp.concatenate(
            [jnp.stack([grad_norm_attn, grad_norm_ffn], axis=1), act_gains], axis=1
        ).astype(BF16)
        gain_grads = jnp.pad(gain_grads, ((0, 0), (0, 124)))
        got_first = scatter_light(
            [grad_qkv_pre[:, :half], jnp.concatenate([grad_qkv_pre[:, half:], gain_grads], axis=1)], place
        )
        got_first = jnp.concatenate(got_first, axis=1)
        small_grads = jnp.pad(
            jnp.concatenate([grad_action_in, grad_state_in], axis=1).astype(BF16), ((0, 0), (0, 64))
        )
        mix_first_rows = (
            grad_mix_first.reshape(devices, 2, r32, DS).transpose(0, 2, 1, 3).reshape(devices * r32, 2 * DS)
        )
        mixes = jnp.concatenate([grad_mix_second, mix_first_rows, small_grads], axis=1)
        got_third = jnp.concatenate(scatter_light([grad_qkv_act, mixes], place), axis=1)

        wide_end = width + 2 * HD
        tail = got_third[:, at + 3 * DS :]
        return (
            out_prefix[None],
            out_actions[None, None],
            grad_prefix[None],
            grad_actions[None, None],
            got_first[:, :width],
            got_first[:, width : width + HD],
            got_first[:, width + HD : wide_end],
            got_second[:, :width],
            got_first[:, wide_end],
            got_first[:, wide_end + 1],
            got_third[:, :width],
            got_third[:, width : width + HD],
            got_third[:, width + HD : wide_end],
            got_second[:, width:],
            got_first[:r32, wide_end + 2],
            got_first[:r32, wide_end + 3],
            tail[:, :32],
            jnp.concatenate([got_third[:, at + DS : at + 2 * DS], got_third[:, at + 2 * DS : at + 3 * DS]]),
            got_third[:, at : at + DS],
            tail[:, 32:64],
            grad_gate_pre,
            grad_up_pre,
            grad_down_pre,
            grad_gate_act,
            grad_up_act,
            grad_down_act,
        )

    return per_device


def solution(mesh):
    rows = P(("dp", "ctx"), None)
    line = P(("dp", "ctx"))
    return jax.shard_map(
        make_body(mesh.shape["dp"], mesh.shape["ctx"]),
        mesh=mesh,
        in_specs=(
            P("dp", "ctx", None),
            P("dp", "ctx", None, None),
            P("dp", None),
            P("dp"),
            P("dp", "ctx"),
            rows,
            rows,
            rows,
            rows,
            line,
            line,
            rows,
            rows,
            rows,
            rows,
            line,
            line,
            rows,
            rows,
            rows,
            rows,
            P("dp", "ctx"),
            P("dp", "ctx"),
            P("ctx", "dp"),
            P("dp", "ctx"),
            P("dp", "ctx"),
            P("ctx", "dp"),
            P("dp", "ctx", None),
            P("dp", "ctx", None, None),
        ),
        out_specs=(
            P("dp", "ctx", None),
            P("dp", "ctx", None, None),
            P("dp", "ctx", None),
            P("dp", "ctx", None, None),
            rows,
            rows,
            rows,
            rows,
            line,
            line,
            rows,
            rows,
            rows,
            rows,
            line,
            line,
            rows,
            rows,
            rows,
            rows,
            P("dp", "ctx"),
            P("dp", "ctx"),
            P("ctx", "dp"),
            P("dp", "ctx"),
            P("dp", "ctx"),
            P("ctx", "dp"),
        ),
        check_vma=False,
    )
```

time: 4350 us -> 1580 us (0.36)
  waiting for transfers between devices: 3600 us -> 672 us
  blocking collectives: 329 us -> 0 us
  starting transfers between devices: 14.8 us -> 241 us
  other arithmetic: 30.7 us -> 194 us
  local copies, waits for them, and re-layouts: 42.2 us -> 174 us
    reduce_scatter x19 -> x2, waiting for transfers between devices: 2490 us -> 34.4 us  [scatter_act(): lax.psum_scatter(block, AXES, scatter_dimension=0, tiled=True, axis_index...]
    all_gather x16 -> x3, waiting for transfers between devices: 1100 us -> 0.02 us  [the longest x2 0.02 us: gather_act(): lax.all_gather(block, AXES, axis=0, tiled=True, axis_index_groups=sharing)]
    ppermute x0 -> x110, waiting for transfers between devices: none -> 638 us  [send(): return lax.ppermute(array, AXES, pairs)]
    ppermute x0 -> x110, starting transfers between devices: none -> 240 us  [send(): return lax.ppermute(array, AXES, pairs)]
    all_gather x8 -> x0, blocking collectives: 184 us -> none  [the longest x1 40.8 us: per_device(): lax.all_gather(action_in, ('dp', 'ctx'), axis=0, tiled=True)]
    unnamed x4 -> x0, blocking collectives: 145 us -> none
    select_n x0 -> x38, other arithmetic: none -> 63.5 us  [the longest x23 49.6 us: in_order(): jnp.where(bit == 0, jnp.stack([mine, other], axis), jnp.stack([other, min...]
    concatenate x0 -> x28, other arithmetic: none -> 48.7 us  [the longest x1 14.8 us: per_device(): jnp.concatenate([grad_out_pre, grad_out_act], axis=1)]
  transfers between devices with their start and end apart: 40 -> 116, of which waited for: 30 -> 53; matrix products, arithmetic and copies ran while one was open for 10% -> 37% of each run, Pallas kernels for 0% -> 0%
where the time goes in v1:
time: 1580 us; the launch traced here: 1570 us
  waiting for transfers between devices  672 us (43%)
  matrix products  267 us (17%)
  starting transfers between devices  241 us (15%)
  other arithmetic  194 us (12%)
  local copies, waits for them, and re-layouts  174 us (11%)
  between operations  20.3 us (1%)
    ppermute x110, waiting for transfers between devices, send(): return lax.ppermute(array, AXES, pairs)  638 us
    ppermute x110, starting transfers between devices, send(): return lax.ppermute(array, AXES, pairs)  240 us
    dot_general x23, matrix products, mm_tr(): lax.dot_general(left, right, (((1,), (1,)), ((), ())), preferred_element_...  96 us
    dot_general x22, matrix products, mm(): return jnp.dot(left, right, preferred_element_type=F32)  86.3 us
    unnamed x462, local copies, waits for them, and re-layouts  83.2 us
    dot_general x13, matrix products, outer_sum(): lax.dot_general(left, right, (((0,), (0,)), ((), ())), preferred_element_...  71.3 us
    select_n x23, other arithmetic, in_order(): jnp.where(bit == 0, jnp.stack([mine, other], axis), jnp.stack([other, min...  49.6 us
    convert_element_type x26, other arithmetic, add_low(): return (left.astype(F32) + right.astype(F32)).astype(BF16)  35.8 us
  transfers between devices with their start and end apart: 116, of which 53 were waited for; matrix products, arithmetic and copies ran while one was open for 37% of the time, Pallas kernels for 0%

profile of v1, /device:TPU:0, one launch (start us, length us, event | category | flops | bytes accessed | tf_op | source)
XLA Modules:
  0.0 1567.9 jit_solution(2916980588364345996)
XLA Ops:
  40.2 11.0 collective-permute-done.1
  69.7 24.2 %collective-permute-done.12 = bf16[64,3072]{1,0:T(8,128)(2,1)S(1)} collective-permute-done((bf16[64,3072]{1,0:T(8,128)(2,1)S(1)}, bf16[64,3072]{1,0:T(8,128)(2,1)S(1)}, u32[]{:S(2)}, u32[]{:S(2)}) %collective-permute-start.12) | collective-permute-done | bytes 393248 | tf_op jit(solution)/shard_map/ppermute | solution.py:96
  103.3 15.6 collective-permute-done.24
  118.9 24.6 %collective-permute-done.22 = bf16[1408,256]{1,0:T(8,128)(2,1)S(1)} collective-permute-done((bf16[1408,256]{1,0:T(8,128)(2,1)S(1)}, bf16[1408,256]{1,0:T(8,128)(2,1)S(1)}, u32[]{:S(2)}, u32[]{:S(2)}) %collective-permute-start.22) | collective-permute-done | bytes 720928 | tf_op jit(solution)/shard_map/ppermute | solution.py:96
  143.5 36.6 %collective-permute-done.23 = bf16[1408,256]{1,0:T(8,128)(2,1)S(1)} collective-permute-done((bf16[1408,256]{1,0:T(8,128)(2,1)S(1)}, bf16[1408,256]{1,0:T(8,128)(2,1)S(1)}, u32[]{:S(2)}, u32[]{:S(2)}) %collective-permute-start.23) | collective-permute-done | bytes 720928 | tf_op jit(solution)/shard_map/ppermute | solution.py:96
  187.5 39.6 %collective-permute-done.25 = bf16[256,1024]{1,0:T(8,128)(2,1)S(1)} collective-permute-done((bf16[256,1024]{1,0:T(8,128)(2,1)S(1)}, bf16[256,1024]{1,0:T(8,128)(2,1)S(1)}, u32[]{:S(2)}, u32[]{:S(2)}) %collective-permute-start.25) | collective-permute-done | bytes 524320 | tf_op jit(solution)/shard_map/ppermute | solution.py:96
  246.6 12.0 collective-permute-start.32
  281.5 15.3 collective-permute-done.33
  296.8 12.2 collective-permute-start.54
  367.0 14.7 collective-permute-done.56
  429.1 15.1 maximum_select_fusion.6
  452.4 22.9 %collective-permute-done.30 = bf16[1408,1024]{1,0:T(8,128)(2,1)S(1)} collective-permute-done((bf16[1408,1024]{1,0:T(8,128)(2,1)}, bf16[1408,1024]{1,0:T(8,128)(2,1)S(1)}, u32[]{:S(2)}, u32[]{:S(2)}) %collective-permute-start.30) | collective-permute-done | bytes 2883616 | tf_op jit(solution)/shard_map/ppermute | solution.py:96
  556.6 11.4 collective-permute-done.40
  569.6 13.1 collective-permute-done.21
  687.9 14.3 fusion.39
  702.3 16.6 %fusion.45 = bf16[2048,1024]{1,0:T(8,128)(2,1)S(1)} fusion(bf16[2560,2048]{1,0:T(8,128)(2,1)} %copy-done.97, bf16[640,1024]{1,0:T(8,128)(2,1)S(1)} %copy-done.174, bf16[640,1024]{1,0:T(8,128)(2,1)} %get-tuple-element.244, bf16[640,1024]{1,0:T(8,128)(2,1)} %get-tuple-element.247, bf16[640,1024]{1,0:T(8,128)(2,1)} %get-tuple-element.250), kind=kOutput, calls=%fused_computation.75 | convolution fusion | flops 10760486912 | bytes 19922944 | tf_op jit(solution)/shard_map/dot_general | solution.py:48
  729.5 15.3 fusion.42
  767.1 16.8 %collective-permute-done.38 = bf16[320,2048]{1,0:T(8,128)(2,1)S(1)} collective-permute-done((bf16[320,2048]{1,0:T(8,128)(2,1)S(1)}, bf16[320,2048]{1,0:T(8,128)(2,1)S(1)}, u32[]{:S(2)}, u32[]{:S(2)}) %collective-permute-start.38) | collective-permute-done | bytes 1310752 | tf_op jit(solution)/shard_map/ppermute | solution.py:96
  785.6 26.4 %collective-permute-done.59 = bf16[320,2048]{1,0:T(8,128)(2,1)S(1)} collective-permute-done((bf16[320,2048]{1,0:T(8,128)(2,1)S(1)}, bf16[320,2048]{1,0:T(8,128)(2,1)S(1)}, u32[]{:S(2)}, u32[]{:S(2)}) %collective-permute-start.59) | collective-permute-done | bytes 1310752 | tf_op jit(solution)/shard_map/ppermute | solution.py:96
  813.7 26.4 %collective-permute-done.44 = bf16[320,2048]{1,0:T(8,128)(2,1)S(1)} collective-permute-done((bf16[320,2048]{1,0:T(8,128)(2,1)S(1)}, bf16[320,2048]{1,0:T(8,128)(2,1)S(1)}, u32[]{:S(2)}, u32[]{:S(2)}) %collective-permute-start.44) | collective-permute-done | bytes 1310752 | tf_op jit(solution)/shard_map/ppermute | solution.py:96
  849.4 17.9 %collective-permute-done.65 = bf16[320,2048]{1,0:T(8,128)(2,1)S(1)} collective-permute-done((bf16[320,2048]{1,0:T(8,128)(2,1)S(1)}, bf16[320,2048]{1,0:T(8,128)(2,1)S(1)}, u32[]{:S(2)}, u32[]{:S(2)}) %collective-permute-start.65) | collective-permute-done | bytes 1310752 | tf_op jit(solution)/shard_map/ppermute | solution.py:96
  942.9 13.1 collective-permute-done.67
  1044.0 39.5 %collective-permute-done.99 = bf16[1408,1024]{1,0:T(8,128)(2,1)} collective-permute-done((bf16[1408,1024]{1,0:T(8,128)(2,1)}, bf16[1408,1024]{1,0:T(8,128)(2,1)}, u32[]{:S(2)}, u32[]{:S(2)}) %collective-permute-start.99) | collective-permute-done | bytes 2883616 | tf_op jit(solution)/shard_map/ppermute | solution.py:96
  1121.0 34.4 %reduce-scatter.6.cloned.1.call-done = bf16[64,1024]{1,0:T(8,128)(2,1)} async-done(((bf16[1024,1024]{1,0:T(8,128)(2,1)}), bf16[64,1024]{1,0:T(8,128)(2,1)}) %reduce-scatter.6.cloned.1.call-update) | async-done | bytes 131088 | tf_op jit(solution)/shard_map/reduce_scatter | solution.py:427
  1193.8 14.8 pad_maximum_fusion
  1215.0 16.6 %copy.328 = bf16[2048,3072]{1,0:T(8,128)(2,1)} copy(bf16[2048,3072]{0,1:T(8,128)(2,1)} %pad_maximum_fusion) | data formatting | bytes 25165824
  1290.2 25.0 %collective-permute-start.108 = (bf16[256,1024]{1,0:T(8,128)(2,1)S(1)}, bf16[256,1024]{1,0:T(8,128)(2,1)S(1)}, u32[]{:S(2)}, u32[]{:S(2)}) collective-permute-start(bf16[256,1024]{1,0:T(8,128)(2,1)S(1)} %get-tuple-element.283), channel_id=1, source_target_pairs={{0,16},{1,17},{2,18},{3,19},{4,20},{5,21},{6,22},{7,23},{8,24},{9,... | collective-permute-start | bytes 1572872 | tf_op jit(solution)/shard_map/ppermute | solution.py:96
  1317.0 42.6 %collective-permute-start.107 = (bf16[256,1024]{1,0:T(8,128)(2,1)S(1)}, bf16[256,1024]{1,0:T(8,128)(2,1)S(1)}, u32[]{:S(2)}, u32[]{:S(2)}) collective-permute-start(bf16[256,1024]{1,0:T(8,128)(2,1)S(1)} %get-tuple-element.284), channel_id=1, source_target_pairs={{0,8},{1,9},{2,10},{3,11},{4,12},{5,13},{6,14},{7,15},{8,0},{9,1},... | collective-permute-start | bytes 1572872 | tf_op jit(solution)/shard_map/ppermute | solution.py:96
  1371.0 14.8 collective-permute-done.107
  1401.6 25.6 %collective-permute-done.87 = bf16[4,2,32,2560]{3,2,0,1:T(8,128)(2,1)} collective-permute-done((bf16[4,2,32,2560]{3,2,0,1:T(8,128)(2,1)}, bf16[4,2,32,2560]{3,2,0,1:T(8,128)(2,1)}, u32[]{:S(2)}, u32[]{:S(2)}) %collective-permute-start.87) | collective-permute-done | bytes 1310752 | tf_op jit(solution)/shard_map/ppermute | solution.py:96
  1431.3 23.1 %collective-permute-done.75 = bf16[4,2,64,1280]{3,2,0,1:T(8,128)(2,1)S(1)} collective-permute-done((bf16[4,2,64,1280]{3,2,0,1:T(8,128)(2,1)S(1)}, bf16[4,2,64,1280]{3,2,0,1:T(8,128)(2,1)S(1)}, u32[]{:S(2)}, u32[]{:S(2)}) %collective-permute-start.75) | collective-permute-done | bytes 1310752 | tf_op jit(solution)/shard_map/ppermute | solution.py:96
  1473.5 13.7 collective-permute-done.81
  (1038 shorter events, 882.3 us)
Async XLA Ops:
  7.3 478.3 %all-gather.8.cloned.1.call-start = ((), (), s32[]{:S(2)}) async-start(), calls=%async_computation.6 | async-start | bytes 2228224 | tf_op jit(solution)/shard_map/all_gather | solution.py:424
  9.0 867.5 %all-gather.4.cloned.1.call-start = ((), (), s32[]{:S(2)}) async-start(), calls=%async_computation.3 | async-start | bytes 12165120 | tf_op jit(solution)/shard_map/all_gather | solution.py:390
  28.0 955.8 %all-gather.6.cloned.1.call-start = ((), (), s32[]{:S(2)}) async-start(), calls=%async_computation.4 | async-start | bytes 2228224 | tf_op jit(solution)/shard_map/all_gather | solution.py:424
  95.7 84.4 %collective-permute-start.23 = (bf16[1408,256]{1,0:T(8,128)(2,1)S(1)}, bf16[1408,256]{1,0:T(8,128)(2,1)S(1)}, u32[]{:S(2)}, u32[]{:S(2)}) collective-permute-start(bf16[1408,256]{1,0:T(8,128)(2,1)S(1)} %maximum_maximum_fusion.1), channel_id=1, source_target_pairs={{0,16},{1,17},{2,18},{3,19},{4,20},{5,21},{6,22},{7,23},{8,24},{9,... | collective-permute-start | bytes 2162696 | tf_op jit(solution)/shard_map/ppermute | solution.py:96
  99.0 165.9 %collective-permute-start.7 = (bf16[4,2,64,1280]{3,2,0,1:T(8,128)(2,1)S(1)}, bf16[4,2,64,1280]{3,2,0,1:T(8,128)(2,1)S(1)}, u32[]{:S(2)}, u32[]{:S(2)}) collective-permute-start(bf16[4,2,64,1280]{3,2,0,1:T(8,128)(2,1)S(1)} %maximum_select_fusion.15), channel_id=1, source_target_pairs={{0,4},{1,5},{2,6},{3,7},{4,0},{5,1},{6,2},{7,3},{8,12},{9,13},{10,... | collective-permute-start | bytes 3932168 | tf_op jit(solution)/shard_map/ppermute | solution.py:96
  101.2 164.7 %collective-permute-start.4 = (bf16[4,2,64,1408]{3,2,1,0:T(8,128)(2,1)S(1)}, bf16[4,2,64,1408]{3,2,1,0:T(8,128)(2,1)S(1)}, u32[]{:S(2)}, u32[]{:S(2)}) collective-permute-start(bf16[4,2,64,1408]{3,2,1,0:T(8,128)(2,1)S(1)} %maximum_select_fusion.13), channel_id=1, source_target_pairs={{0,2},{1,3},{2,0},{3,1},{4,6},{5,7},{6,4},{7,5},{8,10},{9,11},{10,... | collective-permute-start | bytes 4325384 | tf_op jit(solution)/shard_map/ppermute | solution.py:96
  265.4 95.7 %collective-permute-start.8 = (bf16[4,2,2,64,1280]{4,3,0,2,1:T(8,128)(2,1)S(1)}, bf16[4,2,2,64,1280]{4,3,0,2,1:T(8,128)(2,1)}, u32[]{:S(2)}, u32[]{:S(2)}) collective-permute-start(bf16[4,2,2,64,1280]{4,3,0,2,1:T(8,128)(2,1)S(1)} %maximum_select_fusion.9), channel_id=1, source_target_pairs={{0,1},{1,0},{2,3},{3,2},{4,5},{5,4},{6,7},{7,6},{8,9},{9,8},{10,11... | collective-permute-start | bytes 7864328 | tf_op jit(solution)/shard_map/ppermute | solution.py:96
  314.7 68.8 %collective-permute-start.5 = (bf16[4,2,2,64,1408]{4,3,2,1,0:T(8,128)(2,1)}, bf16[4,2,2,64,1408]{4,3,2,1,0:T(8,128)(2,1)}, u32[]{:S(2)}, u32[]{:S(2)}) collective-permute-start(bf16[4,2,2,64,1408]{4,3,2,1,0:T(8,128)(2,1)} %maximum_select_fusion.7), channel_id=1, source_target_pairs={{0,1},{1,0},{2,3},{3,2},{4,5},{5,4},{6,7},{7,6},{8,9},{9,8},{10,11... | collective-permute-start | bytes 8650760 | tf_op jit(solution)/shard_map/ppermute | solution.py:96
  330.0 80.2 %collective-permute-start.15 = (bf16[4,2,64,2048]{3,2,1,0:T(8,128)(2,1)}, bf16[4,2,64,2048]{3,2,1,0:T(8,128)(2,1)}, u32[]{:S(2)}, u32[]{:S(2)}) collective-permute-start(bf16[4,2,64,2048]{3,2,1,0:T(8,128)(2,1)} %maximum_select_fusion.10), channel_id=1, source_target_pairs={{0,4},{1,5},{2,6},{3,7},{4,0},{5,1},{6,2},{7,3},{8,12},{9,13},{10,... | collective-permute-start | bytes 6291464 | tf_op jit(solution)/shard_map/ppermute | solution.py:96
  359.7 68.7 %collective-permute-start.51 = (bf16[4,2,2,64,1024]{4,3,0,2,1:T(8,128)(2,1)}, bf16[4,2,2,64,1024]{4,3,0,2,1:T(8,128)(2,1)}, u32[]{:S(2)}, u32[]{:S(2)}) collective-permute-start(bf16[4,2,2,64,1024]{4,3,0,2,1:T(8,128)(2,1)} %maximum_select_fusion.12), channel_id=1, source_target_pairs={{0,1},{1,0},{2,3},{3,2},{4,5},{5,4},{6,7},{7,6},{8,9},{9,8},{10,11... | collective-permute-start | bytes 6291464 | tf_op jit(solution)/shard_map/ppermute | solution.py:96
  383.5 66.2 %collective-permute-start.57 = (bf16[640,2048]{1,0:T(8,128)(2,1)}, bf16[640,2048]{1,0:T(8,128)(2,1)}, u32[]{:S(2)}, u32[]{:S(2)}) collective-permute-start(bf16[640,2048]{1,0:T(8,128)(2,1)} %pad_maximum_fusion.16), channel_id=1, source_target_pairs={{0,1},{1,0},{2,3},{3,2},{4,5},{5,4},{6,7},{7,6},{8,9},{9,8},{10,11... | collective-permute-start | bytes 7864328 | tf_op jit(solution)/shard_map/ppermute | solution.py:96
  410.2 65.1 %collective-permute-start.30 = (bf16[1408,1024]{1,0:T(8,128)(2,1)}, bf16[1408,1024]{1,0:T(8,128)(2,1)S(1)}, u32[]{:S(2)}, u32[]{:S(2)}) collective-permute-start(bf16[1408,1024]{1,0:T(8,128)(2,1)} %pad_maximum_fusion.12), channel_id=1, source_target_pairs={{0,4},{1,5},{2,6},{3,7},{4,0},{5,1},{6,2},{7,3},{8,12},{9,13},{10,... | collective-permute-start | bytes 8650760 | tf_op jit(solution)/shard_map/ppermute | solution.py:96
  424.2 75.7 %collective-permute-start.16 = (bf16[4,2,2,64,2048]{4,3,2,1,0:T(8,128)(2,1)}, bf16[4,2,2,64,2048]{4,3,2,1,0:T(8,128)(2,1)}, u32[]{:S(2)}, u32[]{:S(2)}) collective-permute-start(bf16[4,2,2,64,2048]{4,3,2,1,0:T(8,128)(2,1)} %maximum_select_fusion.3), channel_id=1, source_target_pairs={{0,1},{1,0},{2,3},{3,2},{4,5},{5,4},{6,7},{7,6},{8,9},{9,8},{10,11... | collective-permute-start | bytes 12582920 | tf_op jit(solution)/shard_map/ppermute | solution.py:96
  648.8 97.6 %collective-permute-start.37 = (bf16[640,2048]{1,0:T(8,128)(2,1)}, bf16[640,2048]{1,0:T(8,128)(2,1)}, u32[]{:S(2)}, u32[]{:S(2)}) collective-permute-start(bf16[640,2048]{1,0:T(8,128)(2,1)} %convolution_convert_fusion.7), channel_id=1, source_target_pairs={{0,1},{1,0},{2,3},{3,2},{4,5},{5,4},{6,7},{7,6},{8,9},{9,8},{10,11... | collective-permute-start | bytes 7864328 | tf_op jit(solution)/shard_map/ppermute | solution.py:96
  660.6 92.3 %collective-permute-start.58 = (bf16[640,2048]{1,0:T(8,128)(2,1)}, bf16[640,2048]{1,0:T(8,128)(2,1)}, u32[]{:S(2)}, u32[]{:S(2)}) collective-permute-start(bf16[640,2048]{1,0:T(8,128)(2,1)} %add_convert_fusion.4), channel_id=1, source_target_pairs={{0,1},{1,0},{2,3},{3,2},{4,5},{5,4},{6,7},{7,6},{8,9},{9,8},{10,11... | collective-permute-start | bytes 7864328 | tf_op jit(solution)/shard_map/ppermute | solution.py:96
  676.7 81.3 %collective-permute-start.43 = (bf16[640,2048]{1,0:T(8,128)(2,1)}, bf16[640,2048]{1,0:T(8,128)(2,1)}, u32[]{:S(2)}, u32[]{:S(2)}) collective-permute-start(bf16[640,2048]{1,0:T(8,128)(2,1)} %convolution_convert_fusion.5), channel_id=1, source_target_pairs={{0,1},{1,0},{2,3},{3,2},{4,5},{5,4},{6,7},{7,6},{8,9},{9,8},{10,11... | collective-permute-start | bytes 7864328 | tf_op jit(solution)/shard_map/ppermute | solution.py:96
  728.3 191.8 %collective-permute-start.98 = (bf16[4,256,1024]{2,1,0:T(8,128)(2,1)}, bf16[4,256,1024]{2,1,0:T(8,128)(2,1)}, u32[]{:S(2)}, u32[]{:S(2)}) collective-permute-start(bf16[4,256,1024]{2,1,0:T(8,128)(2,1)} %dynamic-slice_bitcast_fusion.2), channel_id=1, source_target_pairs={{0,4},{1,5},{2,6},{3,7},{4,0},{5,1},{6,2},{7,3},{8,12},{9,13},{10,... | collective-permute-start | bytes 6291464 | tf_op jit(solution)/shard_map/ppermute | solution.py:96
  762.9 77.2 %collective-permute-start.44 = (bf16[320,2048]{1,0:T(8,128)(2,1)S(1)}, bf16[320,2048]{1,0:T(8,128)(2,1)S(1)}, u32[]{:S(2)}, u32[]{:S(2)}) collective-permute-start(bf16[320,2048]{1,0:T(8,128)(2,1)S(1)} %slice.849), channel_id=1, source_target_pairs={{0,2},{1,3},{2,0},{3,1},{4,6},{5,7},{6,4},{7,5},{8,10},{9,11},{10,... | collective-permute-start | bytes 3932168 | tf_op jit(solution)/shard_map/ppermute | solution.py:96
  765.6 101.7 %collective-permute-start.65 = (bf16[320,2048]{1,0:T(8,128)(2,1)S(1)}, bf16[320,2048]{1,0:T(8,128)(2,1)S(1)}, u32[]{:S(2)}, u32[]{:S(2)}) collective-permute-start(bf16[320,2048]{1,0:T(8,128)(2,1)S(1)} %slice.909), channel_id=1, source_target_pairs={{0,2},{1,3},{2,0},{3,1},{4,6},{5,7},{6,4},{7,5},{8,10},{9,11},{10,... | collective-permute-start | bytes 3932168 | tf_op jit(solution)/shard_map/ppermute | solution.py:96
  841.8 67.5 %collective-permute-start.45 = (bf16[160,2048]{1,0:T(8,128)(2,1)}, bf16[160,2048]{1,0:T(8,128)(2,1)}, u32[]{:S(2)}, u32[]{:S(2)}) collective-permute-start(bf16[160,2048]{1,0:T(8,128)(2,1)} %get-tuple-element.336), channel_id=1, source_target_pairs={{0,8},{1,9},{2,10},{3,11},{4,12},{5,13},{6,14},{7,15}} | collective-permute-start | bytes 1966088 | tf_op jit(solution)/shard_map/ppermute | solution.py:96
  909.3 188.7 %reduce-scatter.8.cloned.1.call-start = ((), (), s32[]{:S(2)}) async-start(), calls=%async_computation.7 | async-start | bytes 2228224 | tf_op jit(solution)/shard_map/reduce_scatter | solution.py:427
  1007.3 148.1 %reduce-scatter.6.cloned.1.call-start = ((), (), s32[]{:S(2)}) async-start(), calls=%async_computation.5 | async-start | bytes 2228224 | tf_op jit(solution)/shard_map/reduce_scatter | solution.py:427
  1043.5 512.6 %reduce-scatter.10.cloned.1.call-start = ((), (), s32[]{:S(2)}) async-start(), calls=%async_computation.8 | async-start | bytes 12976128
  1090.5 144.7 %collective-permute-start.102 = (bf16[1408,256]{1,0:T(8,128)(2,1)}, bf16[1408,256]{1,0:T(8,128)(2,1)}, u32[]{:S(2)}, u32[]{:S(2)}) collective-permute-start(bf16[1408,256]{1,0:T(8,128)(2,1)} %get-tuple-element.208), channel_id=1, source_target_pairs={{0,24},{1,25},{2,26},{3,27},{4,28},{5,29},{6,30},{7,31},{8,16},{9,... | collective-permute-start | bytes 2162696 | tf_op jit(solution)/shard_map/ppermute | solution.py:96
  1095.2 141.9 %collective-permute-start.101 = (bf16[1408,256]{1,0:T(8,128)(2,1)}, bf16[1408,256]{1,0:T(8,128)(2,1)}, u32[]{:S(2)}, u32[]{:S(2)}) collective-permute-start(bf16[1408,256]{1,0:T(8,128)(2,1)} %get-tuple-element.274), channel_id=1, source_target_pairs={{0,16},{1,17},{2,18},{3,19},{4,20},{5,21},{6,22},{7,23},{8,24},{9,... | collective-permute-start | bytes 2162696 | tf_op jit(solution)/shard_map/ppermute | solution.py:96
  1098.0 139.1 %collective-permute-start.100 = (bf16[1408,256]{1,0:T(8,128)(2,1)}, bf16[1408,256]{1,0:T(8,128)(2,1)}, u32[]{:S(2)}, u32[]{:S(2)}) collective-permute-start(bf16[1408,256]{1,0:T(8,128)(2,1)} %get-tuple-element.275), channel_id=1, source_target_pairs={{0,8},{1,9},{2,10},{3,11},{4,12},{5,13},{6,14},{7,15},{8,0},{9,1},... | collective-permute-start | bytes 2162696 | tf_op jit(solution)/shard_map/ppermute | solution.py:96
  1189.3 208.3 %collective-permute-start.92 = (bf16[4,2,2,32,3200]{4,3,2,1,0:T(8,128)(2,1)}, bf16[4,2,2,32,3200]{4,3,2,1,0:T(8,128)(2,1)}, u32[]{:S(2)}, u32[]{:S(2)}) collective-permute-start(bf16[4,2,2,32,3200]{4,3,2,1,0:T(8,128)(2,1)} %dynamic-slice_bitcast_fusion), channel_id=1, source_target_pairs={{0,1},{1,0},{2,3},{3,2},{4,5},{5,4},{6,7},{7,6},{8,9},{9,8},{10,11... | collective-permute-start | bytes 9830408 | tf_op jit(solution)/shard_map/ppermute | solution.py:96
  1233.6 155.1 %collective-permute-start.86 = (bf16[4,2,2,32,2560]{4,3,0,2,1:T(8,128)(2,1)}, bf16[4,2,2,32,2560]{4,3,0,2,1:T(8,128)(2,1)}, u32[]{:S(2)}, u32[]{:S(2)}) collective-permute-start(bf16[4,2,2,32,2560]{4,3,0,2,1:T(8,128)(2,1)} %bitcast.618), channel_id=1, source_target_pairs={{0,1},{1,0},{2,3},{3,2},{4,5},{5,4},{6,7},{7,6},{8,9},{9,8},{10,11... | collective-permute-start | bytes 7864328 | tf_op jit(solution)/shard_map/ppermute | solution.py:96
  1281.3 112.8 %collective-permute-start.74 = (bf16[4,2,2,64,1280]{4,3,0,2,1:T(8,128)(2,1)S(1)}, bf16[4,2,2,64,1280]{4,3,0,2,1:T(8,128)(2,1)}, u32[]{:S(2)}, u32[]{:S(2)}) collective-permute-start(bf16[4,2,2,64,1280]{4,3,0,2,1:T(8,128)(2,1)S(1)} %bitcast.619), channel_id=1, source_target_pairs={{0,1},{1,0},{2,3},{3,2},{4,5},{5,4},{6,7},{7,6},{8,9},{9,8},{10,11... | collective-permute-start | bytes 7864328 | tf_op jit(solution)/shard_map/ppermute | solution.py:96
  1290.2 80.9 %collective-permute-start.108 = (bf16[256,1024]{1,0:T(8,128)(2,1)S(1)}, bf16[256,1024]{1,0:T(8,128)(2,1)S(1)}, u32[]{:S(2)}, u32[]{:S(2)}) collective-permute-start(bf16[256,1024]{1,0:T(8,128)(2,1)S(1)} %get-tuple-element.283), channel_id=1, source_target_pairs={{0,16},{1,17},{2,18},{3,19},{4,20},{5,21},{6,22},{7,23},{8,24},{9,... | collective-permute-start | bytes 1572872 | tf_op jit(solution)/shard_map/ppermute | solution.py:96
  1317.0 68.9 %collective-permute-start.107 = (bf16[256,1024]{1,0:T(8,128)(2,1)S(1)}, bf16[256,1024]{1,0:T(8,128)(2,1)S(1)}, u32[]{:S(2)}, u32[]{:S(2)}) collective-permute-start(bf16[256,1024]{1,0:T(8,128)(2,1)S(1)} %get-tuple-element.284), channel_id=1, source_target_pairs={{0,8},{1,9},{2,10},{3,11},{4,12},{5,13},{6,14},{7,15},{8,0},{9,1},... | collective-permute-start | bytes 1572872 | tf_op jit(solution)/shard_map/ppermute | solution.py:96
  1400.6 88.4 %collective-permute-start.93 = (bf16[4,2,32,3200]{3,2,1,0:T(8,128)(2,1)S(1)}, bf16[4,2,32,3200]{3,2,1,0:T(8,128)(2,1)S(1)}, u32[]{:S(2)}, u32[]{:S(2)}) collective-permute-start(bf16[4,2,32,3200]{3,2,1,0:T(8,128)(2,1)S(1)} %dynamic-slice_bitcast_fusion.3), channel_id=1, source_target_pairs={{0,2},{1,3},{2,0},{3,1},{4,6},{5,7},{6,4},{7,5},{8,10},{9,11},{10,... | collective-permute-start | bytes 4915208 | tf_op jit(solution)/shard_map/ppermute | solution.py:96
  (279 other events, 5805.4 us)
Sparse Core Ops, SparseCore 0:
  10.8 71.4 all-gather.7
  85.3 167.4 all-gather.3
  909.4 45.3 all-gather.5
  1007.4 62.9 reduce-scatter.7
  1075.0 80.3 reduce-scatter.5
  1231.8 193.5 reduce-scatter.9

commit v2 on v1

v2 whole, which is shorter than its diff:
```python
import math

import jax
import jax.numpy as jnp
from jax import lax
from jax.experimental import pallas as pl
from jax.experimental.pallas import tpu as pltpu
from jax.sharding import PartitionSpec as P

DS = 1024
HEADS = 8
HD = 256
CAMS = 3
PATCH = 192
NTIME = 1000
AXES = ("dp", "ctx")

masked_score = -1e30
F32 = jnp.float32
BF16 = jnp.bfloat16


def rms_norm(values, norm_gain):
    return values * lax.rsqrt(jnp.mean(values * values, axis=-1, keepdims=True) + 1e-06) * norm_gain


def norm_back(values, norm_gain, cotangent):
    _, pullback = jax.vjp(rms_norm, values, norm_gain)
    return pullback(cotangent)


def time_embed(sample_index):
    flow_time = (sample_index.astype(F32) + 0.5) / NTIME
    halves = DS // 2
    fraction = jnp.arange(halves, dtype=F32) / (halves - 1)
    period = 0.004 * jnp.power(1000.0, fraction)
    angles = 2.0 * math.pi * flow_time[..., None] / period
    return jnp.concatenate([jnp.sin(angles), jnp.cos(angles)], axis=-1)


def mm(left, right):
    return jnp.dot(left, right, preferred_element_type=F32)


def mm_tr(left, right):
    return lax.dot_general(left, right, (((1,), (1,)), ((), ())), preferred_element_type=F32)


def outer_sum(left, right):
    return lax.dot_general(left, right, (((0,), (0,)), ((), ())), preferred_element_type=F32)


def ein(spec, left, right):
    return jnp.einsum(spec, left, right, preferred_element_type=F32)


def add_low(left, right):
    return (left.astype(F32) + right.astype(F32)).astype(BF16)


def sync(*arrays):
    return lax.optimization_barrier(arrays)


def together(groups):
    flat = sync(*[array for group in groups for array in group])
    out, at = [], 0
    for group in groups:
        out.append(list(flat[at : at + len(group)]))
        at += len(group)
    return out


def pad_rows(array, rows):
    return jnp.pad(array, ((0, rows - array.shape[0]), (0, 0)))


def gated_unit(gate_value, up_value):
    return jax.nn.gelu(gate_value, approximate=True) * up_value


VMEM_BYTES = 40 * 2**20


def outer_kernel(count, *refs):
    left, right, out_ref = refs[:count], refs[count : 2 * count], refs[2 * count]
    total = None
    for one, other in zip(left, right, strict=True):
        part = lax.dot_general(one[...], other[...], (((0,), (0,)), ((), ())), preferred_element_type=F32)
        total = part if total is None else total + part
    out_ref[...] = total.astype(BF16)


def outer_sums(lefts, rights, tile=256):
    count, rows = len(lefts), lefts[0].shape[0]
    height, width = lefts[0].shape[1], rights[0].shape[1]
    return pl.pallas_call(
        lambda *refs: outer_kernel(count, *refs),
        grid=(height // tile,),
        in_specs=[pl.BlockSpec((rows, tile), lambda i: (0, i))] * count
        + [pl.BlockSpec((rows, width), lambda i: (0, 0))] * count,
        out_specs=pl.BlockSpec((tile, width), lambda i: (i, 0)),
        out_shape=jax.ShapeDtypeStruct((height, width), BF16),
        compiler_params=pltpu.CompilerParams(vmem_limit_bytes=VMEM_BYTES),
        cost_estimate=pl.CostEstimate(
            flops=2 * count * rows * height * width,
            bytes_accessed=2 * count * rows * (height + width) + 2 * height * width,
            transcendentals=0,
        ),
    )(*lefts, *rights)


def make_body(n, q):
    m = 4 if n >= 8 else n // 2
    high = n // (2 * m)

    def flat(dp, ctx):
        return dp * q + ctx

    def xor_pairs(dp_mask, ctx_mask):
        return [(flat(d, c), flat(d ^ dp_mask, c ^ ctx_mask)) for d in range(n) for c in range(q)]

    swap_c = xor_pairs(0, 1)
    swap_y = xor_pairs(0, 2)
    swap_x = xor_pairs(1, 0)
    swap_high = [xor_pairs(2 * m * 2**i, 0) for i in range(high.bit_length() - 1)]

    lines_z = [
        [flat((h * m + z) * 2 + x, c) for z in range(m)] for h in range(high) for x in range(2) for c in range(q)
    ]

    def send(array, pairs):
        return lax.ppermute(array, AXES, pairs)

    def z_swap(parts):
        return lax.all_to_all(parts, AXES, 0, 0, axis_index_groups=lines_z)

    def z_gather(own):
        return z_swap(jnp.broadcast_to(own[None], (m,) + own.shape))

    def in_order(bit, mine, other, axis):
        return jnp.where(bit == 0, jnp.stack([mine, other], axis), jnp.stack([other, mine], axis))

    def with_highs(lines, place):
        lines = lines[None]
        for bit, pairs in zip(place[4], swap_high, strict=True):
            lines = in_order(bit, lines, send(lines, pairs), 0)
            lines = lines.reshape((-1,) + lines.shape[2:])
        return lines.reshape((-1,) + lines.shape[2:])

    def down_piece(down_pre, gate_act, up_act, down_act):
        cols = down_pre.shape[0] // m
        cols_act = gate_act.shape[1] // m

        def piece_of(t):
            last = cut(down_act, t, cols_act, 0)
            return jnp.concatenate(
                [
                    cut(down_pre, t, cols, 0),
                    narrowed(cut(gate_act, t, cols_act, 1)),
                    narrowed(cut(up_act, t, cols_act, 1)),
                    jnp.concatenate([last[: cols_act // 2], last[cols_act // 2 :]], axis=1),
                ],
                axis=0,
            )

        return piece_of

    def columns_full(near, far, place):
        x, highs = place[1], place[4]
        blocks = []
        for t in range(m):
            blocks += [jnp.where(x == 0, near[t], far[t]), jnp.where(x == 0, far[t], near[t])]
        full = jnp.concatenate(blocks, axis=1)
        for bit, pairs in zip(highs, swap_high, strict=True):
            other = send(full, pairs)
            full = jnp.concatenate(
                [jnp.where(bit == 0, full, other), jnp.where(bit == 0, other, full)], axis=1
            )
        return full

    def rows_full(near, far, place):
        x, highs = place[1], place[4]
        _, w, cols = near.shape
        full = in_order(x, near, far, 1).reshape(1, 2 * m * w, cols)
        for bit, pairs in zip(highs, swap_high, strict=True):
            full = in_order(bit, full, send(full, pairs), 0).reshape(1, -1, cols)
        return full.reshape(n * w, cols)

    def act_weights(down_full, cols, cols_act, w_act):
        w = 2 * w_act
        flat_act = high * w_act

        def rows_act(start):
            part = down_full[start : start + flat_act]
            return jnp.concatenate([widened(part[:, d * w : (d + 1) * w]) for d in range(n)])

        wide_act = (rows_act(cols), rows_act(cols + flat_act))
        last = down_full[cols + 2 * flat_act :]
        narrow_act = jnp.concatenate(
            [
                jnp.concatenate([last[:, d * w : d * w + w_act], last[:, d * w + w_act : (d + 1) * w]])
                for d in range(n)
            ],
            axis=1,
        )
        return wide_act, narrow_act

    def split_bit(array, bit, axis):
        mine = lax.dynamic_index_in_dim(array, bit, axis, keepdims=False)
        return mine, lax.dynamic_index_in_dim(array, 1 - bit, axis, keepdims=False)

    def split_columns(total, place):
        x, highs = place[1], place[4]
        w = total.shape[1] // n
        for bit, pairs in zip(reversed(highs), reversed(swap_high), strict=True):
            half = total.shape[1] // 2
            theirs = jnp.where(bit == 0, total[:, half:], total[:, :half])
            mine = jnp.where(bit == 0, total[:, :half], total[:, half:])
            total = add_low(mine, send(theirs, pairs))
        blocks = [total[:, d * w : (d + 1) * w] for d in range(2 * m)]
        theirs = [jnp.where(x == 0, blocks[2 * t + 1], blocks[2 * t]) for t in range(m)]
        mine = [jnp.where(x == 0, blocks[2 * t], blocks[2 * t + 1]) for t in range(m)]
        return jnp.stack(mine), jnp.stack(theirs)

    def split_rows(total, place):
        x, highs = place[1], place[4]
        w = total.shape[0] // n
        total = total.reshape(n, w, total.shape[1])
        for bit, pairs in zip(reversed(highs), reversed(swap_high), strict=True):
            mine, theirs = split_bit(total.reshape((2, -1) + total.shape[1:]), bit, 0)
            total = add_low(mine, send(theirs, pairs))
        return split_bit(total.reshape(m, 2, w, total.shape[2]), x, 1)

    def light_core(part, place):
        rows = part.shape[0] // (n * q)
        return split_bit(part.reshape(high * m, 2, 2, 2, rows, part.shape[1]), place[3], 3)

    def light_highs(part, place):
        highs = place[4]
        for bit, pairs in zip(reversed(highs), reversed(swap_high), strict=True):
            mine, theirs = split_bit(part.reshape((2, -1) + part.shape[1:]), bit, 0)
            part = add_low(mine, send(theirs, pairs))
        return part

    def add_all(pieces):
        total = pieces[0].astype(F32)
        for k in range(1, m):
            total = total + pieces[k].astype(F32)
        return total

    def pairs_of(mine, other):
        return jnp.concatenate([mine, other]).reshape(-1, mine.shape[-1])

    def core_order(rows):
        old, new = jnp.arange(HD)[:, None], jnp.arange(HD)[None, :]
        half = HD // 2
        same = (old // (2 * rows) == (new % half) // rows) & (old // rows % 2 == new // half)
        return (same & (old % rows == new % rows)).astype(BF16)

    def core_parts(blocks):
        half = blocks.shape[-1] // 2
        return [blocks[..., at : at + half].reshape(blocks.shape[0], -1) for at in (0, half)]

    def by_core(c, mine, other):
        width = mine.shape[-1]
        return [
            jnp.where(c == 0, mine, other).reshape(-1, width),
            jnp.where(c == 0, other, mine).reshape(-1, width),
        ]

    def narrowed(array):
        size = array.shape[-1] // high
        return jnp.concatenate([array[..., i * size : (i + 1) * size] for i in range(high)], axis=-2)

    def widened(array):
        size = array.shape[-2] // high
        return jnp.concatenate([array[..., i * size : (i + 1) * size, :] for i in range(high)], axis=-1)

    def cut(array, index, size, axis):
        return lax.dynamic_slice_in_dim(array, index * size, size, axis)

    def ffn_unit(gate_value, rows, up_weight, narrow):
        up_value = mm(rows, up_weight)
        hidden = gated_unit(gate_value, up_value).astype(BF16)
        return gate_value, up_value, hidden, mm(hidden, narrow).astype(BF16)

    def ffn_back(d_hidden, gate_value, up_value, wide):
        _, pullback = jax.vjp(gated_unit, gate_value, up_value)
        d_gate, d_up = pullback(d_hidden)
        d_gate, d_up = d_gate.astype(BF16), d_up.astype(BF16)
        d_rows = (mm_tr(d_gate, wide[0]) + mm_tr(d_up, wide[1])).astype(BF16)
        return d_rows, d_gate, d_up

    def per_device(
        prefix_tokens,
        actions,
        robot_state,
        text_len,
        flow_index,
        query_pre,
        key_pre,
        value_pre,
        out_pre,
        gain_attn_pre,
        gain_ffn_pre,
        query_act,
        key_act,
        value_act,
        out_act,
        gain_attn_act,
        gain_ffn_act,
        action_in,
        mix_first,
        mix_second,
        state_in,
        gate_pre,
        up_pre,
        down_pre,
        gate_act,
        up_act,
        down_act,
        grad_pre,
        grad_act,
    ):
        dp = lax.axis_index("dp")
        ctx = lax.axis_index("ctx")
        z, x = (dp // 2) % m, dp % 2
        y, c = ctx // 2, ctx % 2
        highs = [(dp // (2 * m * 2**i)) % 2 for i in range(len(swap_high))]
        place = (z, x, y, c, highs)
        width = prefix_tokens.shape[2]
        tokens = prefix_tokens.shape[1]
        rows_pre = -(-tokens // 32) * 32
        suffix = grad_act.shape[2]
        rows_act = -(-suffix // 32) * 32
        acts = actions.shape[2]
        devices = n * q
        r64, r32 = query_pre.shape[0], query_act.shape[0]

        cols = gate_pre.shape[1] // m
        cols_act = gate_act.shape[1] // m
        w = gate_pre.shape[0]
        w_act = gate_act.shape[0]
        flat_act = high * w_act
        half = width // 2 + HD
        at = width + 2 * HD
        scale = HD ** (-0.5)

        pad = jnp.zeros((r64 - r32,), BF16)
        gains = jnp.stack(
            [
                gain_attn_pre,
                gain_ffn_pre,
                jnp.concatenate([gain_attn_act, pad]),
                jnp.concatenate([gain_ffn_act, pad]),
            ],
            axis=1,
        )
        gains = jnp.pad(gains, ((0, 0), (0, 124)))
        first = jnp.concatenate([query_pre, key_pre, value_pre, gains], axis=1)
        small = jnp.pad(jnp.concatenate([action_in, state_in], axis=1), ((0, 0), (0, 64)))
        third = jnp.concatenate(
            [query_act, key_act, value_act, mix_second, small], axis=1
        )
        second = jnp.concatenate([out_pre, out_act, mix_first], axis=1)
        third_half = third.shape[1] // 256 * 128
        sharing = [
            [flat((h * m + a) * 2 + b, d) for a in range(m) for d in range(q)]
            for h in range(high)
            for b in range(2)
        ]

        def gather_act(block):
            return lax.all_gather(block, AXES, axis=0, tiled=True, axis_index_groups=sharing)

        def scatter_act(block):
            return lax.psum_scatter(
                block, AXES, scatter_dimension=0, tiled=True, axis_index_groups=sharing
            ).astype(F32)

        prefix_in = pad_rows(prefix_tokens[0], rows_pre).astype(F32)
        cot_own = pad_rows(grad_pre[0], rows_pre)
        piece_of = down_piece(down_pre, gate_act, up_act, down_act)
        down_own = jnp.stack([piece_of(t) for t in range(m)])
        gate_own = jnp.stack([gate_pre[:, t * cols : (t + 1) * cols] for t in range(m)])
        up_own = jnp.stack([up_pre[:, t * cols : (t + 1) * cols] for t in range(m)])

        first_z = z_gather(first)
        first_z, second = sync(first_z, second)
        first_z = with_highs(first_z, place)
        one_a, one_b = first_z[:, :, :half], first_z[:, :, half:]
        got_a, got_b = send(one_a, swap_y), send(one_b, swap_x)
        second_z = z_gather(second)
        got_a, got_b, third, cot_act_own = sync(got_a, got_b, third, pad_rows(grad_act[0, 0], rows_act))
        cot_all_act = gather_act(cot_act_own)
        one_a, one_b = in_order(y, one_a, got_a, 1), in_order(x, one_b, got_b, 1)
        got_a, got_b = send(one_a, swap_x), send(one_b, swap_y)
        got_a, got_b, third, second_z = sync(got_a, got_b, third, second_z)
        one_a, one_b = in_order(x, one_a, got_a, 1), in_order(y, one_b, got_b, 2)
        got_a, got_b = send(one_a, swap_c), send(one_b, swap_c)
        third_z = z_gather(third)
        second_z = with_highs(second_z, place)
        two_a, two_b = second_z[:, :, :width], second_z[:, :, width:]
        side_a, side_b = send(two_a, swap_y), send(two_b, swap_x)
        got_a, got_b, down_own = sync(got_a, got_b, down_own)
        first_a = in_order(c, one_a, got_a, 3).reshape(-1, half)
        first_b = in_order(c, one_b, got_b, 3).reshape(-1, half + 128)
        first_b, gain_cols = first_b[:, :half], first_b[:, half:]
        gain_rows = gain_cols.astype(F32)
        norm_attn, norm_ffn = gain_rows[:, 0], gain_rows[:, 1]
        gain_small = gain_rows[:, 2:4].reshape(devices, r64, 2)[:, :r32].reshape(devices * r32, 2)
        norm_attn_act, norm_ffn_act = gain_small[:, 0], gain_small[:, 1]
        normed_pre = rms_norm(prefix_in, norm_attn).astype(BF16)
        qkv_pre = jnp.concatenate(
            [mm(normed_pre, first_a).astype(BF16), mm(normed_pre, first_b).astype(BF16)], axis=1
        )
        ordered = core_order(r64)
        kv_own = jnp.concatenate(
            [qkv_pre[:, width : width + HD], mm(qkv_pre[:, width + HD :], ordered).astype(BF16)], axis=1
        )
        kv_own, side_a, side_b, third_z, down_own = sync(kv_own, side_a, side_b, third_z, down_own)
        down_z = z_swap(down_own)
        two_a, two_b = in_order(y, two_a, side_a, 1), in_order(x, two_b, side_b, 1)
        side_a, side_b = send(two_a, swap_x), send(two_b, swap_y)
        kv_y = send(kv_own, swap_y)
        kv_c = send(jnp.stack([kv_own, kv_y]), swap_c)
        (kv_c,) = sync(kv_c)
        queries_pre = qkv_pre[:, :width].reshape(rows_pre, HEADS, HD)
        both_kv = jnp.concatenate([kv_own[None], kv_y[None], kv_c]).reshape(q * rows_pre, 2 * HD)
        keys, values = both_kv[:, :HD], both_kv[:, HD:]
        key_count = q * rows_pre
        order = jnp.array([0, 2, 1, 3])
        spot = jnp.arange(rows_pre)
        positions = (ctx ^ order)[:, None] * tokens + spot[None, :]
        camera_rows = CAMS * PATCH
        key_valid = (positions < camera_rows) | (positions - camera_rows < text_len[0])
        key_valid = (key_valid & (spot < tokens)[None, :]).reshape(-1)

        def prefix_scores():
            scores = ein("qhd,kd->hqk", queries_pre, keys) * scale
            return jnp.where(key_valid[None, None, :], scores, masked_score)

        def soft_rows(scores):
            highest = jnp.max(scores, axis=-1, keepdims=True)
            totals = jnp.sum(jnp.exp(scores - highest), axis=-1, keepdims=True)
            log_total = highest + jnp.log(totals)
            return jnp.exp(scores - log_total), log_total

        probs_pre, total_pre = soft_rows(prefix_scores())
        probs_pre = probs_pre.astype(BF16)
        probs_pre, side_a, side_b, cot_all_act = sync(probs_pre, side_a, side_b, cot_all_act)
        two_a, two_b = in_order(x, two_a, side_a, 1), in_order(y, two_b, side_b, 2)
        side_a, side_b = send(two_a, swap_c), send(two_b, swap_c)
        attn_pre = ein("hqk,kd->qhd", probs_pre, values)
        attn_pre = attn_pre.astype(BF16)
        attn_pre, side_a, side_b, down_z, gate_own = sync(attn_pre, side_a, side_b, down_z, gate_own)
        gate_z = z_swap(gate_own)
        two = m // 2
        down_z_a, down_z_b = down_z[:two], down_z[two:]
        down_far_a = send(down_z_a, swap_x)
        out_parts = by_core(c, two_a, side_a)
        others = by_core(c, two_b, side_b)
        out_act_parts = [part[:, :DS] for part in others]
        mixer_parts = [part[:, DS:] for part in others]
        attn_parts = core_parts(attn_pre)
        mid_pre = prefix_in + mm(attn_parts[0], out_parts[0]) + mm(attn_parts[1], out_parts[1])
        normed_two_pre = rms_norm(mid_pre, norm_ffn).astype(BF16)
        normed_two_pre, cot_own, third_z, gate_z, up_own, down_far_a, down_z_b = sync(
            normed_two_pre, cot_own, third_z, gate_z, up_own, down_far_a, down_z_b
        )
        up_z = z_swap(up_own)
        down_far_b = send(down_z_b, swap_x)
        gate_far = send(gate_z, swap_x)
        third_z = with_highs(third_z, place)
        three_a, three_b = third_z[:, :, :third_half], third_z[:, :, third_half:]
        third_a, third_b = send(three_a, swap_y), send(three_b, swap_x)
        up_z, down_far_b, third_a, third_b = sync(up_z, down_far_b, third_a, third_b)
        row_z = z_gather(normed_two_pre)
        three_a, three_b = in_order(y, three_a, third_a, 1), in_order(x, three_b, third_b, 1)
        third_a, third_b = send(three_a, swap_x), send(three_b, swap_y)
        down_full = columns_full(down_z, jnp.concatenate([down_far_a, down_far_b]), place)
        third_a, third_b, gate_far, up_z = sync(third_a, third_b, gate_far, up_z)
        up_far = send(up_z, swap_x)
        gate_full = rows_full(gate_z, gate_far, place)
        three_a, three_b = in_order(x, three_a, third_a, 1), in_order(y, three_b, third_b, 2)
        third_a, third_b = send(three_a, swap_c), send(three_b, swap_c)
        third = jnp.concatenate(
            [
                in_order(c, three_a, third_a, 3).reshape(devices * r32, -1),
                in_order(c, three_b, third_b, 3).reshape(devices * r32, -1),
            ],
            axis=1,
        )
        qkv_act_w = third[:, :at]
        mixer_second = third[:, at : at + DS]
        action_full = third[:, at + DS : at + DS + 32]
        state_full = third[:, at + DS + 32 : at + DS + 64]
        time_rows = time_embed(flow_index[0, 0])
        action_emb = mm_tr(actions[0, 0], action_full)
        mix_input = jnp.concatenate(
            [action_emb, jnp.broadcast_to(time_rows[None, :], action_emb.shape)], axis=-1
        ).astype(BF16)
        mix_parts = core_parts(ein("tbk,kj->tbj", mix_input.reshape(acts, -1, HD), ordered).astype(BF16))
        pre_mix = mm(mix_parts[0], mixer_parts[0]) + mm(mix_parts[1], mixer_parts[1])
        mixed_act = jax.nn.silu(pre_mix).astype(BF16)
        action_rows = mm(mixed_act, mixer_second)
        state_row = mm_tr(robot_state, state_full)
        side_input = pad_rows(jnp.concatenate([state_row, action_rows], axis=0), rows_act)
        normed_act = rms_norm(side_input, norm_attn_act).astype(BF16)
        qkv_act = mm(normed_act, qkv_act_w).astype(BF16)
        row_z, qkv_act, gate_full, cot_own, down_full = sync(
            row_z, qkv_act, gate_full, cot_own, down_full
        )
        cot_z = z_gather(cot_own)
        row_got = send(row_z[:two], swap_y)
        narrow = down_full[:cols]
        wide_act, narrow_act = act_weights(down_full, cols, cols_act, w_act)
        queries_act = qkv_act[:, :width].reshape(rows_act, HEADS, HD)
        keys_act = qkv_act[:, width : width + HD]
        values_act = mm(qkv_act[:, width + HD :], ordered).astype(BF16)
        groups = jnp.arange(rows_act) > 0
        own_block = (groups[None, :] <= groups[:, None]) & (jnp.arange(rows_act) < suffix)[None, :]

        def side_scores():
            far = ein("qhd,kd->hqk", queries_act, keys) * scale
            far = jnp.where(key_valid[None, None, :], far, masked_score)
            near = ein("qhd,kd->hqk", queries_act, keys_act) * scale
            near = jnp.where(own_block[None], near, masked_score)
            return jnp.concatenate([far, near], axis=-1)

        probs_act, total_act = soft_rows(side_scores())
        probs_act_low = probs_act.astype(BF16)
        attn_act = ein("hqk,kd->qhd", probs_act_low[..., :key_count], values) + ein(
            "hqk,kd->qhd", probs_act_low[..., key_count:], values_act
        )
        attn_act_parts = core_parts(attn_act.astype(BF16))
        mid_act = (
            side_input + mm(attn_act_parts[0], out_act_parts[0]) + mm(attn_act_parts[1], out_act_parts[1])
        )
        normed_two_act = rms_norm(mid_act, norm_ffn_act).astype(BF16)
        row_got, normed_two_act, row_z_odd = sync(row_got, normed_two_act, row_z[two:])
        rows_all_act = gather_act(normed_two_act)
        near = pairs_of(row_z[:two], row_got)
        row_far = send(near, swap_c)
        row_got = send(row_z_odd, swap_y)
        up_full = rows_full(up_z, up_far, place)
        row_far, up_full = sync(row_far, up_full)
        row_e = jnp.concatenate([near, row_far])
        wide = (gate_full, up_full)
        unit_e = ffn_unit(mm(row_e, gate_full), row_e, up_full, narrow)
        row_got, part_e, cot_z = sync(row_got, unit_e[3], cot_z)
        near = pairs_of(row_z[two:], row_got)
        row_far = send(near, swap_c)
        cot_got = send(cot_z[:two], swap_y)
        cot_other_got = send(cot_z[two:], swap_y)
        (row_far,) = sync(row_far)
        row_o = jnp.concatenate([near, row_far])
        four_rows = 2 * two * rows_pre
        even_got = send(part_e[four_rows:], swap_c)
        unit_o = ffn_unit(mm(row_o, gate_full), row_o, up_full, narrow)
        even_got, cot_got, part_o = sync(even_got, cot_got, unit_o[3])
        near_e = pairs_of(cot_z[:two], cot_got)
        far_e = send(near_e, swap_c)
        cot_got = cot_other_got
        two_rows = 2 * rows_pre
        out_even = add_low(part_e[:four_rows], even_got)
        odd_got = send(part_o[four_rows:], swap_c)
        gate_act_value, up_act_value, hidden_act, part_act = ffn_unit(
            mm(rows_all_act, wide_act[0]), rows_all_act, wide_act[1], narrow_act
        )
        d_rows_act, d_gate_act, d_up_act = ffn_back(
            mm_tr(cot_all_act, narrow_act), gate_act_value, up_act_value, wide_act
        )
        grad_down_act = outer_sum(hidden_act, cot_all_act).astype(BF16)
        half_act = cols_act // 2

        def blocks_act(total):
            return jnp.concatenate(
                [narrowed(total[d * w_act : (d + 1) * w_act]) for d in range(n)], axis=1
            )

        narrow_parts = jnp.concatenate(
            [
                blocks_act(outer_sum(rows_all_act, d_gate_act).astype(BF16)),
                blocks_act(outer_sum(rows_all_act, d_up_act).astype(BF16)),
                jnp.concatenate(
                    [
                        grad_down_act[at_row : at_row + half_act, d * w_act : (d + 1) * w_act]
                        for d in range(n)
                        for at_row in (0, half_act)
                    ],
                    axis=1,
                ),
            ],
            axis=0,
        )
        small_mine, small_theirs = split_columns(narrow_parts, place)
        far_e, cot_got, odd_got, d_rows_act, part_act, small_theirs = sync(
            far_e, cot_got, odd_got, d_rows_act, part_act, small_theirs
        )
        d_branch_act = scatter_act(d_rows_act)
        small_got = send(small_theirs, swap_x)
        cot_e = jnp.concatenate([near_e, far_e])
        near_o = pairs_of(cot_z[two:], cot_got)
        far_o = send(near_o, swap_c)
        even_got = send(out_even[two_rows:], swap_y)
        d_hidden_e = mm_tr(cot_e, narrow)
        far_o, d_hidden_e = sync(far_o, d_hidden_e)
        cot_o = jnp.concatenate([near_o, far_o])
        grad_down = outer_sums([unit_e[2], unit_o[2]], [cot_e, cot_o])
        down_mine, down_theirs = split_columns(grad_down, place)
        d_hidden_o = mm_tr(cot_o, narrow)
        even_got, down_theirs, d_hidden_o, part_act = sync(even_got, down_theirs, d_hidden_o, part_act)
        branch_act = scatter_act(part_act)
        out_even = add_low(out_even[:two_rows], even_got)
        out_odd = add_low(part_o[:four_rows], odd_got)
        odd_got = send(out_odd[two_rows:], swap_y)
        down_got = send(down_theirs, swap_x)
        back_o = ffn_back(d_hidden_o, unit_o[0], unit_o[1], wide)
        odd_got, back_o_rows, small_got, down_got = sync(odd_got, back_o[0], small_got, down_got)
        out_odd = add_low(out_odd[:two_rows], odd_got)
        out_z = z_swap(jnp.concatenate([out_even, out_odd]).reshape(m, rows_pre, width))
        odd_got = send(back_o_rows[four_rows:], swap_c)
        back_e = ffn_back(d_hidden_e, unit_e[0], unit_e[1], wide)
        odd_got, back_e_rows = sync(odd_got, back_e[0])
        d_odd = add_low(back_o_rows[:four_rows], odd_got)
        odd_got = send(d_odd[two_rows:], swap_y)
        even_got = send(back_e_rows[four_rows:], swap_c)
        down_both = [add_low(down_mine, down_got), add_low(small_mine, small_got)]
        down_sums = jnp.concatenate(down_both, axis=1)
        grad_gate = outer_sums([row_e, row_o], [back_e[1], back_o[1]])
        odd_got, even_got, grad_gate, down_sums = sync(odd_got, even_got, grad_gate, down_sums)
        down_z = z_swap(down_sums)
        d_odd = add_low(d_odd[:two_rows], odd_got)
        d_even = add_low(back_e_rows[:four_rows], even_got)
        even_got = send(d_even[two_rows:], swap_y)
        gate_mine, gate_theirs = split_rows(grad_gate, place)
        gate_got = send(gate_theirs, swap_x)
        grad_up = outer_sums([row_e, row_o], [back_e[2], back_o[2]])
        even_got, grad_up, d_branch_act, branch_act = sync(even_got, grad_up, d_branch_act, branch_act)
        d_even = add_low(d_even[:two_rows], even_got)
        d_z = z_swap(jnp.concatenate([d_even, d_odd]).reshape(m, rows_pre, width))
        up_mine, up_theirs = split_rows(grad_up, place)
        up_got = send(up_theirs, swap_x)
        d_mid_act, grad_norm_ffn_act = norm_back(mid_act, norm_ffn_act, d_branch_act)
        d_mid_act = d_mid_act + pad_rows(grad_act[0, 0], rows_act).astype(F32)
        d_mid_act_low = d_mid_act.astype(BF16)
        grads_out_act = [outer_sum(part, d_mid_act_low).astype(BF16) for part in attn_act_parts]

        def heads_of(d_mid, parts):
            halves = [mm_tr(d_mid, part).astype(BF16).reshape(-1, HEADS, HD // 2) for part in parts]
            return jnp.concatenate(halves, axis=-1)

        d_attn_act = heads_of(d_mid_act_low, out_act_parts)
        probs_act = jnp.exp(side_scores() - total_act)
        probs_act_low = probs_act.astype(BF16)
        d_probs_act = jnp.concatenate(
            [ein("qhd,kd->hqk", d_attn_act, values), ein("qhd,kd->hqk", d_attn_act, values_act)], axis=-1
        )
        d_scores_act = probs_act * (
            d_probs_act - jnp.sum(probs_act * d_probs_act, axis=-1, keepdims=True)
        )
        d_scores_act = d_scores_act.astype(BF16)
        far, near = d_scores_act[..., :key_count], d_scores_act[..., key_count:]
        d_query_act = ein("hqk,kd->qhd", far, keys) + ein("hqk,kd->qhd", near, keys_act)
        d_query_act = (d_query_act * scale).reshape(rows_act, width).astype(BF16)
        d_keys_act = (ein("hqk,qhd->kd", near, queries_act) * scale).astype(BF16)
        d_values_act = ein("hqk,qhd->kd", probs_act_low[..., key_count:], d_attn_act).astype(BF16)
        d_values_act = mm_tr(d_values_act, ordered).astype(BF16)
        d_qkv_act = jnp.concatenate([d_query_act, d_keys_act, d_values_act], axis=1)
        d_normed_act = mm_tr(d_qkv_act, qkv_act_w)
        grad_qkv_act = outer_sum(normed_act, d_qkv_act).astype(BF16)
        d_side, grad_norm_attn_act = norm_back(side_input, norm_attn_act, d_normed_act)
        d_side = d_side + d_mid_act
        grad_state_in = outer_sum(d_side[:1].astype(BF16), robot_state)
        d_action_rows = d_side[1 : 1 + acts].astype(BF16)
        grad_mix_second = outer_sum(mixed_act, d_action_rows).astype(BF16)
        d_mixed = mm_tr(d_action_rows, mixer_second)
        _, silu_back = jax.vjp(jax.nn.silu, pre_mix)
        d_pre_mix = silu_back(d_mixed)[0].astype(BF16)
        grads_mix_first = [outer_sum(part, d_pre_mix).astype(BF16) for part in mix_parts]
        d_emb = [
            mm_tr(d_pre_mix, part[: DS // 2]).astype(BF16).reshape(acts, -1, HD // 2) for part in mixer_parts
        ]
        d_action_emb = ein("tbj,kj->tbk", jnp.concatenate(d_emb, axis=-1), ordered)
        d_action_emb = d_action_emb.astype(BF16).reshape(acts, DS)
        grad_action_in = outer_sum(d_action_emb, actions[0, 0])
        grad_actions = mm(d_action_emb, action_full)
        small_grads = jnp.pad(
            jnp.concatenate([grad_action_in, grad_state_in], axis=1).astype(BF16), ((0, 0), (0, 64))
        )
        three = jnp.concatenate([grad_qkv_act, grad_mix_second, small_grads], axis=1)
        mine_a, theirs_a = light_core(three[:, :third_half], place)
        mine_b, theirs_b = light_core(three[:, third_half:], place)

        def of_core(bit, pair):
            part = jnp.where(bit == 0, pair[0], pair[1])
            return part.reshape(high * m, 2, 2, r64, part.shape[1])

        twos = [grads_out_act, grads_mix_first]
        theirs_twos = [of_core(1 - c, pair) for pair in twos]
        (d_z, theirs_a, theirs_b, gate_got), theirs_twos, *twos = together(
            [[d_z, theirs_a, theirs_b, gate_got], theirs_twos] + twos
        )
        gate_z = z_swap(add_low(gate_mine, gate_got))
        got_a, got_b = send(theirs_a, swap_c), send(theirs_b, swap_c)
        two_got = [send(theirs, swap_c) for theirs in theirs_twos]
        d_branch = add_all(d_z)
        d_mid_pre, grad_norm_ffn = norm_back(mid_pre, norm_ffn, d_branch)
        d_mid_pre = d_mid_pre + cot_own.astype(F32)
        d_mid_low = d_mid_pre.astype(BF16)
        grads_out_pre = [outer_sum(part, d_mid_low).astype(BF16) for part in attn_parts]
        d_attn_pre = heads_of(d_mid_low, out_parts)
        theirs_out = of_core(1 - c, grads_out_pre)
        small_z = down_z[:, cols:]
        (d_attn_pre, up_got, got_a, got_b, theirs_out), two_got, grads_out_pre, *twos = together(
            [[d_attn_pre, up_got, got_a, got_b, theirs_out], two_got, grads_out_pre] + twos
        )
        out_got = send(theirs_out, swap_c)
        halves = [
            split_bit(add_low(of_core(c, pair), got), y, 2) for pair, got in zip(twos, two_got, strict=True)
        ]
        two_got = [send(part[1], swap_y) for part in halves]
        share_a, share_b = add_low(mine_a, got_a), add_low(mine_b, got_b)
        mine_a, theirs_a = split_bit(share_a, x, 1)
        mine_b, theirs_b = split_bit(share_b, y, 2)
        got_a, got_b = send(theirs_a, swap_x), send(theirs_b, swap_y)
        probs_pre = jnp.exp(prefix_scores() - total_pre)
        d_probs = ein("qhd,kd->hqk", d_attn_pre, values)
        d_probs, probs_pre, out_got, got_a, got_b = sync(d_probs, probs_pre, out_got, got_a, got_b)
        out_half = split_bit(add_low(of_core(c, grads_out_pre), out_got), x, 1)
        out_got = send(out_half[1], swap_x)
        d_scores = probs_pre * (d_probs - jnp.sum(probs_pre * d_probs, axis=-1, keepdims=True))
        d_scores = d_scores.astype(BF16)
        (d_scores,) = sync(d_scores)
        share_a, share_b = add_low(mine_a, got_a), add_low(mine_b, got_b)
        mine_a, theirs_a = split_bit(share_a, y, 1)
        mine_b, theirs_b = split_bit(share_b, x, 1)
        got_a, got_b = send(theirs_a, swap_y), send(theirs_b, swap_x)
        key_terms = ein("hqk,qhd->kd", d_scores, queries_pre) + ein("hqk,qhd->kd", far, queries_act)
        value_terms = ein("hqk,qhd->kd", probs_pre.astype(BF16), d_attn_pre)
        value_terms = value_terms + ein("hqk,qhd->kd", probs_act_low[..., :key_count], d_attn_act)
        kv_terms = jnp.concatenate([key_terms * scale, value_terms], axis=1).astype(BF16)
        kv_terms = kv_terms.reshape(q, rows_pre, 2 * HD)
        kv_got = send(kv_terms[2:], swap_c)
        d_query_pre = (ein("hqk,kd->qhd", d_scores, keys) * scale).reshape(rows_pre, width).astype(BF16)
        up_swapped = add_low(up_mine, up_got)
        (kv_got, d_query_pre, gate_z, up_swapped), two_got = together(
            [[kv_got, d_query_pre, gate_z, up_swapped], two_got]
        )
        up_z = z_swap(up_swapped)
        kv_pair = add_low(kv_terms[:2], kv_got)
        kv_got = send(kv_pair[1], swap_y)
        rest = width - half
        d_normed_pre = mm_tr(d_query_pre[:, :half], first_a)
        d_normed_pre = d_normed_pre + mm_tr(d_query_pre[:, half:], first_b[:, :rest])
        grad_query = outer_sum(normed_pre, d_query_pre).astype(BF16)
        halves = [
            split_bit(add_low(part[0], got), x, 1) for part, got in zip(halves, two_got, strict=True)
        ]
        two_got = [send(part[1], swap_x) for part in halves]
        kv_got, grad_query, out_got = sync(kv_got, grad_query, out_got)
        out_half = split_bit(add_low(out_half[0], out_got), y, 1)
        out_got = send(out_half[1], swap_y)
        d_kv = (kv_pair[0].astype(F32) + kv_got.astype(F32)).astype(BF16)
        d_kv = jnp.concatenate([d_kv[:, :HD], mm_tr(d_kv[:, HD:], ordered).astype(BF16)], axis=1)
        d_normed_pre = d_normed_pre + mm_tr(d_kv, first_b[:, rest:])
        grad_kv = outer_sum(normed_pre, d_kv).astype(BF16)
        grad_prefix, grad_norm_attn = norm_back(prefix_in, norm_attn, d_normed_pre)
        grad_prefix = (grad_prefix + d_mid_pre)[:tokens]
        act_gains = jnp.stack([grad_norm_attn_act, grad_norm_ffn_act], axis=1).reshape(devices, r32, 2)
        act_gains = jnp.pad(act_gains, ((0, 0), (0, r64 - r32), (0, 0))).reshape(devices * r64, 2)
        gain_grads = jnp.concatenate(
            [jnp.stack([grad_norm_attn, grad_norm_ffn], axis=1), act_gains], axis=1
        ).astype(BF16)
        gain_grads = jnp.pad(gain_grads, ((0, 0), (0, 124)))
        last_a, far_a = light_core(grad_query[:, :half], place)
        last_b, far_b = light_core(
            jnp.concatenate([grad_query[:, half:], grad_kv, gain_grads], axis=1), place
        )
        two_got, (got_a, got_b, far_a, far_b, out_got) = together(
            [two_got, [got_a, got_b, far_a, far_b, out_got]]
        )
        mine_twos = [add_low(out_half[0], out_got)]
        mine_twos += [add_low(part[0], got) for part, got in zip(halves, two_got, strict=True)]
        share_a, share_b = add_low(mine_a, got_a), add_low(mine_b, got_b)
        shares = jnp.concatenate([share_a, share_b], axis=2)
        wide_third = shares.shape[2] // 2
        shares = jnp.concatenate([shares[:, :, :wide_third], shares[:, :, wide_third:]], axis=1)
        second_sums = light_highs(jnp.concatenate(mine_twos + [shares], axis=2), place)
        last_got_a, last_got_b = send(far_a, swap_c), send(far_b, swap_c)
        last_got_a, last_got_b, second_sums, up_z = sync(last_got_a, last_got_b, second_sums, up_z)
        second_z = z_swap(second_sums)
        share_a, share_b = add_low(last_a, last_got_a), add_low(last_b, last_got_b)
        last_a, far_a = split_bit(share_a, x, 1)
        last_b, far_b = split_bit(share_b, y, 2)
        got_a, got_b = send(far_a, swap_x), send(far_b, swap_y)

        def beside(pieces):
            return jnp.concatenate([pieces[t] for t in range(m)], axis=1).astype(F32)

        grad_down_pre = down_z[:, :cols].reshape(m * cols, w).astype(F32)
        grad_gate_act = beside([widened(small_z[t, :flat_act]) for t in range(m)])
        grad_up_act = beside([widened(small_z[t, flat_act : 2 * flat_act]) for t in range(m)])
        last = small_z[:, 2 * flat_act :]
        grad_down_act = jnp.concatenate([last[:, :, :w_act], last[:, :, w_act:]], axis=1)
        grad_down_act = grad_down_act.reshape(m * cols_act, w_act).astype(F32)
        grad_gate_pre = beside(gate_z)
        out_prefix = (mid_pre + add_all(out_z))[:tokens]
        out_actions = (mid_act + branch_act)[:suffix]
        grad_up_pre = beside(up_z)
        got_a, got_b, grad_down_pre, grad_gate_pre, grad_up_pre, out_prefix, out_actions = sync(
            got_a, got_b, grad_down_pre, grad_gate_pre, grad_up_pre, out_prefix, out_actions
        )
        share_a, share_b = add_low(last_a, got_a), add_low(last_b, got_b)
        last_a, far_a = split_bit(share_a, y, 1)
        last_b, far_b = split_bit(share_b, x, 1)
        got_a, got_b = send(far_a, swap_y), send(far_b, swap_x)
        got_a, got_b, second_z = sync(got_a, got_b, second_z)
        got_second = add_all(second_z)
        got_third = got_second[:, width + 2 * DS :]
        got_third = jnp.concatenate([got_third[:r32], got_third[r32:]], axis=1)
        share_a, share_b = add_low(last_a, got_a), add_low(last_b, got_b)
        first_z = z_swap(light_highs(jnp.concatenate([share_a, share_b], axis=2), place))
        got_first = add_all(first_z)

        wide_end = width + 2 * HD
        tail = got_third[:, at + DS :]
        return (
            out_prefix[None],
            out_actions[None, None],
            grad_prefix[None],
            grad_actions[None, None],
            got_first[:, :width],
            got_first[:, width : width + HD],
            got_first[:, width + HD : wide_end],
            got_second[:, :width],
            got_first[:, wide_end],
            got_first[:, wide_end + 1],
            got_third[:, :width],
            got_third[:, width : width + HD],
            got_third[:, width + HD : wide_end],
            got_second[:, width : width + DS],
            got_first[:r32, wide_end + 2],
            got_first[:r32, wide_end + 3],
            tail[:, :32],
            got_second[:, width + DS : width + 2 * DS],
            got_third[:, at : at + DS],
            tail[:, 32:64],
            grad_gate_pre,
            grad_up_pre,
            grad_down_pre,
            grad_gate_act,
            grad_up_act,
            grad_down_act,
        )

    return per_device


def solution(mesh):
    rows = P(("dp", "ctx"), None)
    line = P(("dp", "ctx"))
    return jax.shard_map(
        make_body(mesh.shape["dp"], mesh.shape["ctx"]),
        mesh=mesh,
        in_specs=(
            P("dp", "ctx", None),
            P("dp", "ctx", None, None),
            P("dp", None),
            P("dp"),
            P("dp", "ctx"),
            rows,
            rows,
            rows,
            rows,
            line,
            line,
            rows,
            rows,
            rows,
            rows,
            line,
            line,
            rows,
            rows,
            rows,
            rows,
            P("dp", "ctx"),
            P("dp", "ctx"),
            P("ctx", "dp"),
            P("dp", "ctx"),
            P("dp", "ctx"),
            P("ctx", "dp"),
            P("dp", "ctx", None),
            P("dp", "ctx", None, None),
        ),
        out_specs=(
            P("dp", "ctx", None),
            P("dp", "ctx", None, None),
            P("dp", "ctx", None),
            P("dp", "ctx", None, None),
            rows,
            rows,
            rows,
            rows,
            line,
            line,
            rows,
            rows,
            rows,
            rows,
            line,
            line,
            rows,
            rows,
            rows,
            rows,
            P("dp", "ctx"),
            P("dp", "ctx"),
            P("ctx", "dp"),
            P("dp", "ctx"),
            P("dp", "ctx"),
            P("ctx", "dp"),
        ),
        check_vma=False,
    )
```

time: 1580 us -> 1300 us (0.82)
  waiting for transfers between devices: 672 us -> 392 us
  starting transfers between devices: 241 us -> 125 us
  other arithmetic: 194 us -> 296 us
  Pallas kernels: 0 us -> 44.2 us
  matrix products: 267 us -> 225 us
    ppermute x110 -> x67, waiting for transfers between devices: 638 us -> 257 us  [send(): return lax.ppermute(array, AXES, pairs)]
    ppermute x110 -> x67, starting transfers between devices: 240 us -> 51.1 us  [send(): return lax.ppermute(array, AXES, pairs)]
    all_to_all x0 -> x15, waiting for transfers between devices: none -> 135 us  [z_swap(): return lax.all_to_all(parts, AXES, 0, 0, axis_index_groups=lines_z)]
    all_to_all x0 -> x15, starting transfers between devices: none -> 73.8 us  [z_swap(): return lax.all_to_all(parts, AXES, 0, 0, axis_index_groups=lines_z)]
    dot_general x13 -> x14, matrix products: 71.3 us -> 22.2 us  [outer_sum(): lax.dot_general(left, right, (((0,), (0,)), ((), ())), preferred_element_...]
    pallas_call x0 -> x3, Pallas kernels: none -> 44.2 us  [outer_sums(): pl.pallas_call(lambda *refs: outer_kernel(count, *refs), grid=(height //...]
    convert_element_type x26 -> x34, other arithmetic: 35.8 us -> 72 us  [add_low(): return (left.astype(F32) + right.astype(F32)).astype(BF16)]
    reduce_scatter x2, waiting for transfers between devices: 34.4 us -> 0.01 us  [scatter_act(): lax.psum_scatter(block, AXES, scatter_dimension=0, tiled=True, axis_index...]
  transfers between devices with their start and end apart: 116 -> 86, of which waited for: 53 -> 34; matrix products, arithmetic and copies ran while one was open for 37% -> 50% of each run, Pallas kernels for 0% -> 3%
where the time goes in v2:
time: 1300 us; the launch traced here: 1280 us
  waiting for transfers between devices  392 us (30%)
  other arithmetic  296 us (23%)
  matrix products  225 us (17%)
  local copies, waits for them, and re-layouts  183 us (14%)
  starting transfers between devices  125 us (10%)
  Pallas kernels  44.2 us (3%)
  between operations  19.5 us (2%)
    ppermute x67, waiting for transfers between devices, send(): return lax.ppermute(array, AXES, pairs)  257 us
    all_to_all x15, waiting for transfers between devices, z_swap(): return lax.all_to_all(parts, AXES, 0, 0, axis_index_groups=lines_z)  135 us
    dot_general x24, matrix products, mm_tr(): lax.dot_general(left, right, (((1,), (1,)), ((), ())), preferred_element_...  98.3 us
    dot_general x22, matrix products, mm(): return jnp.dot(left, right, preferred_element_type=F32)  88.2 us
    all_to_all x15, starting transfers between devices, z_swap(): return lax.all_to_all(parts, AXES, 0, 0, axis_index_groups=lines_z)  73.8 us
    convert_element_type x34, other arithmetic, add_low(): return (left.astype(F32) + right.astype(F32)).astype(BF16)  72 us
    select_n x28, other arithmetic, in_order(): jnp.where(bit == 0, jnp.stack([mine, other], axis), jnp.stack([other, min...  62.6 us
    unnamed x576, local copies, waits for them, and re-layouts  52.8 us
  transfers between devices with their start and end apart: 86, of which 34 were waited for; matrix products, arithmetic and copies ran while one was open for 50% of the time, Pallas kernels for 3%

profile of v2, /device:TPU:0, one launch (start us, length us, event | category | flops | bytes accessed | tf_op | source)
XLA Modules:
  0.0 1284.3 jit_solution(4803867952742200989)
XLA Ops:
  24.4 25.9 %all-to-all-done = bf16[4,64,2688]{2,1,0:T(8,128)(2,1)S(1)} async-done(((bf16[4,64,2688]{2,1,0:T(8,128)(2,1)}), bf16[4,64,2688]{2,1,0:T(8,128)(2,1)S(1)}, u32[]{:S(2)}, u32[]{:S(2)}) %all-to-all-start) | async-done | bytes 1376288 | tf_op jit(solution)/shard_map/all_to_all | solution.py:136
  67.3 9.0 collective-permute-done
  83.4 24.8 %collective-permute-done.2 = bf16[4,2,64,1280]{3,2,0,1:T(8,128)(2,1)} collective-permute-done((bf16[4,2,64,1280]{3,2,0,1:T(8,128)(2,1)S(1)}, bf16[4,2,64,1280]{3,2,0,1:T(8,128)(2,1)}, u32[]{:S(2)}, u32[]{:S(2)}) %collective-permute-start.2) | collective-permute-done | bytes 1310752 | tf_op jit(solution)/shard_map/ppermute | solution.py:133
  185.1 24.2 %collective-permute-done.10 = bf16[4,2,64,2048]{3,2,1,0:T(8,128)(2,1)} collective-permute-done((bf16[4,2,64,2048]{3,2,1,0:T(8,128)(2,1)}, bf16[4,2,64,2048]{3,2,1,0:T(8,128)(2,1)}, u32[]{:S(2)}, u32[]{:S(2)}) %collective-permute-start.10) | collective-permute-done | bytes 2097184 | tf_op jit(solution)/shard_map/ppermute | solution.py:133
  260.5 22.6 %collective-permute-done.14 = bf16[2,1408,256]{2,1,0:T(8,128)(2,1)} collective-permute-done((bf16[2,1408,256]{2,1,0:T(8,128)(2,1)S(1)}, bf16[2,1408,256]{2,1,0:T(8,128)(2,1)}, u32[]{:S(2)}, u32[]{:S(2)}) %collective-permute-start.14) | collective-permute-done | bytes 1441824 | tf_op jit(solution)/shard_map/ppermute | solution.py:133
  283.1 13.9 %all-to-all-done.4 = bf16[4,256,1024]{2,1,0:T(8,128)(2,1)} async-done(((bf16[4,256,1024]{2,1,0:T(8,128)(2,1)}), bf16[4,256,1024]{2,1,0:T(8,128)(2,1)}, u32[]{:S(2)}, u32[]{:S(2)}) %all-to-all-start.4) | async-done | bytes 2097184 | tf_op jit(solution)/shard_map/all_to_all | solution.py:136
  328.0 21.2 %all-to-all-done.6 = bf16[4,256,1024]{2,1,0:T(8,128)(2,1)} async-done(((bf16[4,256,1024]{2,1,0:T(8,128)(2,1)}), bf16[4,256,1024]{2,1,0:T(8,128)(2,1)}, u32[]{:S(2)}, u32[]{:S(2)}) %all-to-all-start.6) | async-done | bytes 2097184 | tf_op jit(solution)/shard_map/all_to_all | solution.py:136
  380.8 25.9 %collective-permute-done.20 = bf16[4,256,1024]{2,1,0:T(8,128)(2,1)} collective-permute-done((bf16[4,256,1024]{2,1,0:T(8,128)(2,1)}, bf16[4,256,1024]{2,1,0:T(8,128)(2,1)}, u32[]{:S(2)}, u32[]{:S(2)}) %collective-permute-start.20) | collective-permute-done | bytes 2097184 | tf_op jit(solution)/shard_map/ppermute | solution.py:133
  406.7 17.3 %collective-permute-done.18 = bf16[4,2,32,1792]{3,2,0,1:T(8,128)(2,1)S(1)} collective-permute-done((bf16[4,2,32,1792]{3,2,0,1:T(8,128)(2,1)S(1)}, bf16[4,2,32,1792]{3,2,0,1:T(8,128)(2,1)S(1)}, u32[]{:S(2)}, u32[]{:S(2)}) %collective-permute-start.18) | collective-permute-done | bytes 917536 | tf_op jit(solution)/shard_map/ppermute | solution.py:133
  473.3 13.2 %collective-permute-done.23 = bf16[2,160,2048]{2,1,0:T(8,128)(2,1)} collective-permute-done((bf16[2,160,2048]{2,1,0:T(8,128)(2,1)S(1)}, bf16[2,160,2048]{2,1,0:T(8,128)(2,1)}, u32[]{:S(2)}, u32[]{:S(2)}) %collective-permute-start.23) | collective-permute-done | bytes 1310752 | tf_op jit(solution)/shard_map/ppermute | solution.py:133
  511.9 9.6 fusion.264
  521.5 13.4 %multiply_convert_fusion.3 = (bf16[1280,1024]{1,0:T(8,128)(2,1)S(1)}, f32[1280,1024]{1,0:T(8,128)}) fusion(f32[1280,1024]{1,0:T(8,128)S(1)} %fusion.264, bf16[2048,1024]{1,0:T(8,128)(2,1)S(1)} %bitcast.722, bf16[640,2048]{1,0:T(8,128)(2,1)} %collective-permute-done.25, bf16[640,2048]{1,0:T(8,128)(2,1)} %bitcast.665), kind=kOutput, calls=%fused_computation.53 | convolution fusion | flops 5392302080 | bytes 22544384 | tf_op jit(solution)/shard_map/dot_general | solution.py:42
  534.9 9.8 convolution_convert_fusion.1
  571.9 8.1 fusion.262
  580.1 13.4 %multiply_convert_fusion.2 = (bf16[1280,1024]{1,0:T(8,128)(2,1)S(1)}, f32[1280,1024]{1,0:T(8,128)}) fusion(f32[1280,1024]{1,0:T(8,128)S(1)} %fusion.262, bf16[2048,1024]{1,0:T(8,128)(2,1)S(1)} %bitcast.723, bf16[640,2048]{1,0:T(8,128)(2,1)} %collective-permute-done.29, bf16[640,2048]{1,0:T(8,128)(2,1)} %bitcast.108), kind=kOutput, calls=%fused_computation.52 | convolution fusion | flops 5392302080 | bytes 22544384 | tf_op jit(solution)/shard_map/dot_general | solution.py:42
  593.5 9.4 convolution_convert_fusion
  659.3 9.2 fusion.43
  674.4 16.2 %shard_map.485 = bf16[1024,2048]{1,0:T(8,128)(2,1)S(1)} custom-call(bf16[1280,1024]{1,0:T(8,128)(2,1)S(1)} %get-tuple-element.636.refs_0_, bf16[1280,1024]{1,0:T(8,128)(2,1)S(1)} %copy-done.11, bf16[1280,2048]{1,0:T(8,128)(2,1)} %pad_maximum_fusion.3.refs_2_, bf16[1280,2048]{1,0:T(8,128)(2,1)} %pad_maximum_fusion.4.refs_3_), custom_call_target="tpu_custom_call" | custom-call | flops 10737418240 | bytes 19922944 | tf_op jit(solution)/shard_map/pallas_call | solution.py:97
  693.6 11.4 fusion.41
  713.2 10.7 fusion.290
  729.6 10.1 add_convert_fusion.1
  739.8 8.2 fusion.291
  754.2 10.5 add_convert_fusion
  778.6 14.0 %shard_map.487 = bf16[2048,1024]{1,0:T(8,128)(2,1)S(1)} custom-call(bf16[1280,2048]{1,0:T(8,128)(2,1)} %pad_maximum_fusion.1.refs_0_, bf16[1280,2048]{1,0:T(8,128)(2,1)} %pad_maximum_fusion.2.refs_1_, bf16[1280,1024]{1,0:T(8,128)(2,1)S(1)} %copy-done.9, bf16[1280,1024]{1,0:T(8,128)(2,1)S(1)} %copy-done.7), custom_call_target="tpu_custom_call" | custom-call | flops 10737418240 | bytes 19922944 | tf_op jit(solution)/shard_map/pallas_call | solution.py:97
  805.5 14.0 %shard_map.486 = bf16[2048,1024]{1,0:T(8,128)(2,1)S(1)} custom-call(bf16[1280,2048]{1,0:T(8,128)(2,1)} %pad_maximum_fusion.1.refs_0_, bf16[1280,2048]{1,0:T(8,128)(2,1)} %pad_maximum_fusion.2.refs_1_, bf16[1280,1024]{1,0:T(8,128)(2,1)S(1)} %copy-done.6, bf16[1280,1024]{1,0:T(8,128)(2,1)S(1)} %get-tuple-element.462.refs_3_), custom_call_target="tpu_custom_call" | custom-call | flops 10737418240 | bytes 19922944 | tf_op jit(solution)/shard_map/pallas_call | solution.py:97
  857.6 13.0 %collective-permute-done.41 = bf16[320,2048]{1,0:T(8,128)(2,1)} collective-permute-done((bf16[320,2048]{1,0:T(8,128)(2,1)S(1)}, bf16[320,2048]{1,0:T(8,128)(2,1)}, u32[]{:S(2)}, u32[]{:S(2)}) %collective-permute-start.41) | collective-permute-done | bytes 1310752 | tf_op jit(solution)/shard_map/ppermute | solution.py:133
  945.6 33.7 %all-to-all-done.8 = bf16[4,160,2048]{2,1,0:T(8,128)(2,1)} async-done(((bf16[4,160,2048]{2,1,0:T(8,128)(2,1)}), bf16[4,160,2048]{2,1,0:T(8,128)(2,1)}, u32[]{:S(2)}, u32[]{:S(2)}) %all-to-all-start.8) | async-done | bytes 2621472 | tf_op jit(solution)/shard_map/all_to_all | solution.py:136
  1066.8 21.3 %collective-permute-done.53 = bf16[4,2,64,1024]{3,2,0,1:T(8,128)(2,1)} collective-permute-done((bf16[4,2,64,1024]{3,2,0,1:T(8,128)(2,1)}, bf16[4,2,64,1024]{3,2,0,1:T(8,128)(2,1)}, u32[]{:S(2)}, u32[]{:S(2)}) %collective-permute-start.53) | collective-permute-done | bytes 1048608 | tf_op jit(solution)/shard_map/ppermute | solution.py:133
  1137.6 9.5 collective-permute-done.60
  1178.6 22.6 %collective-permute-done.63 = bf16[4,2,64,1280]{3,2,0,1:T(8,128)(2,1)S(1)} collective-permute-done((bf16[4,2,64,1280]{3,2,0,1:T(8,128)(2,1)S(1)}, bf16[4,2,64,1280]{3,2,0,1:T(8,128)(2,1)S(1)}, u32[]{:S(2)}, u32[]{:S(2)}) %collective-permute-start.63) | collective-permute-done | bytes 1310752 | tf_op jit(solution)/shard_map/ppermute | solution.py:133
  1221.3 11.0 all-to-all-done.13
  1245.9 27.4 %all-to-all-done.14 = bf16[4,64,2688]{2,1,0:T(8,128)(2,1)} async-done(((bf16[4,64,2688]{2,1,0:T(8,128)(2,1)}), bf16[4,64,2688]{2,1,0:T(8,128)(2,1)}, u32[]{:S(2)}, u32[]{:S(2)}) %all-to-all-start.14) | async-done | bytes 1376288 | tf_op jit(solution)/shard_map/all_to_all | solution.py:136
  (1110 shorter events, 760.3 us)
Async XLA Ops:
  51.8 57.7 %all-to-all-start.1 = ((bf16[4,64,4096]{2,1,0:T(8,128)(2,1)}), bf16[4,64,4096]{2,1,0:T(8,128)(2,1)}, u32[]{:S(2)}, u32[]{:S(2)}) async-start(bf16[4,64,4096]{2,1,0:T(8,128)(2,1)} %broadcast_in_dim.81), calls=%async_computation.1 | async-start | bytes 4194304 | tf_op jit(solution)/shard_map/all_to_all | solution.py:136
  56.3 128.8 %all-gather.3.cloned.1.call-start = ((), (), s32[]{:S(2)}) async-start(), calls=%async_computation.17 | async-start | bytes 2228224 | tf_op jit(solution)/shard_map/all_gather | solution.py:375
  153.3 90.4 %all-to-all-start.3 = ((bf16[4,1408,256]{2,1,0:T(8,128)(2,1)}), bf16[4,1408,256]{2,1,0:T(8,128)(2,1)S(1)}, u32[]{:S(2)}, u32[]{:S(2)}) async-start(bf16[4,1408,256]{2,1,0:T(8,128)(2,1)} %pad_maximum_fusion.9), calls=%async_computation.3 | async-start | bytes 5767168 | tf_op jit(solution)/shard_map/all_to_all | solution.py:136
  243.6 53.3 %all-to-all-start.4 = ((bf16[4,256,1024]{2,1,0:T(8,128)(2,1)}), bf16[4,256,1024]{2,1,0:T(8,128)(2,1)}, u32[]{:S(2)}, u32[]{:S(2)}) async-start(bf16[4,256,1024]{2,1,0:T(8,128)(2,1)} %pad_maximum_fusion.21), calls=%async_computation.4 | async-start | bytes 4194304 | tf_op jit(solution)/shard_map/all_to_all | solution.py:136
  296.9 52.2 %all-to-all-start.6 = ((bf16[4,256,1024]{2,1,0:T(8,128)(2,1)}), bf16[4,256,1024]{2,1,0:T(8,128)(2,1)}, u32[]{:S(2)}, u32[]{:S(2)}) async-start(bf16[4,256,1024]{2,1,0:T(8,128)(2,1)} %pad_maximum_fusion.22), calls=%async_computation.6 | async-start | bytes 4194304 | tf_op jit(solution)/shard_map/all_to_all | solution.py:136
  318.4 88.3 %collective-permute-start.20 = (bf16[4,256,1024]{2,1,0:T(8,128)(2,1)}, bf16[4,256,1024]{2,1,0:T(8,128)(2,1)}, u32[]{:S(2)}, u32[]{:S(2)}) collective-permute-start(bf16[4,256,1024]{2,1,0:T(8,128)(2,1)} %all-to-all-done.4), channel_id=1, source_target_pairs={{0,4},{1,5},{2,6},{3,7},{4,0},{5,1},{6,2},{7,3},{8,12},{9,13},{10,... | collective-permute-start | bytes 6291464 | tf_op jit(solution)/shard_map/ppermute | solution.py:133
  352.1 96.9 %all-to-all-start.5 = ((bf16[4,160,2048]{2,1,0:T(8,128)(2,1)}), bf16[4,160,2048]{2,1,0:T(8,128)(2,1)}, u32[]{:S(2)}, u32[]{:S(2)}) async-start(bf16[4,160,2048]{2,1,0:T(8,128)(2,1)} %broadcast_in_dim.147), calls=%async_computation.5 | async-start | bytes 5242880 | tf_op jit(solution)/shard_map/all_to_all | solution.py:136
  363.4 60.6 %collective-permute-start.18 = (bf16[4,2,32,1792]{3,2,0,1:T(8,128)(2,1)S(1)}, bf16[4,2,32,1792]{3,2,0,1:T(8,128)(2,1)S(1)}, u32[]{:S(2)}, u32[]{:S(2)}) collective-permute-start(bf16[4,2,32,1792]{3,2,0,1:T(8,128)(2,1)S(1)} %maximum_select_fusion.21), channel_id=1, source_target_pairs={{0,4},{1,5},{2,6},{3,7},{4,0},{5,1},{6,2},{7,3},{8,12},{9,13},{10,... | collective-permute-start | bytes 2752520 | tf_op jit(solution)/shard_map/ppermute | solution.py:133
  365.8 58.3 %collective-permute-start.19 = (bf16[4,2,32,1920]{3,2,1,0:T(8,128)(2,1)S(1)}, bf16[4,2,32,1920]{3,2,1,0:T(8,128)(2,1)S(1)}, u32[]{:S(2)}, u32[]{:S(2)}) collective-permute-start(bf16[4,2,32,1920]{3,2,1,0:T(8,128)(2,1)S(1)} %maximum_select_fusion.20), channel_id=1, source_target_pairs={{0,2},{1,3},{2,0},{3,1},{4,6},{5,7},{6,4},{7,5},{8,10},{9,11},{10,... | collective-permute-start | bytes 2949128 | tf_op jit(solution)/shard_map/ppermute | solution.py:133
  425.2 79.2 %collective-permute-start.26 = (bf16[4,256,1024]{2,1,0:T(8,128)(2,1)}, bf16[4,256,1024]{2,1,0:T(8,128)(2,1)}, u32[]{:S(2)}, u32[]{:S(2)}) collective-permute-start(bf16[4,256,1024]{2,1,0:T(8,128)(2,1)} %all-to-all-done.6), channel_id=1, source_target_pairs={{0,4},{1,5},{2,6},{3,7},{4,0},{5,1},{6,2},{7,3},{8,12},{9,13},{10,... | collective-permute-start | bytes 6291464 | tf_op jit(solution)/shard_map/ppermute | solution.py:133
  459.3 87.8 %all-to-all-start.7 = ((bf16[4,160,2048]{2,1,0:T(8,128)(2,1)}), bf16[4,160,2048]{2,1,0:T(8,128)(2,1)}, u32[]{:S(2)}, u32[]{:S(2)}) async-start(bf16[4,160,2048]{2,1,0:T(8,128)(2,1)} %broadcast_in_dim.153), calls=%async_computation.7 | async-start | bytes 5242880 | tf_op jit(solution)/shard_map/all_to_all | solution.py:136
  464.1 99.4 %all-gather.5.cloned.1.call-start = ((), (), s32[]{:S(2)}) async-start(), calls=%async_computation.18 | async-start | bytes 2228224 | tf_op jit(solution)/shard_map/all_gather | solution.py:375
  510.2 311.3 %reduce-scatter.3.cloned.1.call-start = ((), (), s32[]{:S(2)}) async-start(), calls=%async_computation.19 | async-start | bytes 2228224 | tf_op jit(solution)/shard_map/reduce_scatter | solution.py:378
  550.8 83.2 %collective-permute-start.31 = (bf16[2,160,2048]{2,1,0:T(8,128)(2,1)}, bf16[2,160,2048]{2,1,0:T(8,128)(2,1)}, u32[]{:S(2)}, u32[]{:S(2)}) collective-permute-start(bf16[2,160,2048]{2,1,0:T(8,128)(2,1)} %get-tuple-element.529), channel_id=1, source_target_pairs={{0,2},{1,3},{2,0},{3,1},{4,6},{5,7},{6,4},{7,5},{8,10},{9,11},{10,... | collective-permute-start | bytes 3932168 | tf_op jit(solution)/shard_map/ppermute | solution.py:133
  553.3 55.6 %collective-permute-start.28 = (bf16[2,160,2048]{2,1,0:T(8,128)(2,1)}, bf16[2,160,2048]{2,1,0:T(8,128)(2,1)}, u32[]{:S(2)}, u32[]{:S(2)}) collective-permute-start(bf16[2,160,2048]{2,1,0:T(8,128)(2,1)} %get-tuple-element.530), channel_id=1, source_target_pairs={{0,2},{1,3},{2,0},{3,1},{4,6},{5,7},{6,4},{7,5},{8,10},{9,11},{10,... | collective-permute-start | bytes 3932168 | tf_op jit(solution)/shard_map/ppermute | solution.py:133
  555.0 53.9 %collective-permute-start.27 = (bf16[640,2048]{1,0:T(8,128)(2,1)}, bf16[640,2048]{1,0:T(8,128)(2,1)}, u32[]{:S(2)}, u32[]{:S(2)}) collective-permute-start(bf16[640,2048]{1,0:T(8,128)(2,1)} %slice.886), channel_id=1, source_target_pairs={{0,1},{1,0},{2,3},{3,2},{4,5},{5,4},{6,7},{7,6},{8,9},{9,8},{10,11... | collective-permute-start | bytes 7864328 | tf_op jit(solution)/shard_map/ppermute | solution.py:133
  643.8 61.2 %collective-permute-start.34 = (bf16[320,2048]{1,0:T(8,128)(2,1)}, bf16[320,2048]{1,0:T(8,128)(2,1)}, u32[]{:S(2)}, u32[]{:S(2)}) collective-permute-start(bf16[320,2048]{1,0:T(8,128)(2,1)} %slice.1129), channel_id=1, source_target_pairs={{0,2},{1,3},{2,0},{3,1},{4,6},{5,7},{6,4},{7,5},{8,10},{9,11},{10,... | collective-permute-start | bytes 3932168 | tf_op jit(solution)/shard_map/ppermute | solution.py:133
  645.5 182.7 %reduce-scatter.5.cloned.1.call-start = ((), (), s32[]{:S(2)}) async-start(), calls=%async_computation.20 | async-start | bytes 2228224 | tf_op jit(solution)/shard_map/reduce_scatter | solution.py:378
  645.6 102.4 %collective-permute-start.36 = (bf16[4,384,256]{2,1,0:T(8,128)(2,1)}, bf16[4,384,256]{2,1,0:T(8,128)(2,1)}, u32[]{:S(2)}, u32[]{:S(2)}) collective-permute-start(bf16[4,384,256]{2,1,0:T(8,128)(2,1)} %pad_maximum_fusion.35), channel_id=1, source_target_pairs={{0,4},{1,5},{2,6},{3,7},{4,0},{5,1},{6,2},{7,3},{8,12},{9,13},{10,... | collective-permute-start | bytes 2359304 | tf_op jit(solution)/shard_map/ppermute | solution.py:133
  653.1 94.8 %collective-permute-start.33 = (bf16[320,2048]{1,0:T(8,128)(2,1)}, bf16[320,2048]{1,0:T(8,128)(2,1)}, u32[]{:S(2)}, u32[]{:S(2)}) collective-permute-start(bf16[320,2048]{1,0:T(8,128)(2,1)} %slice.1128), channel_id=1, source_target_pairs={{0,2},{1,3},{2,0},{3,1},{4,6},{5,7},{6,4},{7,5},{8,10},{9,11},{10,... | collective-permute-start | bytes 3932168 | tf_op jit(solution)/shard_map/ppermute | solution.py:133
  770.2 71.7 %all-to-all-start.12 = ((bf16[4,160,2048]{2,1,0:T(8,128)(2,1)}), bf16[4,160,2048]{2,1,0:T(8,128)(2,1)}, u32[]{:S(2)}, u32[]{:S(2)}) async-start(bf16[4,160,2048]{2,1,0:T(8,128)(2,1)} %bitcast.668), calls=%async_computation.14 | async-start | bytes 5242880 | tf_op jit(solution)/shard_map/all_to_all | solution.py:136
  845.3 70.2 %all-to-all-start.11 = ((bf16[4,1408,256]{2,1,0:T(8,128)(2,1)}), bf16[4,1408,256]{2,1,0:T(8,128)(2,1)}, u32[]{:S(2)}, u32[]{:S(2)}) async-start(bf16[4,1408,256]{2,1,0:T(8,128)(2,1)} %pad_maximum_fusion.10), calls=%async_computation.13 | async-start | bytes 5767168 | tf_op jit(solution)/shard_map/all_to_all | solution.py:136
  854.0 91.7 %collective-permute-start.42 = (bf16[4,256,1024]{2,1,0:T(8,128)(2,1)}, bf16[4,256,1024]{2,1,0:T(8,128)(2,1)}, u32[]{:S(2)}, u32[]{:S(2)}) collective-permute-start(bf16[4,256,1024]{2,1,0:T(8,128)(2,1)} %dynamic-slice_bitcast_fusion.2), channel_id=1, source_target_pairs={{0,4},{1,5},{2,6},{3,7},{4,0},{5,1},{6,2},{7,3},{8,12},{9,13},{10,... | collective-permute-start | bytes 6291464 | tf_op jit(solution)/shard_map/ppermute | solution.py:133
  901.6 106.2 %collective-permute-start.43 = (bf16[4,256,1024]{2,1,0:T(8,128)(2,1)}, bf16[4,256,1024]{2,1,0:T(8,128)(2,1)}, u32[]{:S(2)}, u32[]{:S(2)}) collective-permute-start(bf16[4,256,1024]{2,1,0:T(8,128)(2,1)} %dynamic-slice_bitcast_fusion.1), channel_id=1, source_target_pairs={{0,4},{1,5},{2,6},{3,7},{4,0},{5,1},{6,2},{7,3},{8,12},{9,13},{10,... | collective-permute-start | bytes 6291464 | tf_op jit(solution)/shard_map/ppermute | solution.py:133
  915.5 63.8 %all-to-all-start.8 = ((bf16[4,160,2048]{2,1,0:T(8,128)(2,1)}), bf16[4,160,2048]{2,1,0:T(8,128)(2,1)}, u32[]{:S(2)}, u32[]{:S(2)}) async-start(bf16[4,160,2048]{2,1,0:T(8,128)(2,1)} %bitcast.667), calls=%async_computation.10 | async-start | bytes 5242880 | tf_op jit(solution)/shard_map/all_to_all | solution.py:136
  999.0 67.8 %all-to-all-start.9 = ((bf16[4,256,1024]{2,1,0:T(8,128)(2,1)}), bf16[4,256,1024]{2,1,0:T(8,128)(2,1)}, u32[]{:S(2)}, u32[]{:S(2)}) async-start(bf16[4,256,1024]{2,1,0:T(8,128)(2,1)} %fusion.26), calls=%async_computation.11 | async-start | bytes 4194304 | tf_op jit(solution)/shard_map/all_to_all | solution.py:136
  1028.3 59.8 %collective-permute-start.53 = (bf16[4,2,64,1024]{3,2,0,1:T(8,128)(2,1)}, bf16[4,2,64,1024]{3,2,0,1:T(8,128)(2,1)}, u32[]{:S(2)}, u32[]{:S(2)}) collective-permute-start(bf16[4,2,64,1024]{3,2,0,1:T(8,128)(2,1)} %dynamic-slice_bitcast_fusion.6), channel_id=1, source_target_pairs={{0,2},{1,3},{2,0},{3,1},{4,6},{5,7},{6,4},{7,5},{8,10},{9,11},{10,... | collective-permute-start | bytes 3145736 | tf_op jit(solution)/shard_map/ppermute | solution.py:133
  1050.8 86.7 %collective-permute-start.58 = (bf16[4,32,1792]{2,1,0:T(8,128)(2,1)}, bf16[4,32,1792]{2,1,0:T(8,128)(2,1)}, u32[]{:S(2)}, u32[]{:S(2)}) collective-permute-start(bf16[4,32,1792]{2,1,0:T(8,128)(2,1)} %dynamic-slice_bitcast_fusion.15), channel_id=1, source_target_pairs={{0,2},{1,3},{2,0},{3,1},{4,6},{5,7},{6,4},{7,5},{8,10},{9,11},{10,... | collective-permute-start | bytes 1376264 | tf_op jit(solution)/shard_map/ppermute | solution.py:133
  1054.2 83.4 %collective-permute-start.59 = (bf16[4,32,1920]{2,1,0:T(8,128)(2,1)}, bf16[4,32,1920]{2,1,0:T(8,128)(2,1)}, u32[]{:S(2)}, u32[]{:S(2)}) collective-permute-start(bf16[4,32,1920]{2,1,0:T(8,128)(2,1)} %dynamic-slice_bitcast_fusion.14), channel_id=1, source_target_pairs={{0,4},{1,5},{2,6},{3,7},{4,0},{5,1},{6,2},{7,3},{8,12},{9,13},{10,... | collective-permute-start | bytes 1474568 | tf_op jit(solution)/shard_map/ppermute | solution.py:133
  1065.6 48.9 %collective-permute-start.55 = (bf16[4,2,64,2048]{3,2,0,1:T(8,128)(2,1)}, bf16[4,2,64,2048]{3,2,0,1:T(8,128)(2,1)}, u32[]{:S(2)}, u32[]{:S(2)}) collective-permute-start(bf16[4,2,64,2048]{3,2,0,1:T(8,128)(2,1)} %dynamic-slice_bitcast_fusion), channel_id=1, source_target_pairs={{0,4},{1,5},{2,6},{3,7},{4,0},{5,1},{6,2},{7,3},{8,12},{9,13},{10,... | collective-permute-start | bytes 6291464 | tf_op jit(solution)/shard_map/ppermute | solution.py:133
  1088.8 68.9 %all-to-all-start.10 = ((bf16[4,256,1024]{2,1,0:T(8,128)(2,1)}), bf16[4,256,1024]{2,1,0:T(8,128)(2,1)}, u32[]{:S(2)}, u32[]{:S(2)}) async-start(bf16[4,256,1024]{2,1,0:T(8,128)(2,1)} %fusion.25), calls=%async_computation.12 | async-start | bytes 4194304 | tf_op jit(solution)/shard_map/all_to_all | solution.py:136
  1157.7 74.6 %all-to-all-start.13 = ((bf16[4,64,5952]{2,1,0:T(8,128)(2,1)}), bf16[4,64,5952]{2,1,0:T(8,128)(2,1)S(1)}, u32[]{:S(2)}, u32[]{:S(2)}) async-start(bf16[4,64,5952]{2,1,0:T(8,128)(2,1)} %fusion.39), calls=%async_computation.15 | async-start | bytes 6160384 | tf_op jit(solution)/shard_map/all_to_all | solution.py:136
  (316 other events, 4246.7 us)
Sparse Core Ops, SparseCore 0:
  117.2 67.8 all-gather.2
  510.3 48.3 all-gather.4
  645.7 68.0 reduce-scatter.2
  729.7 72.1 reduce-scatter.4

commit v3 on v2

--- a/solution.py
+++ b/solution.py
@@ -374,11 +374,6 @@
         def gather_act(block):
             return lax.all_gather(block, AXES, axis=0, tiled=True, axis_index_groups=sharing)
 
-        def scatter_act(block):
-            return lax.psum_scatter(
-                block, AXES, scatter_dimension=0, tiled=True, axis_index_groups=sharing
-            ).astype(F32)
-
         prefix_in = pad_rows(prefix_tokens[0], rows_pre).astype(F32)
         cot_own = pad_rows(grad_pre[0], rows_pre)
         piece_of = down_piece(down_pre, gate_act, up_act, down_act)
@@ -466,11 +461,12 @@
         attn_parts = core_parts(attn_pre)
         mid_pre = prefix_in + mm(attn_parts[0], out_parts[0]) + mm(attn_parts[1], out_parts[1])
         normed_two_pre = rms_norm(mid_pre, norm_ffn).astype(BF16)
-        normed_two_pre, cot_own, third_z, gate_z, up_own, down_far_a, down_z_b = sync(
-            normed_two_pre, cot_own, third_z, gate_z, up_own, down_far_a, down_z_b
-        )
+        normed_two_pre, cot_own, third_z, down_far_a, down_z_b = sync(
+            normed_two_pre, cot_own, third_z, down_far_a, down_z_b
+        )
+        down_far_b = send(down_z_b, swap_x)
+        gate_z, up_own, down_far_b = sync(gate_z, up_own, down_far_b)
         up_z = z_swap(up_own)
-        down_far_b = send(down_z_b, swap_x)
         gate_far = send(gate_z, swap_x)
         third_z = with_highs(third_z, place)
         three_a, three_b = third_z[:, :, :third_half], third_z[:, :, third_half:]
@@ -480,9 +476,10 @@
         three_a, three_b = in_order(y, three_a, third_a, 1), in_order(x, three_b, third_b, 1)
         third_a, third_b = send(three_a, swap_x), send(three_b, swap_y)
         down_full = columns_full(down_z, jnp.concatenate([down_far_a, down_far_b]), place)
-        third_a, third_b, gate_far, up_z = sync(third_a, third_b, gate_far, up_z)
+        gate_far, up_z = sync(gate_far, up_z)
         up_far = send(up_z, swap_x)
         gate_full = rows_full(gate_z, gate_far, place)
+        third_a, third_b, gate_full = sync(third_a, third_b, gate_full)
         three_a, three_b = in_order(x, three_a, third_a, 1), in_order(y, three_b, third_b, 2)
         third_a, third_b = send(three_a, swap_c), send(three_b, swap_c)
         third = jnp.concatenate(
@@ -539,7 +536,7 @@
             side_input + mm(attn_act_parts[0], out_act_parts[0]) + mm(attn_act_parts[1], out_act_parts[1])
         )
         normed_two_act = rms_norm(mid_act, norm_ffn_act).astype(BF16)
-        row_got, normed_two_act, row_z_odd = sync(row_got, normed_two_act, row_z[two:])
+        row_got, normed_two_act, row_z_odd, up_far = sync(row_got, normed_two_act, row_z[two:], up_far)
         rows_all_act = gather_act(normed_two_act)
         near = pairs_of(row_z[:two], row_got)
         row_far = send(near, swap_c)
@@ -559,13 +556,6 @@
         four_rows = 2 * two * rows_pre
         even_got = send(part_e[four_rows:], swap_c)
         unit_o = ffn_unit(mm(row_o, gate_full), row_o, up_full, narrow)
-        even_got, cot_got, part_o = sync(even_got, cot_got, unit_o[3])
-        near_e = pairs_of(cot_z[:two], cot_got)
-        far_e = send(near_e, swap_c)
-        cot_got = cot_other_got
-        two_rows = 2 * rows_pre
-        out_even = add_low(part_e[:four_rows], even_got)
-        odd_got = send(part_o[four_rows:], swap_c)
         gate_act_value, up_act_value, hidden_act, part_act = ffn_unit(
             mm(rows_all_act, wide_act[0]), rows_all_act, wide_act[1], narrow_act
         )
@@ -596,53 +586,70 @@
             axis=0,
         )
         small_mine, small_theirs = split_columns(narrow_parts, place)
-        far_e, cot_got, odd_got, d_rows_act, part_act, small_theirs = sync(
-            far_e, cot_got, odd_got, d_rows_act, part_act, small_theirs
-        )
-        d_branch_act = scatter_act(d_rows_act)
+        act_sums = jnp.concatenate(
+            [part.reshape(m, 2, 2, rows_act, DS) for part in (part_act, d_rows_act)], axis=3
+        )
+        act_mine, act_theirs = split_bit(act_sums, c, 2)
+        even_got, cot_got, part_o, act_theirs, small_theirs = sync(
+            even_got, cot_got, unit_o[3], act_theirs, small_theirs
+        )
+        act_got = send(act_theirs, swap_c)
         small_got = send(small_theirs, swap_x)
+        near_e = pairs_of(cot_z[:two], cot_got)
+        far_e = send(near_e, swap_c)
+        cot_got = cot_other_got
+        two_rows = 2 * rows_pre
+        out_even = add_low(part_e[:four_rows], even_got)
+        even_got = send(out_even[two_rows:], swap_y)
+        odd_got = send(part_o[four_rows:], swap_c)
+        far_e, cot_got, odd_got, act_got = sync(far_e, cot_got, odd_got, act_got)
+        act_mine, act_theirs = split_bit(add_low(act_mine, act_got), y, 1)
+        act_got = send(act_theirs, swap_y)
         cot_e = jnp.concatenate([near_e, far_e])
         near_o = pairs_of(cot_z[two:], cot_got)
         far_o = send(near_o, swap_c)
-        even_got = send(out_even[two_rows:], swap_y)
+        out_odd = add_low(part_o[:four_rows], odd_got)
+        odd_got = send(out_odd[two_rows:], swap_y)
         d_hidden_e = mm_tr(cot_e, narrow)
-        far_o, d_hidden_e = sync(far_o, d_hidden_e)
+        far_o, d_hidden_e, act_got, even_got = sync(far_o, d_hidden_e, act_got, even_got)
+        act_mine = add_low(act_mine, act_got)
+        act_z = z_swap(jnp.concatenate([act_mine[:, :rows_act], act_mine[:, rows_act:]], axis=2))
         cot_o = jnp.concatenate([near_o, far_o])
         grad_down = outer_sums([unit_e[2], unit_o[2]], [cot_e, cot_o])
         down_mine, down_theirs = split_columns(grad_down, place)
         d_hidden_o = mm_tr(cot_o, narrow)
-        even_got, down_theirs, d_hidden_o, part_act = sync(even_got, down_theirs, d_hidden_o, part_act)
-        branch_act = scatter_act(part_act)
+        odd_got, down_theirs, d_hidden_o, act_z = sync(odd_got, down_theirs, d_hidden_o, act_z)
         out_even = add_low(out_even[:two_rows], even_got)
-        out_odd = add_low(part_o[:four_rows], odd_got)
-        odd_got = send(out_odd[two_rows:], swap_y)
+        out_odd = add_low(out_odd[:two_rows], odd_got)
+        out_z = z_swap(jnp.concatenate([out_even, out_odd]).reshape(m, rows_pre, width))
         down_got = send(down_theirs, swap_x)
         back_o = ffn_back(d_hidden_o, unit_o[0], unit_o[1], wide)
-        odd_got, back_o_rows, small_got, down_got = sync(odd_got, back_o[0], small_got, down_got)
-        out_odd = add_low(out_odd[:two_rows], odd_got)
-        out_z = z_swap(jnp.concatenate([out_even, out_odd]).reshape(m, rows_pre, width))
+        (back_o_rows,) = sync(back_o[0])
         odd_got = send(back_o_rows[four_rows:], swap_c)
         back_e = ffn_back(d_hidden_e, unit_e[0], unit_e[1], wide)
-        odd_got, back_e_rows = sync(odd_got, back_e[0])
+        odd_got, back_e_rows, row_e, row_o, small_got, down_got = sync(
+            odd_got, back_e[0], row_e, row_o, small_got, down_got
+        )
         d_odd = add_low(back_o_rows[:four_rows], odd_got)
         odd_got = send(d_odd[two_rows:], swap_y)
         even_got = send(back_e_rows[four_rows:], swap_c)
         down_both = [add_low(down_mine, down_got), add_low(small_mine, small_got)]
-        down_sums = jnp.concatenate(down_both, axis=1)
+        down_z = z_swap(jnp.concatenate(down_both, axis=1))
         grad_gate = outer_sums([row_e, row_o], [back_e[1], back_o[1]])
-        odd_got, even_got, grad_gate, down_sums = sync(odd_got, even_got, grad_gate, down_sums)
-        down_z = z_swap(down_sums)
+        odd_got, even_got, grad_gate, row_e, row_o = sync(odd_got, even_got, grad_gate, row_e, row_o)
         d_odd = add_low(d_odd[:two_rows], odd_got)
         d_even = add_low(back_e_rows[:four_rows], even_got)
         even_got = send(d_even[two_rows:], swap_y)
         gate_mine, gate_theirs = split_rows(grad_gate, place)
         gate_got = send(gate_theirs, swap_x)
         grad_up = outer_sums([row_e, row_o], [back_e[2], back_o[2]])
-        even_got, grad_up, d_branch_act, branch_act = sync(even_got, grad_up, d_branch_act, branch_act)
+        even_got, grad_up, act_z, gate_got = sync(even_got, grad_up, act_z, gate_got)
         d_even = add_low(d_even[:two_rows], even_got)
         d_z = z_swap(jnp.concatenate([d_even, d_odd]).reshape(m, rows_pre, width))
         up_mine, up_theirs = split_rows(grad_up, place)
         up_got = send(up_theirs, swap_x)
+        act_total = add_all(act_z)
+        branch_act, d_branch_act = act_total[:, :DS], act_total[:, DS:]
         d_mid_act, grad_norm_ffn_act = norm_back(mid_act, norm_ffn_act, d_branch_act)
         d_mid_act = d_mid_act + pad_rows(grad_act[0, 0], rows_act).astype(F32)
         d_mid_act_low = d_mid_act.astype(BF16)
@@ -700,8 +707,8 @@
 
         twos = [grads_out_act, grads_mix_first]
         theirs_twos = [of_core(1 - c, pair) for pair in twos]
-        (d_z, theirs_a, theirs_b, gate_got), theirs_twos, *twos = together(
-            [[d_z, theirs_a, theirs_b, gate_got], theirs_twos] + twos
+        (d_z, theirs_a, theirs_b), theirs_twos, *twos = together(
+            [[d_z, theirs_a, theirs_b], theirs_twos] + twos
         )
         gate_z = z_swap(add_low(gate_mine, gate_got))
         got_a, got_b = send(theirs_a, swap_c), send(theirs_b, swap_c)
@@ -746,9 +753,7 @@
         kv_got = send(kv_terms[2:], swap_c)
         d_query_pre = (ein("hqk,kd->qhd", d_scores, keys) * scale).reshape(rows_pre, width).astype(BF16)
         up_swapped = add_low(up_mine, up_got)
-        (kv_got, d_query_pre, gate_z, up_swapped), two_got = together(
-            [[kv_got, d_query_pre, gate_z, up_swapped], two_got]
-        )
+        kv_got, d_query_pre, gate_z, up_swapped = sync(kv_got, d_query_pre, gate_z, up_swapped)
         up_z = z_swap(up_swapped)
         kv_pair = add_low(kv_terms[:2], kv_got)
         kv_got = send(kv_pair[1], swap_y)
@@ -756,11 +761,11 @@
         d_normed_pre = mm_tr(d_query_pre[:, :half], first_a)
         d_normed_pre = d_normed_pre + mm_tr(d_query_pre[:, half:], first_b[:, :rest])
         grad_query = outer_sum(normed_pre, d_query_pre).astype(BF16)
+        (kv_got, grad_query, out_got), two_got = together([[kv_got, grad_query, out_got], two_got])
         halves = [
             split_bit(add_low(part[0], got), x, 1) for part, got in zip(halves, two_got, strict=True)
         ]
         two_got = [send(part[1], swap_x) for part in halves]
-        kv_got, grad_query, out_got = sync(kv_got, grad_query, out_got)
         out_half = split_bit(add_low(out_half[0], out_got), y, 1)
         out_got = send(out_half[1], swap_y)
         d_kv = (kv_pair[0].astype(F32) + kv_got.astype(F32)).astype(BF16)

time: 1300 us -> 1280 us (0.985)
  matrix products: 225 us -> 203 us
  waiting for transfers between devices: 392 us -> 409 us
  local copies, waits for them, and re-layouts: 183 us -> 167 us
    ppermute x67 -> x69, waiting for transfers between devices: 257 us -> 275 us  [send(): return lax.ppermute(array, AXES, pairs)]
    dot_general x24, matrix products: 98.3 us -> 82.7 us  [mm_tr(): lax.dot_general(left, right, (((1,), (1,)), ((), ())), preferred_element_...]
    all_to_all x15 -> x16, starting transfers between devices: 73.8 us -> 79.8 us  [z_swap(): return lax.all_to_all(parts, AXES, 0, 0, axis_index_groups=lines_z)]
    ppermute x67 -> x69, starting transfers between devices: 51.1 us -> 48 us  [send(): return lax.ppermute(array, AXES, pairs)]
    all_to_all x15 -> x16, waiting for transfers between devices: 135 us -> 132 us  [z_swap(): return lax.all_to_all(parts, AXES, 0, 0, axis_index_groups=lines_z)]
    convert_element_type x34 -> x36, other arithmetic: 72 us -> 73.4 us  [add_low(): return (left.astype(F32) + right.astype(F32)).astype(BF16)]
    unnamed x576 -> x603, local copies, waits for them, and re-layouts: 52.8 us -> 53.2 us
  transfers between devices with their start and end apart: 86 -> 87, of which waited for: 34 -> 37; matrix products, arithmetic and copies ran while one was open for 50% -> 46% of each run, Pallas kernels for 3% -> 3%
where the time goes in v3:
time: 1280 us; the launch traced here: 1270 us
  waiting for transfers between devices  409 us (32%)
  other arithmetic  296 us (23%)
  matrix products  203 us (16%)
  local copies, waits for them, and re-layouts  167 us (13%)
  starting transfers between devices  128 us (10%)
  Pallas kernels  44.2 us (3%)
  between operations  20.1 us (2%)
    ppermute x69, waiting for transfers between devices, send(): return lax.ppermute(array, AXES, pairs)  275 us
    all_to_all x16, waiting for transfers between devices, z_swap(): return lax.all_to_all(parts, AXES, 0, 0, axis_index_groups=lines_z)  132 us
    dot_general x24, matrix products, mm_tr(): lax.dot_general(left, right, (((1,), (1,)), ((), ())), preferred_element_...  82.7 us
    dot_general x22, matrix products, mm(): return jnp.dot(left, right, preferred_element_type=F32)  80.5 us
    all_to_all x16, starting transfers between devices, z_swap(): return lax.all_to_all(parts, AXES, 0, 0, axis_index_groups=lines_z)  79.8 us
    convert_element_type x36, other arithmetic, add_low(): return (left.astype(F32) + right.astype(F32)).astype(BF16)  73.4 us
    select_n x28, other arithmetic, in_order(): jnp.where(bit == 0, jnp.stack([mine, other], axis), jnp.stack([other, min...  60.5 us
    unnamed x603, local copies, waits for them, and re-layouts  53.2 us
  transfers between devices with their start and end apart: 87, of which 37 were waited for; matrix products, arithmetic and copies ran while one was open for 46% of the time, Pallas kernels for 3%

profile of v3, /device:TPU:0, one launch (start us, length us, event | category | flops | bytes accessed | tf_op | source)
XLA Modules:
  0.0 1266.9 jit_solution(1259388213342105157)
XLA Ops:
  24.3 26.0 %all-to-all-done = bf16[4,64,2688]{2,1,0:T(8,128)(2,1)S(1)} async-done(((bf16[4,64,2688]{2,1,0:T(8,128)(2,1)}), bf16[4,64,2688]{2,1,0:T(8,128)(2,1)S(1)}, u32[]{:S(2)}, u32[]{:S(2)}) %all-to-all-start) | async-done | bytes 1376288 | tf_op jit(solution)/shard_map/all_to_all | solution.py:136
  67.3 9.0 collective-permute-done
  83.4 24.8 %collective-permute-done.2 = bf16[4,2,64,1280]{3,2,0,1:T(8,128)(2,1)} collective-permute-done((bf16[4,2,64,1280]{3,2,0,1:T(8,128)(2,1)S(1)}, bf16[4,2,64,1280]{3,2,0,1:T(8,128)(2,1)}, u32[]{:S(2)}, u32[]{:S(2)}) %collective-permute-start.2) | collective-permute-done | bytes 1310752 | tf_op jit(solution)/shard_map/ppermute | solution.py:133
  185.0 24.1 %collective-permute-done.10 = bf16[4,2,64,2048]{3,2,1,0:T(8,128)(2,1)} collective-permute-done((bf16[4,2,64,2048]{3,2,1,0:T(8,128)(2,1)}, bf16[4,2,64,2048]{3,2,1,0:T(8,128)(2,1)}, u32[]{:S(2)}, u32[]{:S(2)}) %collective-permute-start.10) | collective-permute-done | bytes 2097184 | tf_op jit(solution)/shard_map/ppermute | solution.py:133
  248.9 24.1 %collective-permute-done.14 = bf16[2,1408,256]{2,1,0:T(8,128)(2,1)S(1)} collective-permute-done((bf16[2,1408,256]{2,1,0:T(8,128)(2,1)S(1)}, bf16[2,1408,256]{2,1,0:T(8,128)(2,1)S(1)}, u32[]{:S(2)}, u32[]{:S(2)}) %collective-permute-start.14) | collective-permute-done | bytes 1441824 | tf_op jit(solution)/shard_map/ppermute | solution.py:133
  281.7 25.3 %collective-permute-done.15 = bf16[2,1408,256]{2,1,0:T(8,128)(2,1)} collective-permute-done((bf16[2,1408,256]{2,1,0:T(8,128)(2,1)}, bf16[2,1408,256]{2,1,0:T(8,128)(2,1)}, u32[]{:S(2)}, u32[]{:S(2)}) %collective-permute-start.15) | collective-permute-done | bytes 1441824 | tf_op jit(solution)/shard_map/ppermute | solution.py:133
  333.1 25.3 %all-to-all-done.6 = bf16[4,256,1024]{2,1,0:T(8,128)(2,1)} async-done(((bf16[4,256,1024]{2,1,0:T(8,128)(2,1)}), bf16[4,256,1024]{2,1,0:T(8,128)(2,1)}, u32[]{:S(2)}, u32[]{:S(2)}) %all-to-all-start.6) | async-done | bytes 2097184 | tf_op jit(solution)/shard_map/all_to_all | solution.py:136
  370.6 15.3 %collective-permute-done.20 = bf16[4,256,1024]{2,1,0:T(8,128)(2,1)} collective-permute-done((bf16[4,256,1024]{2,1,0:T(8,128)(2,1)}, bf16[4,256,1024]{2,1,0:T(8,128)(2,1)}, u32[]{:S(2)}, u32[]{:S(2)}) %collective-permute-start.20) | collective-permute-done | bytes 2097184 | tf_op jit(solution)/shard_map/ppermute | solution.py:133
  453.8 13.6 %collective-permute-done.23 = bf16[2,160,2048]{2,1,0:T(8,128)(2,1)} collective-permute-done((bf16[2,160,2048]{2,1,0:T(8,128)(2,1)S(1)}, bf16[2,160,2048]{2,1,0:T(8,128)(2,1)}, u32[]{:S(2)}, u32[]{:S(2)}) %collective-permute-start.23) | collective-permute-done | bytes 1310752 | tf_op jit(solution)/shard_map/ppermute | solution.py:133
  490.4 8.6 fusion.268
  499.0 9.1 multiply_convert_fusion.3
  508.1 10.9 convolution_convert_fusion.1
  560.5 13.5 %multiply_convert_fusion.2 = (bf16[1280,1024]{1,0:T(8,128)(2,1)S(1)}, f32[1280,1024]{1,0:T(8,128)}) fusion(f32[1280,1024]{1,0:T(8,128)S(1)} %fusion.266, bf16[2048,1024]{1,0:T(8,128)(2,1)S(1)} %bitcast.741, bf16[640,2048]{1,0:T(8,128)(2,1)} %collective-permute-done.29, bf16[640,2048]{1,0:T(8,128)(2,1)} %bitcast.108), kind=kOutput, calls=%fused_computation.52 | convolution fusion | flops 5392302080 | bytes 22544384 | tf_op jit(solution)/shard_map/dot_general | solution.py:42
  574.0 9.2 convolution_convert_fusion
  608.3 15.7 %collective-permute-done.31 = bf16[2,160,2048]{2,1,0:T(8,128)(2,1)S(1)} collective-permute-done((bf16[2,160,2048]{2,1,0:T(8,128)(2,1)}, bf16[2,160,2048]{2,1,0:T(8,128)(2,1)S(1)}, u32[]{:S(2)}, u32[]{:S(2)}) %collective-permute-start.31) | collective-permute-done | bytes 1310752 | tf_op jit(solution)/shard_map/ppermute | solution.py:133
  642.9 10.6 fusion.44
  656.0 22.4 %collective-permute-done.36 = bf16[4,128,1024]{2,1,0:T(8,128)(2,1)S(1)} collective-permute-done((bf16[4,128,1024]{2,1,0:T(8,128)(2,1)S(1)}, bf16[4,128,1024]{2,1,0:T(8,128)(2,1)S(1)}, u32[]{:S(2)}, u32[]{:S(2)}) %collective-permute-start.36) | collective-permute-done | bytes 1048608 | tf_op jit(solution)/shard_map/ppermute | solution.py:133
  693.2 8.8 multiply_convert_fusion
  702.1 16.2 %shard_map.485 = bf16[1024,2048]{1,0:T(8,128)(2,1)S(1)} custom-call(bf16[1280,1024]{1,0:T(8,128)(2,1)S(1)} %copy-done.12, bf16[1280,1024]{1,0:T(8,128)(2,1)S(1)} %copy-done.14, bf16[1280,2048]{1,0:T(8,128)(2,1)} %pad_maximum_fusion.3.refs_2_, bf16[1280,2048]{1,0:T(8,128)(2,1)} %pad_maximum_fusion.4.refs_3_), custom_call_target="tpu_custom_call" | custom-call | flops 10737418240 | bytes 19922944 | tf_op jit(solution)/shard_map/pallas_call | solution.py:97
  722.3 9.3 fusion.42
  757.6 9.6 add_convert_fusion.1
  777.1 9.6 add_convert_fusion
  809.2 14.0 %shard_map.486 = bf16[2048,1024]{1,0:T(8,128)(2,1)S(1)} custom-call(bf16[1280,2048]{1,0:T(8,128)(2,1)} %pad_maximum_fusion.1.refs_0_, bf16[1280,2048]{1,0:T(8,128)(2,1)} %pad_maximum_fusion.2.refs_1_, bf16[1280,1024]{1,0:T(8,128)(2,1)S(1)} %copy-done.6, bf16[1280,1024]{1,0:T(8,128)(2,1)S(1)} %copy-done.10), custom_call_target="tpu_custom_call" | custom-call | flops 10737418240 | bytes 19922944 | tf_op jit(solution)/shard_map/pallas_call | solution.py:97
  840.6 14.0 %shard_map.487 = bf16[2048,1024]{1,0:T(8,128)(2,1)S(1)} custom-call(bf16[1280,2048]{1,0:T(8,128)(2,1)} %pad_maximum_fusion.1.refs_0_, bf16[1280,2048]{1,0:T(8,128)(2,1)} %pad_maximum_fusion.2.refs_1_, bf16[1280,1024]{1,0:T(8,128)(2,1)S(1)} %get-tuple-element.469.refs_2_, bf16[1280,1024]{1,0:T(8,128)(2,1)S(1)} %copy-done.8), custom_call_target="tpu_custom_call" | custom-call | flops 10737418240 | bytes 19922944 | tf_op jit(solution)/shard_map/pallas_call | solution.py:97
  856.6 15.0 %all-to-all-done.12 = bf16[4,1408,256]{2,1,0:T(8,128)(2,1)} async-done(((bf16[4,1408,256]{2,1,0:T(8,128)(2,1)}), bf16[4,1408,256]{2,1,0:T(8,128)(2,1)}, u32[]{:S(2)}, u32[]{:S(2)}) %all-to-all-start.12) | async-done | bytes 2883616 | tf_op jit(solution)/shard_map/all_to_all | solution.py:136
  946.8 27.3 %all-to-all-done.9 = bf16[4,160,2048]{2,1,0:T(8,128)(2,1)} async-done(((bf16[4,160,2048]{2,1,0:T(8,128)(2,1)}), bf16[4,160,2048]{2,1,0:T(8,128)(2,1)}, u32[]{:S(2)}, u32[]{:S(2)}) %all-to-all-start.9) | async-done | bytes 2621472 | tf_op jit(solution)/shard_map/all_to_all | solution.py:136
  1066.1 8.4 collective-permute-done.57
  1074.5 12.3 collective-permute-done.54
  1119.8 9.0 collective-permute-done.59
  1161.0 22.5 %collective-permute-done.65 = bf16[4,2,64,1280]{3,2,0,1:T(8,128)(2,1)S(1)} collective-permute-done((bf16[4,2,64,1280]{3,2,0,1:T(8,128)(2,1)S(1)}, bf16[4,2,64,1280]{3,2,0,1:T(8,128)(2,1)S(1)}, u32[]{:S(2)}, u32[]{:S(2)}) %collective-permute-start.65) | collective-permute-done | bytes 1310752 | tf_op jit(solution)/shard_map/ppermute | solution.py:133
  1203.4 11.3 all-to-all-done.14
  1228.2 27.4 %all-to-all-done.15 = bf16[4,64,2688]{2,1,0:T(8,128)(2,1)} async-done(((bf16[4,64,2688]{2,1,0:T(8,128)(2,1)}), bf16[4,64,2688]{2,1,0:T(8,128)(2,1)}, u32[]{:S(2)}, u32[]{:S(2)}) %all-to-all-start.15) | async-done | bytes 1376288 | tf_op jit(solution)/shard_map/all_to_all | solution.py:136
  (1140 shorter events, 744.9 us)
Async XLA Ops:
  51.8 57.7 %all-to-all-start.1 = ((bf16[4,64,4096]{2,1,0:T(8,128)(2,1)}), bf16[4,64,4096]{2,1,0:T(8,128)(2,1)}, u32[]{:S(2)}, u32[]{:S(2)}) async-start(bf16[4,64,4096]{2,1,0:T(8,128)(2,1)} %broadcast_in_dim.81), calls=%async_computation.1 | async-start | bytes 4194304 | tf_op jit(solution)/shard_map/all_to_all | solution.py:136
  56.3 128.6 %all-gather.3.cloned.1.call-start = ((), (), s32[]{:S(2)}) async-start(), calls=%async_computation.16 | async-start | bytes 2228224 | tf_op jit(solution)/shard_map/all_gather | solution.py:375
  153.0 76.7 %all-to-all-start.3 = ((bf16[4,1408,256]{2,1,0:T(8,128)(2,1)}), bf16[4,1408,256]{2,1,0:T(8,128)(2,1)S(1)}, u32[]{:S(2)}, u32[]{:S(2)}) async-start(bf16[4,1408,256]{2,1,0:T(8,128)(2,1)} %pad_maximum_fusion.9), calls=%async_computation.3 | async-start | bytes 5767168 | tf_op jit(solution)/shard_map/all_to_all | solution.py:136
  233.0 74.0 %all-to-all-start.5 = ((bf16[4,256,1024]{2,1,0:T(8,128)(2,1)}), bf16[4,256,1024]{2,1,0:T(8,128)(2,1)}, u32[]{:S(2)}, u32[]{:S(2)}) async-start(bf16[4,256,1024]{2,1,0:T(8,128)(2,1)} %pad_maximum_fusion.21), calls=%async_computation.5 | async-start | bytes 4194304 | tf_op jit(solution)/shard_map/all_to_all | solution.py:136
  307.0 51.3 %all-to-all-start.6 = ((bf16[4,256,1024]{2,1,0:T(8,128)(2,1)}), bf16[4,256,1024]{2,1,0:T(8,128)(2,1)}, u32[]{:S(2)}, u32[]{:S(2)}) async-start(bf16[4,256,1024]{2,1,0:T(8,128)(2,1)} %pad_maximum_fusion.22), calls=%async_computation.6 | async-start | bytes 4194304 | tf_op jit(solution)/shard_map/all_to_all | solution.py:136
  327.1 58.8 %collective-permute-start.20 = (bf16[4,256,1024]{2,1,0:T(8,128)(2,1)}, bf16[4,256,1024]{2,1,0:T(8,128)(2,1)}, u32[]{:S(2)}, u32[]{:S(2)}) collective-permute-start(bf16[4,256,1024]{2,1,0:T(8,128)(2,1)} %all-to-all-done.5), channel_id=1, source_target_pairs={{0,4},{1,5},{2,6},{3,7},{4,0},{5,1},{6,2},{7,3},{8,12},{9,13},{10,... | collective-permute-start | bytes 6291464 | tf_op jit(solution)/shard_map/ppermute | solution.py:133
  361.3 66.5 %all-to-all-start.4 = ((bf16[4,160,2048]{2,1,0:T(8,128)(2,1)}), bf16[4,160,2048]{2,1,0:T(8,128)(2,1)}, u32[]{:S(2)}, u32[]{:S(2)}) async-start(bf16[4,160,2048]{2,1,0:T(8,128)(2,1)} %broadcast_in_dim.147), calls=%async_computation.4 | async-start | bytes 5242880 | tf_op jit(solution)/shard_map/all_to_all | solution.py:136
  385.9 67.9 %collective-permute-start.24 = (bf16[4,256,1024]{2,1,0:T(8,128)(2,1)}, bf16[4,256,1024]{2,1,0:T(8,128)(2,1)}, u32[]{:S(2)}, u32[]{:S(2)}) collective-permute-start(bf16[4,256,1024]{2,1,0:T(8,128)(2,1)} %all-to-all-done.6), channel_id=1, source_target_pairs={{0,4},{1,5},{2,6},{3,7},{4,0},{5,1},{6,2},{7,3},{8,12},{9,13},{10,... | collective-permute-start | bytes 6291464 | tf_op jit(solution)/shard_map/ppermute | solution.py:133
  439.9 80.7 %all-to-all-start.7 = ((bf16[4,160,2048]{2,1,0:T(8,128)(2,1)}), bf16[4,160,2048]{2,1,0:T(8,128)(2,1)}, u32[]{:S(2)}, u32[]{:S(2)}) async-start(bf16[4,160,2048]{2,1,0:T(8,128)(2,1)} %broadcast_in_dim.153), calls=%async_computation.7 | async-start | bytes 5242880 | tf_op jit(solution)/shard_map/all_to_all | solution.py:136
  444.9 89.3 %all-gather.5.cloned.1.call-start = ((), (), s32[]{:S(2)}) async-start(), calls=%async_computation.17 | async-start | bytes 2228224 | tf_op jit(solution)/shard_map/all_gather | solution.py:375
  524.3 58.8 %collective-permute-start.28 = (bf16[2,160,2048]{2,1,0:T(8,128)(2,1)}, bf16[2,160,2048]{2,1,0:T(8,128)(2,1)}, u32[]{:S(2)}, u32[]{:S(2)}) collective-permute-start(bf16[2,160,2048]{2,1,0:T(8,128)(2,1)} %get-tuple-element.542), channel_id=1, source_target_pairs={{0,2},{1,3},{2,0},{3,1},{4,6},{5,7},{6,4},{7,5},{8,10},{9,11},{10,... | collective-permute-start | bytes 3932168 | tf_op jit(solution)/shard_map/ppermute | solution.py:133
  528.7 54.4 %collective-permute-start.27 = (bf16[640,2048]{1,0:T(8,128)(2,1)}, bf16[640,2048]{1,0:T(8,128)(2,1)}, u32[]{:S(2)}, u32[]{:S(2)}) collective-permute-start(bf16[640,2048]{1,0:T(8,128)(2,1)} %slice.910), channel_id=1, source_target_pairs={{0,1},{1,0},{2,3},{3,2},{4,5},{5,4},{6,7},{7,6},{8,9},{9,8},{10,11... | collective-permute-start | bytes 7864328 | tf_op jit(solution)/shard_map/ppermute | solution.py:133
  598.7 188.1 %collective-permute-start.39 = (bf16[4,384,256]{2,1,0:T(8,128)(2,1)}, bf16[4,384,256]{2,1,0:T(8,128)(2,1)}, u32[]{:S(2)}, u32[]{:S(2)}) collective-permute-start(bf16[4,384,256]{2,1,0:T(8,128)(2,1)} %pad_maximum_fusion.36), channel_id=1, source_target_pairs={{0,4},{1,5},{2,6},{3,7},{4,0},{5,1},{6,2},{7,3},{8,12},{9,13},{10,... | collective-permute-start | bytes 2359304 | tf_op jit(solution)/shard_map/ppermute | solution.py:133
  626.1 52.2 %collective-permute-start.35 = (bf16[640,2048]{1,0:T(8,128)(2,1)S(1)}, bf16[640,2048]{1,0:T(8,128)(2,1)S(1)}, u32[]{:S(2)}, u32[]{:S(2)}) collective-permute-start(bf16[640,2048]{1,0:T(8,128)(2,1)S(1)} %bitcast.684), channel_id=1, source_target_pairs={{0,1},{1,0},{2,3},{3,2},{4,5},{5,4},{6,7},{7,6},{8,9},{9,8},{10,11... | collective-permute-start | bytes 7864328 | tf_op jit(solution)/shard_map/ppermute | solution.py:133
  629.7 48.6 %collective-permute-start.36 = (bf16[4,128,1024]{2,1,0:T(8,128)(2,1)S(1)}, bf16[4,128,1024]{2,1,0:T(8,128)(2,1)S(1)}, u32[]{:S(2)}, u32[]{:S(2)}) collective-permute-start(bf16[4,128,1024]{2,1,0:T(8,128)(2,1)S(1)} %dynamic-slice_bitcast_fusion.8), channel_id=1, source_target_pairs={{0,2},{1,3},{2,0},{3,1},{4,6},{5,7},{6,4},{7,5},{8,10},{9,11},{10,... | collective-permute-start | bytes 3145736 | tf_op jit(solution)/shard_map/ppermute | solution.py:133
  636.5 95.2 %collective-permute-start.34 = (bf16[320,2048]{1,0:T(8,128)(2,1)}, bf16[320,2048]{1,0:T(8,128)(2,1)}, u32[]{:S(2)}, u32[]{:S(2)}) collective-permute-start(bf16[320,2048]{1,0:T(8,128)(2,1)} %slice.1160), channel_id=1, source_target_pairs={{0,2},{1,3},{2,0},{3,1},{4,6},{5,7},{6,4},{7,5},{8,10},{9,11},{10,... | collective-permute-start | bytes 3932168 | tf_op jit(solution)/shard_map/ppermute | solution.py:133
  683.6 48.0 %all-to-all-start.8 = ((bf16[4,64,2048]{2,1,0:T(8,128)(2,1)}), bf16[4,64,2048]{2,1,0:T(8,128)(2,1)}, u32[]{:S(2)}, u32[]{:S(2)}) async-start(bf16[4,64,2048]{2,1,0:T(8,128)(2,1)} %pad_maximum_fusion.33), calls=%async_computation.8 | async-start | bytes 2097152 | tf_op jit(solution)/shard_map/all_to_all | solution.py:136
  735.9 64.5 %all-to-all-start.13 = ((bf16[4,160,2048]{2,1,0:T(8,128)(2,1)}), bf16[4,160,2048]{2,1,0:T(8,128)(2,1)}, u32[]{:S(2)}, u32[]{:S(2)}) async-start(bf16[4,160,2048]{2,1,0:T(8,128)(2,1)} %bitcast.687), calls=%async_computation.13 | async-start | bytes 5242880 | tf_op jit(solution)/shard_map/all_to_all | solution.py:136
  741.1 45.6 %collective-permute-start.40 = (bf16[4,1024,256]{2,1,0:T(8,128)(2,1)}, bf16[4,1024,256]{2,1,0:T(8,128)(2,1)}, u32[]{:S(2)}, u32[]{:S(2)}) collective-permute-start(bf16[4,1024,256]{2,1,0:T(8,128)(2,1)} %pad_maximum_fusion.23), channel_id=1, source_target_pairs={{0,4},{1,5},{2,6},{3,7},{4,0},{5,1},{6,2},{7,3},{8,12},{9,13},{10,... | collective-permute-start | bytes 6291464 | tf_op jit(solution)/shard_map/ppermute | solution.py:133
  800.4 71.2 %all-to-all-start.12 = ((bf16[4,1408,256]{2,1,0:T(8,128)(2,1)}), bf16[4,1408,256]{2,1,0:T(8,128)(2,1)}, u32[]{:S(2)}, u32[]{:S(2)}) async-start(bf16[4,1408,256]{2,1,0:T(8,128)(2,1)} %pad_maximum_fusion.10), calls=%async_computation.12 | async-start | bytes 5767168 | tf_op jit(solution)/shard_map/all_to_all | solution.py:136
  833.0 47.5 %collective-permute-start.43 = (bf16[320,2048]{1,0:T(8,128)(2,1)}, bf16[320,2048]{1,0:T(8,128)(2,1)}, u32[]{:S(2)}, u32[]{:S(2)}) collective-permute-start(bf16[320,2048]{1,0:T(8,128)(2,1)} %slice.1176), channel_id=1, source_target_pairs={{0,2},{1,3},{2,0},{3,1},{4,6},{5,7},{6,4},{7,5},{8,10},{9,11},{10,... | collective-permute-start | bytes 3932168 | tf_op jit(solution)/shard_map/ppermute | solution.py:133
  836.2 47.8 %collective-permute-start.44 = (bf16[4,256,1024]{2,1,0:T(8,128)(2,1)}, bf16[4,256,1024]{2,1,0:T(8,128)(2,1)}, u32[]{:S(2)}, u32[]{:S(2)}) collective-permute-start(bf16[4,256,1024]{2,1,0:T(8,128)(2,1)} %dynamic-slice_bitcast_fusion.2), channel_id=1, source_target_pairs={{0,4},{1,5},{2,6},{3,7},{4,0},{5,1},{6,2},{7,3},{8,12},{9,13},{10,... | collective-permute-start | bytes 6291464 | tf_op jit(solution)/shard_map/ppermute | solution.py:133
  910.0 64.1 %all-to-all-start.9 = ((bf16[4,160,2048]{2,1,0:T(8,128)(2,1)}), bf16[4,160,2048]{2,1,0:T(8,128)(2,1)}, u32[]{:S(2)}, u32[]{:S(2)}) async-start(bf16[4,160,2048]{2,1,0:T(8,128)(2,1)} %bitcast.127), calls=%async_computation.9 | async-start | bytes 5242880 | tf_op jit(solution)/shard_map/all_to_all | solution.py:136
  919.8 74.8 %collective-permute-start.45 = (bf16[4,256,1024]{2,1,0:T(8,128)(2,1)}, bf16[4,256,1024]{2,1,0:T(8,128)(2,1)}, u32[]{:S(2)}, u32[]{:S(2)}) collective-permute-start(bf16[4,256,1024]{2,1,0:T(8,128)(2,1)} %dynamic-slice_bitcast_fusion.1), channel_id=1, source_target_pairs={{0,4},{1,5},{2,6},{3,7},{4,0},{5,1},{6,2},{7,3},{8,12},{9,13},{10,... | collective-permute-start | bytes 6291464 | tf_op jit(solution)/shard_map/ppermute | solution.py:133
  974.1 73.0 %all-to-all-start.10 = ((bf16[4,256,1024]{2,1,0:T(8,128)(2,1)}), bf16[4,256,1024]{2,1,0:T(8,128)(2,1)}, u32[]{:S(2)}, u32[]{:S(2)}) async-start(bf16[4,256,1024]{2,1,0:T(8,128)(2,1)} %fusion.26), calls=%async_computation.10 | async-start | bytes 4194304 | tf_op jit(solution)/shard_map/all_to_all | solution.py:136
  1008.1 57.5 %collective-permute-start.56 = (bf16[4,2,64,1024]{3,2,0,1:T(8,128)(2,1)}, bf16[4,2,64,1024]{3,2,0,1:T(8,128)(2,1)}, u32[]{:S(2)}, u32[]{:S(2)}) collective-permute-start(bf16[4,2,64,1024]{3,2,0,1:T(8,128)(2,1)} %dynamic-slice_bitcast_fusion.7), channel_id=1, source_target_pairs={{0,2},{1,3},{2,0},{3,1},{4,6},{5,7},{6,4},{7,5},{8,10},{9,11},{10,... | collective-permute-start | bytes 3145736 | tf_op jit(solution)/shard_map/ppermute | solution.py:133
  1012.1 62.4 %collective-permute-start.57 = (bf16[4,2,64,1024]{3,2,0,1:T(8,128)(2,1)}, bf16[4,2,64,1024]{3,2,0,1:T(8,128)(2,1)}, u32[]{:S(2)}, u32[]{:S(2)}) collective-permute-start(bf16[4,2,64,1024]{3,2,0,1:T(8,128)(2,1)} %dynamic-slice_bitcast_fusion.6), channel_id=1, source_target_pairs={{0,2},{1,3},{2,0},{3,1},{4,6},{5,7},{6,4},{7,5},{8,10},{9,11},{10,... | collective-permute-start | bytes 3145736 | tf_op jit(solution)/shard_map/ppermute | solution.py:133
  1039.3 48.7 %collective-permute-start.55 = (bf16[4,2,64,2048]{3,2,0,1:T(8,128)(2,1)}, bf16[4,2,64,2048]{3,2,0,1:T(8,128)(2,1)}, u32[]{:S(2)}, u32[]{:S(2)}) collective-permute-start(bf16[4,2,64,2048]{3,2,0,1:T(8,128)(2,1)} %dynamic-slice_bitcast_fusion), channel_id=1, source_target_pairs={{0,4},{1,5},{2,6},{3,7},{4,0},{5,1},{6,2},{7,3},{8,12},{9,13},{10,... | collective-permute-start | bytes 6291464 | tf_op jit(solution)/shard_map/ppermute | solution.py:133
  1045.7 74.1 %collective-permute-start.60 = (bf16[4,32,1792]{2,1,0:T(8,128)(2,1)}, bf16[4,32,1792]{2,1,0:T(8,128)(2,1)}, u32[]{:S(2)}, u32[]{:S(2)}) collective-permute-start(bf16[4,32,1792]{2,1,0:T(8,128)(2,1)} %dynamic-slice_bitcast_fusion.16), channel_id=1, source_target_pairs={{0,2},{1,3},{2,0},{3,1},{4,6},{5,7},{6,4},{7,5},{8,10},{9,11},{10,... | collective-permute-start | bytes 1376264 | tf_op jit(solution)/shard_map/ppermute | solution.py:133
  1047.2 92.0 %all-to-all-start.11 = ((bf16[4,256,1024]{2,1,0:T(8,128)(2,1)}), bf16[4,256,1024]{2,1,0:T(8,128)(2,1)}, u32[]{:S(2)}, u32[]{:S(2)}) async-start(bf16[4,256,1024]{2,1,0:T(8,128)(2,1)} %fusion.25), calls=%async_computation.11 | async-start | bytes 4194304 | tf_op jit(solution)/shard_map/all_to_all | solution.py:136
  1065.6 54.2 %collective-permute-start.61 = (bf16[4,32,1920]{2,1,0:T(8,128)(2,1)}, bf16[4,32,1920]{2,1,0:T(8,128)(2,1)}, u32[]{:S(2)}, u32[]{:S(2)}) collective-permute-start(bf16[4,32,1920]{2,1,0:T(8,128)(2,1)} %dynamic-slice_bitcast_fusion.15), channel_id=1, source_target_pairs={{0,4},{1,5},{2,6},{3,7},{4,0},{5,1},{6,2},{7,3},{8,12},{9,13},{10,... | collective-permute-start | bytes 1474568 | tf_op jit(solution)/shard_map/ppermute | solution.py:133
  1139.9 74.8 %all-to-all-start.14 = ((bf16[4,64,5952]{2,1,0:T(8,128)(2,1)}), bf16[4,64,5952]{2,1,0:T(8,128)(2,1)S(1)}, u32[]{:S(2)}, u32[]{:S(2)}) async-start(bf16[4,64,5952]{2,1,0:T(8,128)(2,1)} %fusion.40), calls=%async_computation.14 | async-start | bytes 6160384 | tf_op jit(solution)/shard_map/all_to_all | solution.py:136
  (330 other events, 4002.2 us)
Sparse Core Ops, SparseCore 0:
  116.9 67.9 all-gather.2
  484.3 49.8 all-gather.4

commit v4 on v3

--- a/solution.py
+++ b/solution.py
@@ -135,8 +135,11 @@
     def z_swap(parts):
         return lax.all_to_all(parts, AXES, 0, 0, axis_index_groups=lines_z)
 
+    def copies(own):
+        return jnp.broadcast_to(own[None], (m,) + own.shape)
+
     def z_gather(own):
-        return z_swap(jnp.broadcast_to(own[None], (m,) + own.shape))
+        return z_swap(copies(own))
 
     def in_order(bit, mine, other, axis):
         return jnp.where(bit == 0, jnp.stack([mine, other], axis), jnp.stack([other, mine], axis))
@@ -382,19 +385,21 @@
         up_own = jnp.stack([up_pre[:, t * cols : (t + 1) * cols] for t in range(m)])
 
         first_z = z_gather(first)
-        first_z, second = sync(first_z, second)
+        first_z, second_m = sync(first_z, copies(second))
         first_z = with_highs(first_z, place)
         one_a, one_b = first_z[:, :, :half], first_z[:, :, half:]
         got_a, got_b = send(one_a, swap_y), send(one_b, swap_x)
-        second_z = z_gather(second)
-        got_a, got_b, third, cot_act_own = sync(got_a, got_b, third, pad_rows(grad_act[0, 0], rows_act))
+        second_z = z_swap(second_m)
+        got_a, got_b, third_m, cot_act_own = sync(
+            got_a, got_b, copies(third), pad_rows(grad_act[0, 0], rows_act)
+        )
         cot_all_act = gather_act(cot_act_own)
         one_a, one_b = in_order(y, one_a, got_a, 1), in_order(x, one_b, got_b, 1)
         got_a, got_b = send(one_a, swap_x), send(one_b, swap_y)
-        got_a, got_b, third, second_z = sync(got_a, got_b, third, second_z)
+        got_a, got_b, third_m, second_z = sync(got_a, got_b, third_m, second_z)
         one_a, one_b = in_order(x, one_a, got_a, 1), in_order(y, one_b, got_b, 2)
         got_a, got_b = send(one_a, swap_c), send(one_b, swap_c)
-        third_z = z_gather(third)
+        third_z = z_swap(third_m)
         second_z = with_highs(second_z, place)
         two_a, two_b = second_z[:, :, :width], second_z[:, :, width:]
         side_a, side_b = send(two_a, swap_y), send(two_b, swap_x)
@@ -417,8 +422,8 @@
         kv_own, side_a, side_b, third_z, down_own = sync(kv_own, side_a, side_b, third_z, down_own)
         down_z = z_swap(down_own)
         two_a, two_b = in_order(y, two_a, side_a, 1), in_order(x, two_b, side_b, 1)
+        kv_y, two_a, two_b = sync(send(kv_own, swap_y), two_a, two_b)
         side_a, side_b = send(two_a, swap_x), send(two_b, swap_y)
-        kv_y = send(kv_own, swap_y)
         kv_c = send(jnp.stack([kv_own, kv_y]), swap_c)
         (kv_c,) = sync(kv_c)
         queries_pre = qkv_pre[:, :width].reshape(rows_pre, HEADS, HD)
@@ -465,13 +470,14 @@
             normed_two_pre, cot_own, third_z, down_far_a, down_z_b
         )
         down_far_b = send(down_z_b, swap_x)
-        gate_z, up_own, down_far_b = sync(gate_z, up_own, down_far_b)
+        gate_z, up_own = sync(gate_z, up_own)
         up_z = z_swap(up_own)
+        down_far_b, gate_z = sync(down_far_b, gate_z)
         gate_far = send(gate_z, swap_x)
         third_z = with_highs(third_z, place)
         three_a, three_b = third_z[:, :, :third_half], third_z[:, :, third_half:]
         third_a, third_b = send(three_a, swap_y), send(three_b, swap_x)
-        up_z, down_far_b, third_a, third_b = sync(up_z, down_far_b, third_a, third_b)
+        up_z, third_a, third_b = sync(up_z, third_a, third_b)
         row_z = z_gather(normed_two_pre)
         three_a, three_b = in_order(y, three_a, third_a, 1), in_order(x, three_b, third_b, 1)
         third_a, third_b = send(three_a, swap_x), send(three_b, swap_y)
@@ -506,10 +512,10 @@
         side_input = pad_rows(jnp.concatenate([state_row, action_rows], axis=0), rows_act)
         normed_act = rms_norm(side_input, norm_attn_act).astype(BF16)
         qkv_act = mm(normed_act, qkv_act_w).astype(BF16)
-        row_z, qkv_act, gate_full, cot_own, down_full = sync(
-            row_z, qkv_act, gate_full, cot_own, down_full
-        )
-        cot_z = z_gather(cot_own)
+        row_z, qkv_act, gate_full, cot_m, down_full = sync(
+            row_z, qkv_act, gate_full, copies(cot_own), down_full
+        )
+        cot_z = z_swap(cot_m)
         row_got = send(row_z[:two], swap_y)
         narrow = down_full[:cols]
         wide_act, narrow_act = act_weights(down_full, cols, cols_act, w_act)
@@ -611,14 +617,12 @@
         out_odd = add_low(part_o[:four_rows], odd_got)
         odd_got = send(out_odd[two_rows:], swap_y)
         d_hidden_e = mm_tr(cot_e, narrow)
-        far_o, d_hidden_e, act_got, even_got = sync(far_o, d_hidden_e, act_got, even_got)
-        act_mine = add_low(act_mine, act_got)
-        act_z = z_swap(jnp.concatenate([act_mine[:, :rows_act], act_mine[:, rows_act:]], axis=2))
+        far_o, d_hidden_e, even_got = sync(far_o, d_hidden_e, even_got)
         cot_o = jnp.concatenate([near_o, far_o])
         grad_down = outer_sums([unit_e[2], unit_o[2]], [cot_e, cot_o])
         down_mine, down_theirs = split_columns(grad_down, place)
         d_hidden_o = mm_tr(cot_o, narrow)
-        odd_got, down_theirs, d_hidden_o, act_z = sync(odd_got, down_theirs, d_hidden_o, act_z)
+        odd_got, down_theirs, d_hidden_o = sync(odd_got, down_theirs, d_hidden_o)
         out_even = add_low(out_even[:two_rows], even_got)
         out_odd = add_low(out_odd[:two_rows], odd_got)
         out_z = z_swap(jnp.concatenate([out_even, out_odd]).reshape(m, rows_pre, width))
@@ -627,16 +631,22 @@
         (back_o_rows,) = sync(back_o[0])
         odd_got = send(back_o_rows[four_rows:], swap_c)
         back_e = ffn_back(d_hidden_e, unit_e[0], unit_e[1], wide)
-        odd_got, back_e_rows, row_e, row_o, small_got, down_got = sync(
-            odd_got, back_e[0], row_e, row_o, small_got, down_got
+        act_mine = add_low(act_mine, act_got)
+        act_mine = jnp.concatenate([act_mine[:, :rows_act], act_mine[:, rows_act:]], axis=2)
+        odd_got, back_e_rows, row_e, row_o, small_got, down_got, act_mine, out_z = sync(
+            odd_got, back_e[0], row_e, row_o, small_got, down_got, act_mine, out_z
         )
         d_odd = add_low(back_o_rows[:four_rows], odd_got)
         odd_got = send(d_odd[two_rows:], swap_y)
         even_got = send(back_e_rows[four_rows:], swap_c)
         down_both = [add_low(down_mine, down_got), add_low(small_mine, small_got)]
-        down_z = z_swap(jnp.concatenate(down_both, axis=1))
+        down_sums = jnp.concatenate(down_both, axis=1)
+        act_z = z_swap(act_mine)
         grad_gate = outer_sums([row_e, row_o], [back_e[1], back_o[1]])
-        odd_got, even_got, grad_gate, row_e, row_o = sync(odd_got, even_got, grad_gate, row_e, row_o)
+        odd_got, even_got, grad_gate, row_e, row_o, down_sums, act_z = sync(
+            odd_got, even_got, grad_gate, row_e, row_o, down_sums, act_z
+        )
+        down_z = z_swap(down_sums)
         d_odd = add_low(d_odd[:two_rows], odd_got)
         d_even = add_low(back_e_rows[:four_rows], even_got)
         even_got = send(d_even[two_rows:], swap_y)
@@ -707,8 +717,8 @@
 
         twos = [grads_out_act, grads_mix_first]
         theirs_twos = [of_core(1 - c, pair) for pair in twos]
-        (d_z, theirs_a, theirs_b), theirs_twos, *twos = together(
-            [[d_z, theirs_a, theirs_b], theirs_twos] + twos
+        (d_z, theirs_a, theirs_b, up_got), theirs_twos, *twos = together(
+            [[d_z, theirs_a, theirs_b, up_got], theirs_twos] + twos
         )
         gate_z = z_swap(add_low(gate_mine, gate_got))
         got_a, got_b = send(theirs_a, swap_c), send(theirs_b, swap_c)
@@ -721,8 +731,8 @@
         d_attn_pre = heads_of(d_mid_low, out_parts)
         theirs_out = of_core(1 - c, grads_out_pre)
         small_z = down_z[:, cols:]
-        (d_attn_pre, up_got, got_a, got_b, theirs_out), two_got, grads_out_pre, *twos = together(
-            [[d_attn_pre, up_got, got_a, got_b, theirs_out], two_got, grads_out_pre] + twos
+        (d_attn_pre, got_a, got_b, theirs_out), two_got, grads_out_pre, *twos = together(
+            [[d_attn_pre, got_a, got_b, theirs_out], two_got, grads_out_pre] + twos
         )
         out_got = send(theirs_out, swap_c)
         halves = [
@@ -735,16 +745,12 @@
         got_a, got_b = send(theirs_a, swap_x), send(theirs_b, swap_y)
         probs_pre = jnp.exp(prefix_scores() - total_pre)
         d_probs = ein("qhd,kd->hqk", d_attn_pre, values)
-        d_probs, probs_pre, out_got, got_a, got_b = sync(d_probs, probs_pre, out_got, got_a, got_b)
+        d_probs, probs_pre, out_got = sync(d_probs, probs_pre, out_got)
         out_half = split_bit(add_low(of_core(c, grads_out_pre), out_got), x, 1)
         out_got = send(out_half[1], swap_x)
         d_scores = probs_pre * (d_probs - jnp.sum(probs_pre * d_probs, axis=-1, keepdims=True))
         d_scores = d_scores.astype(BF16)
         (d_scores,) = sync(d_scores)
-        share_a, share_b = add_low(mine_a, got_a), add_low(mine_b, got_b)
-        mine_a, theirs_a = split_bit(share_a, y, 1)
-        mine_b, theirs_b = split_bit(share_b, x, 1)
-        got_a, got_b = send(theirs_a, swap_y), send(theirs_b, swap_x)
         key_terms = ein("hqk,qhd->kd", d_scores, queries_pre) + ein("hqk,qhd->kd", far, queries_act)
         value_terms = ein("hqk,qhd->kd", probs_pre.astype(BF16), d_attn_pre)
         value_terms = value_terms + ein("hqk,qhd->kd", probs_act_low[..., :key_count], d_attn_act)
@@ -753,7 +759,13 @@
         kv_got = send(kv_terms[2:], swap_c)
         d_query_pre = (ein("hqk,kd->qhd", d_scores, keys) * scale).reshape(rows_pre, width).astype(BF16)
         up_swapped = add_low(up_mine, up_got)
-        kv_got, d_query_pre, gate_z, up_swapped = sync(kv_got, d_query_pre, gate_z, up_swapped)
+        kv_got, d_query_pre, gate_z, up_swapped, got_a, got_b = sync(
+            kv_got, d_query_pre, gate_z, up_swapped, got_a, got_b
+        )
+        share_a, share_b = add_low(mine_a, got_a), add_low(mine_b, got_b)
+        mine_a, theirs_a = split_bit(share_a, y, 1)
+        mine_b, theirs_b = split_bit(share_b, x, 1)
+        got_a, got_b = send(theirs_a, swap_y), send(theirs_b, swap_x)
         up_z = z_swap(up_swapped)
         kv_pair = add_low(kv_terms[:2], kv_got)
         kv_got = send(kv_pair[1], swap_y)

time: 1280 us -> 1270 us (level)
  other arithmetic: 296 us -> 283 us
    all_to_all x16, waiting for transfers between devices: 132 us -> 117 us  [z_swap(): return lax.all_to_all(parts, AXES, 0, 0, axis_index_groups=lines_z)]
    select_n x28 -> x26, other arithmetic: 60.5 us -> 57.1 us  [in_order(): jnp.where(bit == 0, jnp.stack([mine, other], axis), jnp.stack([other, min...]
    unnamed x603 -> x589, local copies, waits for them, and re-layouts: 53.2 us -> 51.5 us
  transfers between devices with their start and end apart: 87 -> 87, of which waited for: 37 -> 36; matrix products, arithmetic and copies ran while one was open for 46% -> 47% of each run, Pallas kernels for 3% -> 4%
where the time goes in v4:
time: 1270 us; the launch traced here: 1260 us
  waiting for transfers between devices  408 us (32%)
  other arithmetic  283 us (22%)
  matrix products  201 us (16%)
  local copies, waits for them, and re-layouts  171 us (13%)
  starting transfers between devices  130 us (10%)
  Pallas kernels  45 us (4%)
  between operations  20.4 us (2%)
    ppermute x69, waiting for transfers between devices, send(): return lax.ppermute(array, AXES, pairs)  282 us
    all_to_all x16, waiting for transfers between devices, z_swap(): return lax.all_to_all(parts, AXES, 0, 0, axis_index_groups=lines_z)  117 us
    dot_general x24, matrix products, mm_tr(): lax.dot_general(left, right, (((1,), (1,)), ((), ())), preferred_element_...  83.7 us
    dot_general x22, matrix products, mm(): return jnp.dot(left, right, preferred_element_type=F32)  81.9 us
    all_to_all x16, starting transfers between devices, z_swap(): return lax.all_to_all(parts, AXES, 0, 0, axis_index_groups=lines_z)  77.8 us
    convert_element_type x36, other arithmetic, add_low(): return (left.astype(F32) + right.astype(F32)).astype(BF16)  70.5 us
    select_n x26, other arithmetic, in_order(): jnp.where(bit == 0, jnp.stack([mine, other], axis), jnp.stack([other, min...  57.1 us
    ppermute x69, starting transfers between devices, send(): return lax.ppermute(array, AXES, pairs)  52.2 us
  transfers between devices with their start and end apart: 87, of which 36 were waited for; matrix products, arithmetic and copies ran while one was open for 47% of the time, Pallas kernels for 4%

profile of v4, /device:TPU:0, one launch (start us, length us, event | category | flops | bytes accessed | tf_op | source)
XLA Modules:
  0.0 1257.5 jit_solution(14808773863342485526)
XLA Ops:
  24.3 26.0 %all-to-all-done = bf16[4,64,2688]{2,1,0:T(8,128)(2,1)S(1)} async-done(((bf16[4,64,2688]{2,1,0:T(8,128)(2,1)}), bf16[4,64,2688]{2,1,0:T(8,128)(2,1)S(1)}, u32[]{:S(2)}, u32[]{:S(2)}) %all-to-all-start) | async-done | bytes 1376288 | tf_op jit(solution)/shard_map/all_to_all | solution.py:136
  67.3 9.0 collective-permute-done
  84.5 24.8 %collective-permute-done.2 = bf16[4,2,64,1280]{3,2,0,1:T(8,128)(2,1)} collective-permute-done((bf16[4,2,64,1280]{3,2,0,1:T(8,128)(2,1)S(1)}, bf16[4,2,64,1280]{3,2,0,1:T(8,128)(2,1)}, u32[]{:S(2)}, u32[]{:S(2)}) %collective-permute-start.2) | collective-permute-done | bytes 1310752 | tf_op jit(solution)/shard_map/ppermute | solution.py:133
  185.1 27.2 %collective-permute-done.10 = bf16[4,2,64,2048]{3,2,1,0:T(8,128)(2,1)} collective-permute-done((bf16[4,2,64,2048]{3,2,1,0:T(8,128)(2,1)}, bf16[4,2,64,2048]{3,2,1,0:T(8,128)(2,1)}, u32[]{:S(2)}, u32[]{:S(2)}) %collective-permute-start.10) | collective-permute-done | bytes 2097184 | tf_op jit(solution)/shard_map/ppermute | solution.py:133
  270.9 11.0 collective-permute-done.14
  305.1 25.2 %collective-permute-done.19 = bf16[2,1408,256]{2,1,0:T(8,128)(2,1)} collective-permute-done((bf16[2,1408,256]{2,1,0:T(8,128)(2,1)}, bf16[2,1408,256]{2,1,0:T(8,128)(2,1)}, u32[]{:S(2)}, u32[]{:S(2)}) %collective-permute-start.19) | collective-permute-done | bytes 1441824 | tf_op jit(solution)/shard_map/ppermute | solution.py:133
  337.6 10.5 all-to-all-done.6
  363.4 15.7 %collective-permute-done.20 = bf16[4,256,1024]{2,1,0:T(8,128)(2,1)} collective-permute-done((bf16[4,256,1024]{2,1,0:T(8,128)(2,1)}, bf16[4,256,1024]{2,1,0:T(8,128)(2,1)}, u32[]{:S(2)}, u32[]{:S(2)}) %collective-permute-start.20) | collective-permute-done | bytes 2097184 | tf_op jit(solution)/shard_map/ppermute | solution.py:133
  385.2 10.2 collective-permute-done.17
  446.7 16.2 %collective-permute-done.23 = bf16[2,160,2048]{2,1,0:T(8,128)(2,1)S(1)} collective-permute-done((bf16[2,160,2048]{2,1,0:T(8,128)(2,1)S(1)}, bf16[2,160,2048]{2,1,0:T(8,128)(2,1)S(1)}, u32[]{:S(2)}, u32[]{:S(2)}) %collective-permute-start.23) | collective-permute-done | bytes 1310752 | tf_op jit(solution)/shard_map/ppermute | solution.py:133
  487.1 8.9 fusion.268
  496.0 13.5 %multiply_convert_fusion.3 = (bf16[1280,1024]{1,0:T(8,128)(2,1)S(1)}, f32[1280,1024]{1,0:T(8,128)}) fusion(f32[1280,1024]{1,0:T(8,128)S(1)} %fusion.268, bf16[2048,1024]{1,0:T(8,128)(2,1)S(1)} %bitcast.733, bf16[640,2048]{1,0:T(8,128)(2,1)} %collective-permute-done.26, bf16[640,2048]{1,0:T(8,128)(2,1)} %bitcast.676), kind=kOutput, calls=%fused_computation.53 | convolution fusion | flops 5392302080 | bytes 22544384 | tf_op jit(solution)/shard_map/dot_general | solution.py:42
  549.2 8.2 fusion.266
  557.4 13.5 %multiply_convert_fusion.2 = (bf16[1280,1024]{1,0:T(8,128)(2,1)S(1)}, f32[1280,1024]{1,0:T(8,128)}) fusion(f32[1280,1024]{1,0:T(8,128)S(1)} %fusion.266, bf16[2048,1024]{1,0:T(8,128)(2,1)S(1)} %bitcast.735, bf16[640,2048]{1,0:T(8,128)(2,1)} %collective-permute-done.29, bf16[640,2048]{1,0:T(8,128)(2,1)} %bitcast.106), kind=kOutput, calls=%fused_computation.52 | convolution fusion | flops 5392302080 | bytes 22544384 | tf_op jit(solution)/shard_map/dot_general | solution.py:42
  603.2 14.6 %collective-permute-done.31 = bf16[2,160,2048]{2,1,0:T(8,128)(2,1)S(1)} collective-permute-done((bf16[2,160,2048]{2,1,0:T(8,128)(2,1)}, bf16[2,160,2048]{2,1,0:T(8,128)(2,1)S(1)}, u32[]{:S(2)}, u32[]{:S(2)}) %collective-permute-start.31) | collective-permute-done | bytes 1310752 | tf_op jit(solution)/shard_map/ppermute | solution.py:133
  629.8 10.0 fusion.44
  645.5 26.7 %collective-permute-done.40 = bf16[4,128,1024]{2,1,0:T(8,128)(2,1)S(1)} collective-permute-done((bf16[4,128,1024]{2,1,0:T(8,128)(2,1)S(1)}, bf16[4,128,1024]{2,1,0:T(8,128)(2,1)S(1)}, u32[]{:S(2)}, u32[]{:S(2)}) %collective-permute-start.40) | collective-permute-done | bytes 1048608 | tf_op jit(solution)/shard_map/ppermute | solution.py:133
  678.2 16.5 %shard_map.485 = bf16[1024,2048]{1,0:T(8,128)(2,1)S(1)} custom-call(bf16[1280,1024]{1,0:T(8,128)(2,1)S(1)} %get-tuple-element.658.refs_0_, bf16[1280,1024]{1,0:T(8,128)(2,1)S(1)} %copy-done.12, bf16[1280,2048]{1,0:T(8,128)(2,1)} %pad_maximum_fusion.3.refs_2_, bf16[1280,2048]{1,0:T(8,128)(2,1)} %pad_maximum_fusion.4.refs_3_), custom_call_target="tpu_custom_call" | custom-call | flops 10737418240 | bytes 19922944 | tf_op jit(solution)/shard_map/pallas_call | solution.py:97
  697.5 9.0 fusion.42
  732.1 11.3 add_convert_fusion.1
  752.9 8.3 fusion.297
  761.2 9.9 add_convert_fusion
  798.5 14.0 %shard_map.486 = bf16[2048,1024]{1,0:T(8,128)(2,1)S(1)} custom-call(bf16[1280,2048]{1,0:T(8,128)(2,1)} %pad_maximum_fusion.1.refs_0_, bf16[1280,2048]{1,0:T(8,128)(2,1)} %pad_maximum_fusion.2.refs_1_, bf16[1280,1024]{1,0:T(8,128)(2,1)S(1)} %copy-done.10, bf16[1280,1024]{1,0:T(8,128)(2,1)S(1)} %copy-done.8), custom_call_target="tpu_custom_call" | custom-call | flops 10737418240 | bytes 19922944 | tf_op jit(solution)/shard_map/pallas_call | solution.py:97
  830.9 14.5 %shard_map.487 = bf16[2048,1024]{1,0:T(8,128)(2,1)S(1)} custom-call(bf16[1280,2048]{1,0:T(8,128)(2,1)} %pad_maximum_fusion.1.refs_0_, bf16[1280,2048]{1,0:T(8,128)(2,1)} %pad_maximum_fusion.2.refs_1_, bf16[1280,1024]{1,0:T(8,128)(2,1)S(1)} %copy-done.6, bf16[1280,1024]{1,0:T(8,128)(2,1)S(1)} %get-tuple-element.481.refs_3_), custom_call_target="tpu_custom_call" | custom-call | flops 10737418240 | bytes 19922944 | tf_op jit(solution)/shard_map/pallas_call | solution.py:97
  845.5 11.6 collective-permute-done.43
  857.1 12.0 collective-permute-done.44
  935.6 36.2 %all-to-all-done.10 = bf16[4,160,2048]{2,1,0:T(8,128)(2,1)} async-done(((bf16[4,160,2048]{2,1,0:T(8,128)(2,1)}), bf16[4,160,2048]{2,1,0:T(8,128)(2,1)}, u32[]{:S(2)}, u32[]{:S(2)}) %all-to-all-start.10) | async-done | bytes 2621472 | tf_op jit(solution)/shard_map/all_to_all | solution.py:136
  1056.9 17.9 %collective-permute-done.57 = bf16[4,2,64,1024]{3,2,0,1:T(8,128)(2,1)} collective-permute-done((bf16[4,2,64,1024]{3,2,0,1:T(8,128)(2,1)}, bf16[4,2,64,1024]{3,2,0,1:T(8,128)(2,1)}, u32[]{:S(2)}, u32[]{:S(2)}) %collective-permute-start.57) | collective-permute-done | bytes 1048608 | tf_op jit(solution)/shard_map/ppermute | solution.py:133
  1110.3 9.1 collective-permute-done.59
  1151.6 22.5 %collective-permute-done.65 = bf16[4,2,64,1280]{3,2,0,1:T(8,128)(2,1)S(1)} collective-permute-done((bf16[4,2,64,1280]{3,2,0,1:T(8,128)(2,1)S(1)}, bf16[4,2,64,1280]{3,2,0,1:T(8,128)(2,1)S(1)}, u32[]{:S(2)}, u32[]{:S(2)}) %collective-permute-start.65) | collective-permute-done | bytes 1310752 | tf_op jit(solution)/shard_map/ppermute | solution.py:133
  1194.2 11.1 all-to-all-done.14
  1218.8 27.4 %all-to-all-done.15 = bf16[4,64,2688]{2,1,0:T(8,128)(2,1)} async-done(((bf16[4,64,2688]{2,1,0:T(8,128)(2,1)}), bf16[4,64,2688]{2,1,0:T(8,128)(2,1)}, u32[]{:S(2)}, u32[]{:S(2)}) %all-to-all-start.15) | async-done | bytes 1376288 | tf_op jit(solution)/shard_map/all_to_all | solution.py:136
  (1126 shorter events, 734.6 us)
Async XLA Ops:
  51.8 58.8 %all-to-all-start.1 = ((bf16[4,64,4096]{2,1,0:T(8,128)(2,1)}), bf16[4,64,4096]{2,1,0:T(8,128)(2,1)}, u32[]{:S(2)}, u32[]{:S(2)}) async-start(bf16[4,64,4096]{2,1,0:T(8,128)(2,1)} %broadcast_in_dim.81), calls=%async_computation.1 | async-start | bytes 4194304 | tf_op jit(solution)/shard_map/all_to_all | solution.py:136
  56.3 128.8 %all-gather.3.cloned.1.call-start = ((), (), s32[]{:S(2)}) async-start(), calls=%async_computation.16 | async-start | bytes 2228224 | tf_op jit(solution)/shard_map/all_gather | solution.py:378
  152.7 89.9 %all-to-all-start.3 = ((bf16[4,1408,256]{2,1,0:T(8,128)(2,1)}), bf16[4,1408,256]{2,1,0:T(8,128)(2,1)S(1)}, u32[]{:S(2)}, u32[]{:S(2)}) async-start(bf16[4,1408,256]{2,1,0:T(8,128)(2,1)} %pad_maximum_fusion.9), calls=%async_computation.3 | async-start | bytes 5767168 | tf_op jit(solution)/shard_map/all_to_all | solution.py:136
  242.6 53.3 %all-to-all-start.5 = ((bf16[4,256,1024]{2,1,0:T(8,128)(2,1)}), bf16[4,256,1024]{2,1,0:T(8,128)(2,1)}, u32[]{:S(2)}, u32[]{:S(2)}) async-start(bf16[4,256,1024]{2,1,0:T(8,128)(2,1)} %pad_maximum_fusion.19), calls=%async_computation.5 | async-start | bytes 4194304 | tf_op jit(solution)/shard_map/all_to_all | solution.py:136
  284.3 71.5 %collective-permute-start.15 = (bf16[4,32,1792]{2,1,0:T(8,128)(2,1)}, bf16[4,32,1792]{2,1,0:T(8,128)(2,1)}, u32[]{:S(2)}, u32[]{:S(2)}) collective-permute-start(bf16[4,32,1792]{2,1,0:T(8,128)(2,1)} %get-tuple-element.614), channel_id=1, source_target_pairs={{0,2},{1,3},{2,0},{3,1},{4,6},{5,7},{6,4},{7,5},{8,10},{9,11},{10,... | collective-permute-start | bytes 1376264 | tf_op jit(solution)/shard_map/ppermute | solution.py:133
  287.3 68.5 %collective-permute-start.16 = (bf16[4,32,1920]{2,1,0:T(8,128)(2,1)}, bf16[4,32,1920]{2,1,0:T(8,128)(2,1)}, u32[]{:S(2)}, u32[]{:S(2)}) collective-permute-start(bf16[4,32,1920]{2,1,0:T(8,128)(2,1)} %get-tuple-element.617), channel_id=1, source_target_pairs={{0,4},{1,5},{2,6},{3,7},{4,0},{5,1},{6,2},{7,3},{8,12},{9,13},{10,... | collective-permute-start | bytes 1474568 | tf_op jit(solution)/shard_map/ppermute | solution.py:133
  295.9 52.2 %all-to-all-start.6 = ((bf16[4,256,1024]{2,1,0:T(8,128)(2,1)}), bf16[4,256,1024]{2,1,0:T(8,128)(2,1)}, u32[]{:S(2)}, u32[]{:S(2)}) async-start(bf16[4,256,1024]{2,1,0:T(8,128)(2,1)} %pad_maximum_fusion.20), calls=%async_computation.6 | async-start | bytes 4194304 | tf_op jit(solution)/shard_map/all_to_all | solution.py:136
  330.3 48.9 %collective-permute-start.20 = (bf16[4,256,1024]{2,1,0:T(8,128)(2,1)}, bf16[4,256,1024]{2,1,0:T(8,128)(2,1)}, u32[]{:S(2)}, u32[]{:S(2)}) collective-permute-start(bf16[4,256,1024]{2,1,0:T(8,128)(2,1)} %all-to-all-done.5), channel_id=1, source_target_pairs={{0,4},{1,5},{2,6},{3,7},{4,0},{5,1},{6,2},{7,3},{8,12},{9,13},{10,... | collective-permute-start | bytes 6291464 | tf_op jit(solution)/shard_map/ppermute | solution.py:133
  351.1 67.3 %all-to-all-start.4 = ((bf16[4,160,2048]{2,1,0:T(8,128)(2,1)}), bf16[4,160,2048]{2,1,0:T(8,128)(2,1)}, u32[]{:S(2)}, u32[]{:S(2)}) async-start(bf16[4,160,2048]{2,1,0:T(8,128)(2,1)} %broadcast_in_dim.147), calls=%async_computation.4 | async-start | bytes 5242880 | tf_op jit(solution)/shard_map/all_to_all | solution.py:136
  398.9 47.9 %collective-permute-start.24 = (bf16[4,256,1024]{2,1,0:T(8,128)(2,1)}, bf16[4,256,1024]{2,1,0:T(8,128)(2,1)}, u32[]{:S(2)}, u32[]{:S(2)}) collective-permute-start(bf16[4,256,1024]{2,1,0:T(8,128)(2,1)} %all-to-all-done.6), channel_id=1, source_target_pairs={{0,4},{1,5},{2,6},{3,7},{4,0},{5,1},{6,2},{7,3},{8,12},{9,13},{10,... | collective-permute-start | bytes 6291464 | tf_op jit(solution)/shard_map/ppermute | solution.py:133
  424.4 93.4 %all-to-all-start.7 = ((bf16[4,160,2048]{2,1,0:T(8,128)(2,1)}), bf16[4,160,2048]{2,1,0:T(8,128)(2,1)}, u32[]{:S(2)}, u32[]{:S(2)}) async-start(bf16[4,160,2048]{2,1,0:T(8,128)(2,1)} %broadcast_in_dim.149), calls=%async_computation.7 | async-start | bytes 5242880 | tf_op jit(solution)/shard_map/all_to_all | solution.py:136
  429.1 101.9 %all-gather.5.cloned.1.call-start = ((), (), s32[]{:S(2)}) async-start(), calls=%async_computation.17 | async-start | bytes 2228224 | tf_op jit(solution)/shard_map/all_gather | solution.py:378
  521.5 55.5 %collective-permute-start.28 = (bf16[2,160,2048]{2,1,0:T(8,128)(2,1)}, bf16[2,160,2048]{2,1,0:T(8,128)(2,1)}, u32[]{:S(2)}, u32[]{:S(2)}) collective-permute-start(bf16[2,160,2048]{2,1,0:T(8,128)(2,1)} %get-tuple-element.552), channel_id=1, source_target_pairs={{0,2},{1,3},{2,0},{3,1},{4,6},{5,7},{6,4},{7,5},{8,10},{9,11},{10,... | collective-permute-start | bytes 3932168 | tf_op jit(solution)/shard_map/ppermute | solution.py:133
  525.9 51.1 %collective-permute-start.27 = (bf16[640,2048]{1,0:T(8,128)(2,1)}, bf16[640,2048]{1,0:T(8,128)(2,1)}, u32[]{:S(2)}, u32[]{:S(2)}) collective-permute-start(bf16[640,2048]{1,0:T(8,128)(2,1)} %slice.910), channel_id=1, source_target_pairs={{0,1},{1,0},{2,3},{3,2},{4,5},{5,4},{6,7},{7,6},{8,9},{9,8},{10,11... | collective-permute-start | bytes 7864328 | tf_op jit(solution)/shard_map/ppermute | solution.py:133
  592.4 178.7 %collective-permute-start.38 = (bf16[4,384,256]{2,1,0:T(8,128)(2,1)}, bf16[4,384,256]{2,1,0:T(8,128)(2,1)}, u32[]{:S(2)}, u32[]{:S(2)}) collective-permute-start(bf16[4,384,256]{2,1,0:T(8,128)(2,1)} %pad_maximum_fusion.34), channel_id=1, source_target_pairs={{0,4},{1,5},{2,6},{3,7},{4,0},{5,1},{6,2},{7,3},{8,12},{9,13},{10,... | collective-permute-start | bytes 2359304 | tf_op jit(solution)/shard_map/ppermute | solution.py:133
  617.8 55.9 %collective-permute-start.36 = (bf16[320,2048]{1,0:T(8,128)(2,1)}, bf16[320,2048]{1,0:T(8,128)(2,1)}, u32[]{:S(2)}, u32[]{:S(2)}) collective-permute-start(bf16[320,2048]{1,0:T(8,128)(2,1)} %slice.1161), channel_id=1, source_target_pairs={{0,2},{1,3},{2,0},{3,1},{4,6},{5,7},{6,4},{7,5},{8,10},{9,11},{10,... | collective-permute-start | bytes 3932168 | tf_op jit(solution)/shard_map/ppermute | solution.py:133
  623.4 50.3 %collective-permute-start.35 = (bf16[640,2048]{1,0:T(8,128)(2,1)S(1)}, bf16[640,2048]{1,0:T(8,128)(2,1)S(1)}, u32[]{:S(2)}, u32[]{:S(2)}) collective-permute-start(bf16[640,2048]{1,0:T(8,128)(2,1)S(1)} %bitcast.678), channel_id=1, source_target_pairs={{0,1},{1,0},{2,3},{3,2},{4,5},{5,4},{6,7},{7,6},{8,9},{9,8},{10,11... | collective-permute-start | bytes 7864328 | tf_op jit(solution)/shard_map/ppermute | solution.py:133
  629.5 77.0 %collective-permute-start.34 = (bf16[320,2048]{1,0:T(8,128)(2,1)}, bf16[320,2048]{1,0:T(8,128)(2,1)}, u32[]{:S(2)}, u32[]{:S(2)}) collective-permute-start(bf16[320,2048]{1,0:T(8,128)(2,1)} %slice.1160), channel_id=1, source_target_pairs={{0,2},{1,3},{2,0},{3,1},{4,6},{5,7},{6,4},{7,5},{8,10},{9,11},{10,... | collective-permute-start | bytes 3932168 | tf_op jit(solution)/shard_map/ppermute | solution.py:133
  710.0 61.9 %all-to-all-start.8 = ((bf16[4,160,2048]{2,1,0:T(8,128)(2,1)}), bf16[4,160,2048]{2,1,0:T(8,128)(2,1)}, u32[]{:S(2)}, u32[]{:S(2)}) async-start(bf16[4,160,2048]{2,1,0:T(8,128)(2,1)} %bitcast.123), calls=%async_computation.8 | async-start | bytes 5242880 | tf_op jit(solution)/shard_map/all_to_all | solution.py:136
  715.0 56.2 %collective-permute-start.39 = (bf16[4,1024,256]{2,1,0:T(8,128)(2,1)}, bf16[4,1024,256]{2,1,0:T(8,128)(2,1)}, u32[]{:S(2)}, u32[]{:S(2)}) collective-permute-start(bf16[4,1024,256]{2,1,0:T(8,128)(2,1)} %pad_maximum_fusion.21), channel_id=1, source_target_pairs={{0,4},{1,5},{2,6},{3,7},{4,0},{5,1},{6,2},{7,3},{8,12},{9,13},{10,... | collective-permute-start | bytes 6291464 | tf_op jit(solution)/shard_map/ppermute | solution.py:133
  814.5 93.3 %all-to-all-start.13 = ((bf16[4,1408,256]{2,1,0:T(8,128)(2,1)}), bf16[4,1408,256]{2,1,0:T(8,128)(2,1)}, u32[]{:S(2)}, u32[]{:S(2)}) async-start(bf16[4,1408,256]{2,1,0:T(8,128)(2,1)} %pad_maximum_fusion.10), calls=%async_computation.13 | async-start | bytes 5767168 | tf_op jit(solution)/shard_map/all_to_all | solution.py:136
  821.3 47.8 %collective-permute-start.44 = (bf16[4,256,1024]{2,1,0:T(8,128)(2,1)S(1)}, bf16[4,256,1024]{2,1,0:T(8,128)(2,1)S(1)}, u32[]{:S(2)}, u32[]{:S(2)}) collective-permute-start(bf16[4,256,1024]{2,1,0:T(8,128)(2,1)S(1)} %dynamic-slice_bitcast_fusion.2), channel_id=1, source_target_pairs={{0,4},{1,5},{2,6},{3,7},{4,0},{5,1},{6,2},{7,3},{8,12},{9,13},{10,... | collective-permute-start | bytes 6291464 | tf_op jit(solution)/shard_map/ppermute | solution.py:133
  893.1 83.3 %collective-permute-start.45 = (bf16[4,256,1024]{2,1,0:T(8,128)(2,1)}, bf16[4,256,1024]{2,1,0:T(8,128)(2,1)}, u32[]{:S(2)}, u32[]{:S(2)}) collective-permute-start(bf16[4,256,1024]{2,1,0:T(8,128)(2,1)} %dynamic-slice_bitcast_fusion.1), channel_id=1, source_target_pairs={{0,4},{1,5},{2,6},{3,7},{4,0},{5,1},{6,2},{7,3},{8,12},{9,13},{10,... | collective-permute-start | bytes 6291464 | tf_op jit(solution)/shard_map/ppermute | solution.py:133
  907.8 64.0 %all-to-all-start.10 = ((bf16[4,160,2048]{2,1,0:T(8,128)(2,1)}), bf16[4,160,2048]{2,1,0:T(8,128)(2,1)}, u32[]{:S(2)}, u32[]{:S(2)}) async-start(bf16[4,160,2048]{2,1,0:T(8,128)(2,1)} %bitcast.134), calls=%async_computation.10 | async-start | bytes 5242880 | tf_op jit(solution)/shard_map/all_to_all | solution.py:136
  971.9 57.3 %all-to-all-start.11 = ((bf16[4,256,1024]{2,1,0:T(8,128)(2,1)}), bf16[4,256,1024]{2,1,0:T(8,128)(2,1)}, u32[]{:S(2)}, u32[]{:S(2)}) async-start(bf16[4,256,1024]{2,1,0:T(8,128)(2,1)} %fusion.26), calls=%async_computation.11 | async-start | bytes 4194304 | tf_op jit(solution)/shard_map/all_to_all | solution.py:136
  1008.5 47.5 %collective-permute-start.56 = (bf16[4,2,64,1024]{3,2,0,1:T(8,128)(2,1)}, bf16[4,2,64,1024]{3,2,0,1:T(8,128)(2,1)}, u32[]{:S(2)}, u32[]{:S(2)}) collective-permute-start(bf16[4,2,64,1024]{3,2,0,1:T(8,128)(2,1)} %dynamic-slice_bitcast_fusion.7), channel_id=1, source_target_pairs={{0,2},{1,3},{2,0},{3,1},{4,6},{5,7},{6,4},{7,5},{8,10},{9,11},{10,... | collective-permute-start | bytes 3145736 | tf_op jit(solution)/shard_map/ppermute | solution.py:133
  1012.9 61.9 %collective-permute-start.57 = (bf16[4,2,64,1024]{3,2,0,1:T(8,128)(2,1)}, bf16[4,2,64,1024]{3,2,0,1:T(8,128)(2,1)}, u32[]{:S(2)}, u32[]{:S(2)}) collective-permute-start(bf16[4,2,64,1024]{3,2,0,1:T(8,128)(2,1)} %dynamic-slice_bitcast_fusion.6), channel_id=1, source_target_pairs={{0,2},{1,3},{2,0},{3,1},{4,6},{5,7},{6,4},{7,5},{8,10},{9,11},{10,... | collective-permute-start | bytes 3145736 | tf_op jit(solution)/shard_map/ppermute | solution.py:133
  1028.2 50.1 %collective-permute-start.55 = (bf16[4,2,64,2048]{3,2,0,1:T(8,128)(2,1)}, bf16[4,2,64,2048]{3,2,0,1:T(8,128)(2,1)}, u32[]{:S(2)}, u32[]{:S(2)}) collective-permute-start(bf16[4,2,64,2048]{3,2,0,1:T(8,128)(2,1)} %dynamic-slice_bitcast_fusion), channel_id=1, source_target_pairs={{0,4},{1,5},{2,6},{3,7},{4,0},{5,1},{6,2},{7,3},{8,12},{9,13},{10,... | collective-permute-start | bytes 6291464 | tf_op jit(solution)/shard_map/ppermute | solution.py:133
  1032.5 97.3 %all-to-all-start.12 = ((bf16[4,256,1024]{2,1,0:T(8,128)(2,1)}), bf16[4,256,1024]{2,1,0:T(8,128)(2,1)}, u32[]{:S(2)}, u32[]{:S(2)}) async-start(bf16[4,256,1024]{2,1,0:T(8,128)(2,1)} %fusion.25), calls=%async_computation.12 | async-start | bytes 4194304 | tf_op jit(solution)/shard_map/all_to_all | solution.py:136
  1041.7 68.6 %collective-permute-start.60 = (bf16[4,32,1792]{2,1,0:T(8,128)(2,1)}, bf16[4,32,1792]{2,1,0:T(8,128)(2,1)}, u32[]{:S(2)}, u32[]{:S(2)}) collective-permute-start(bf16[4,32,1792]{2,1,0:T(8,128)(2,1)} %dynamic-slice_bitcast_fusion.16), channel_id=1, source_target_pairs={{0,2},{1,3},{2,0},{3,1},{4,6},{5,7},{6,4},{7,5},{8,10},{9,11},{10,... | collective-permute-start | bytes 1376264 | tf_op jit(solution)/shard_map/ppermute | solution.py:133
  1056.0 54.3 %collective-permute-start.61 = (bf16[4,32,1920]{2,1,0:T(8,128)(2,1)}, bf16[4,32,1920]{2,1,0:T(8,128)(2,1)}, u32[]{:S(2)}, u32[]{:S(2)}) collective-permute-start(bf16[4,32,1920]{2,1,0:T(8,128)(2,1)} %dynamic-slice_bitcast_fusion.15), channel_id=1, source_target_pairs={{0,4},{1,5},{2,6},{3,7},{4,0},{5,1},{6,2},{7,3},{8,12},{9,13},{10,... | collective-permute-start | bytes 1474568 | tf_op jit(solution)/shard_map/ppermute | solution.py:133
  1130.5 74.7 %all-to-all-start.14 = ((bf16[4,64,5952]{2,1,0:T(8,128)(2,1)}), bf16[4,64,5952]{2,1,0:T(8,128)(2,1)S(1)}, u32[]{:S(2)}, u32[]{:S(2)}) async-start(bf16[4,64,5952]{2,1,0:T(8,128)(2,1)} %fusion.40), calls=%async_computation.14 | async-start | bytes 6160384 | tf_op jit(solution)/shard_map/all_to_all | solution.py:136
  (323 other events, 4227.6 us)
Sparse Core Ops, SparseCore 0:
  118.1 66.8 all-gather.2
  481.1 49.9 all-gather.4
